TPU v7x, 32 devices: a whole 2x2x4 slice. The times are simulated.
32 devices in a mesh: wide: 16 (over z, x, core), head: 2 (over y).
Axes of the slice: x: 2, y: 2, z: 4, core: 2. Of those that a mesh axis runs over, the one named last changes fastest.
Arguments:
- branch_query: bfloat16 [64, 8192], P('wide', 'head'), may hold values from -6 to 6
- key_new: bfloat16 [64, 1024], P('wide', 'head'), may hold values from -6 to 6
- value_new: bfloat16 [64, 1024], P('wide', 'head'), may hold values from -6 to 6
- pool_pages: bfloat16 [2, 1024, 16, 1024], P(None, 'wide', None, 'head'), may hold values from -6 to 6
- page_table: int32 [64, 16], P('wide'), may hold values from 0 to 63, as said below
- tail_length: int32 [64], P('wide'), may hold values from 1 to 256
- parent_row: int32 [64], P('wide'), may hold values from 0 to 63, as said below
- residual: bfloat16 [64, 8192], P(('wide', 'head')), may hold values from -6 to 6
- norm_gain: float32 [8192], replicated, may hold values from 0.5 to 1.5
- gate_blocks: bfloat16 [128, 32, 128, 128], P('wide'), may hold values from -0.09375 to 0.09375
- up_blocks: bfloat16 [128, 32, 128, 128], P('wide'), may hold values from -0.09375 to 0.09375
- gate_up_keep: int32 [128, 32], P('wide'), may hold values from 0 to 63, as said below
- gate_scale: float32 [128, 32], P('wide'), may hold values from 0.5 to 2
- up_scale: float32 [128, 32], P('wide'), may hold values from 0.5 to 2
- down_blocks: bfloat16 [128, 32, 128, 128], P('wide'), may hold values from -0.0625 to 0.0625
- down_keep: int32 [128, 32], P('wide'), may hold values from 0 to 63, as said below
- down_scale: float32 [128, 32], P('wide'), may hold values from 0.5 to 2
Outputs:
- layer_out: bfloat16 [64, 8192], P(('wide', 'head'))
Inputs may be any that keep to these rules, and one draw needn't show every extreme that they name: parent_row never falls with the branch index, and parent_row[b] <= b and parent_row[b] > b - 4. `page_table`: the entries of the 4 rows held by one index of wide name each of that index's 64 pages once. `gate_up_keep`: each row names 32 different blocks. `down_keep`: each row names 32 different blocks.
All inputs are finite; a program needn't handle non-finite values.
Results may differ from a plain program's by a relative error of at most 0.017.
Values may be sent and summed in bfloat16 or wider, within the bound.
No kernel may reach another device: no remote copies, remote signals or barrier semaphores. Data moves between devices by JAX's collectives and lax.ppermute only.
A program may use at most 64 MiB of HBM per device.

v0:
```python
import math

import jax
import jax.numpy as jnp
from jax import lax
from jax.sharding import PartitionSpec as P

HD = 128
BLK = 128


def shifted(block, axis, distance):
    devices = range(lax.axis_size(axis))
    route = [(i - distance, i) for i in devices if i - distance in devices]
    return lax.ppermute(block, axis, route)


def attend(branch_query, key_new, value_new, child_tails, child_length):
    row_count = branch_query.shape[0]
    groups = key_new.shape[1] // HD
    per_group = branch_query.shape[1] // (groups * HD)
    tail_size = child_tails.shape[2]
    queries = branch_query.reshape(row_count, groups, per_group, HD)
    tail_keys = child_tails[0].reshape(row_count, tail_size, groups, HD)
    tail_values = child_tails[1].reshape(row_count, tail_size, groups, HD)
    own_keys = key_new.reshape(row_count, groups, HD)
    own_values = value_new.reshape(row_count, groups, HD)
    factor = 1.0 / math.sqrt(HD)
    tail_scores = (
        jnp.einsum("rgjd,rtgd->rgjt", queries, tail_keys, preferred_element_type=jnp.float32)
        * factor
    )
    own_scores = (
        jnp.einsum("rgjd,rgd->rgj", queries, own_keys, preferred_element_type=jnp.float32) * factor
    )
    live_mask = (jnp.arange(tail_size, dtype=jnp.float32)[None, :] < child_length[:, None])[
        :, None, None, :
    ]
    top_score = jnp.maximum(jnp.max(jnp.where(live_mask, tail_scores, -1e30), axis=-1), own_scores)
    tail_exp = jnp.where(live_mask, jnp.exp(tail_scores - top_score[..., None]), 0.0)
    own_exp = jnp.exp(own_scores - top_score)
    totals = jnp.sum(tail_exp, axis=-1) + own_exp
    tail_weights = (tail_exp / totals[..., None]).astype(jnp.bfloat16)
    own_weights = (own_exp / totals).astype(jnp.bfloat16)
    mixture = jnp.einsum(
        "rgjt,rtgd->rgjd", tail_weights, tail_values, preferred_element_type=jnp.float32
    )
    mixture = mixture + own_weights[..., None].astype(jnp.float32) * own_values[
        :, :, None, :
    ].astype(jnp.float32)
    return mixture.reshape(row_count, -1).astype(jnp.bfloat16)


def ffn_terms(
    rows_in, gate_blocks, up_blocks, gate_up_keep, gate_scale, up_scale, down_blocks, down_scale
):
    row_count = rows_in.shape[0]
    blocks = rows_in.reshape(row_count, -1, BLK)
    picked = blocks[:, gate_up_keep]
    gate_part = jnp.einsum(
        "rckd,ckdf->rckf", picked, gate_blocks, preferred_element_type=jnp.float32
    )
    up_part = jnp.einsum("rckd,ckdf->rckf", picked, up_blocks, preferred_element_type=jnp.float32)
    gate_sum = jnp.sum(gate_part * gate_scale[None, :, :, None], axis=2)
    up_sum = jnp.sum(up_part * up_scale[None, :, :, None], axis=2)
    hidden = (jax.nn.silu(gate_sum) * up_sum).astype(jnp.bfloat16)
    contrib = (
        jnp.einsum("rcf,ckfe->rcke", hidden, down_blocks, preferred_element_type=jnp.float32)
        * down_scale[None, :, :, None]
    )
    return contrib.reshape(row_count, -1, BLK)


def feed_forward(
    rows_in,
    gate_blocks,
    up_blocks,
    gate_up_keep,
    gate_scale,
    up_scale,
    down_blocks,
    down_keep,
    down_scale,
):
    row_count = rows_in.shape[0]
    contrib = ffn_terms(
        rows_in, gate_blocks, up_blocks, gate_up_keep, gate_scale, up_scale, down_blocks, down_scale
    )
    placed = jnp.zeros((row_count, rows_in.shape[1] // BLK, BLK), jnp.float32)
    placed = placed.at[:, down_keep.reshape(-1)].add(contrib)
    return placed.reshape(row_count, -1)


def per_device(
    branch_query,
    key_new,
    value_new,
    pool_pages,
    page_table,
    tail_length,
    parent_row,
    residual,
    norm_gain,
    gate_blocks,
    up_blocks,
    gate_up_keep,
    gate_scale,
    up_scale,
    down_blocks,
    down_keep,
    down_scale,
):
    row_count = branch_query.shape[0]
    tail_size = page_table.shape[1] * pool_pages.shape[2]
    own_tails = pool_pages[:, page_table].reshape(2, row_count, tail_size, pool_pages.shape[3])
    own_length = tail_length.astype(jnp.bfloat16)
    prior_tails, prior_length = shifted((own_tails, own_length), "wide", 1)
    both_tails = jnp.concatenate([prior_tails, own_tails], axis=1)
    both_length = jnp.concatenate([prior_length, own_length]).astype(jnp.float32)
    local_parent = parent_row - (lax.axis_index("wide") - 1) * row_count
    child_tails = both_tails[:, local_parent]
    child_length = both_length[local_parent]
    attention = attend(branch_query, key_new, value_new, child_tails, child_length)
    head_rows = lax.all_to_all(attention, "head", split_axis=0, concat_axis=1, tiled=True)
    middle = residual.astype(jnp.float32) + head_rows.astype(jnp.float32)
    normed = (
        middle * lax.rsqrt(jnp.mean(middle * middle, axis=-1, keepdims=True) + 1e-05) * norm_gain
    ).astype(jnp.bfloat16)
    gathered = lax.all_gather(normed, "wide", axis=0, tiled=True)
    ffn_share = lax.psum_scatter(
        feed_forward(
            gathered,
            gate_blocks,
            up_blocks,
            gate_up_keep,
            gate_scale,
            up_scale,
            down_blocks,
            down_keep,
            down_scale,
        ),
        "wide",
        scatter_dimension=0,
        tiled=True,
    )
    return (middle + ffn_share).astype(jnp.bfloat16)


def solution(mesh):
    placed = (
        P("wide", "head"),
        P("wide", "head"),
        P("wide", "head"),
        P(None, "wide", None, "head"),
        P("wide", None),
        P("wide"),
        P("wide"),
        P(("wide", "head"), None),
        P(),
        P("wide", None, None, None),
        P("wide", None, None, None),
        P("wide", None),
        P("wide", None),
        P("wide", None),
        P("wide", None, None, None),
        P("wide", None),
        P("wide", None),
    )
    return jax.shard_map(
        per_device, mesh=mesh, in_specs=placed, out_specs=P(("wide", "head"), None), check_vma=False
    )
```

profile of v0, /device:TPU:0, one launch (start us, length us, event | category | flops | bytes accessed | tf_op | source)
XLA Modules:
  0.0 230.4 jit_solution(7347885102713904006)
XLA Ops:
  6.5 0.0 copy-start
  6.5 0.8 compare_select_fusion.2
  7.4 0.1 reshape.118
  7.5 0.7 copy-done
  8.2 0.0 copy-start.10
  8.2 0.0 copy-start.13
  8.2 0.0 copy-start.6
  8.2 2.0 gather_fusion.1
  10.2 3.1 %copy.33 = bf16[64,2,16,512]{3,2,0,1:T(8,128)(2,1)} copy(bf16[64,2,16,512]{3,2,1,0:T(8,128)(2,1)} %gather_fusion.1) | data formatting | bytes 4194304 | tf_op jit(solution)/shard_map/gather | solution.py:115
  13.3 3.7 %collective-permute-start.1 = (bf16[2,4,256,512]{3,2,1,0:T(8,128)(2,1)}, bf16[2,4,256,512]{3,2,1,0:T(8,128)(2,1)}, u32[]{:S(2)}, u32[]{:S(2)}) collective-permute-start(bf16[2,4,256,512]{3,2,1,0:T(8,128)(2,1)} %bitcast.2), channel_id=1, source_target_pairs={{0,2},{2,4},{4,6},{6,8},{8,10},{10,12},{12,14},{14,16},{16,18},{18... | collective-permute-start | bytes 6291464 | tf_op jit(solution)/shard_map/ppermute | solution.py:15
  17.0 0.0 copy-done.12
  17.0 3.2 %collective-permute-start = (bf16[4]{0:T(256)(128)(2,1)S(1)}, bf16[4]{0:T(256)(128)(2,1)S(1)}, u32[]{:S(2)}, u32[]{:S(2)}) collective-permute-start(bf16[4]{0:T(256)(128)(2,1)S(1)} %convert_element_type.56), channel_id=1, source_target_pairs={{0,2},{2,4},{4,6},{6,8},{8,10},{10,12},{12,14},{14,16},{16,18},{18... | collective-permute-start | bytes 32 | tf_op jit(solution)/shard_map/ppermute | solution.py:15
  20.2 0.0 copy-done.8
  20.3 0.0 copy-done.9
  20.3 0.0 copy-done.11
  20.3 0.1 reshape.134
  20.4 0.0 copy-done.10
  20.4 0.1 reshape.102
  20.5 0.0 copy-done.13
  20.5 0.0 copy-done.6
  20.5 0.1 fusion.14
  20.6 0.4 collective-permute-done
  21.0 0.1 maximum_convert_fusion
  21.1 0.6 gather_fusion
  21.7 0.1 iota_compare_fusion
  21.8 0.0 collective-permute-done.1
  21.8 4.5 %pad_maximum_fusion = bf16[2,8,256,512]{3,2,1,0:T(8,128)(2,1)} fusion(bf16[2,4,256,512]{3,2,1,0:T(8,128)(2,1)} %bitcast.2, bf16[2,4,256,512]{3,2,1,0:T(8,128)(2,1)} %collective-permute-done.1), kind=kLoop, calls=%fused_computation.5 | loop fusion | flops 2097152 | bytes 8388608 | tf_op jit(solution)/shard_map/concatenate | solution.py:118
  26.3 4.2 %gather_fusion.2 = bf16[4,2,256,512]{3,2,1,0:T(8,128)(2,1)} fusion(bf16[2,8,256,512]{3,2,1,0:T(8,128)(2,1)} %pad_maximum_fusion, s32[1024]{0:T(1024)S(1)} %pad_clamp_fusion.2), kind=kCustom, calls=%fused_computation.2 | custom fusion | bytes 4194320 | tf_op jit(solution)/shard_map/gather | solution.py:121
  30.5 3.0 %fusion.24 = (bf16[1,4,256,512]{3,2,0,1:T(8,128)(2,1)}, bf16[1,4,256,512]{3,2,0,1:T(8,128)(2,1)}) fusion(bf16[2,4,256,512]{3,2,0,1:T(8,128)(2,1)} %bitcast.88), kind=kLoop, calls=%fused_computation.58 | loop fusion | bytes 4194304 | tf_op jit(solution)/shard_map/slice | solution.py:24
  33.6 1.5 copy.34
  35.0 0.3 select_reduce_fusion
  35.4 0.2 bitcast_reduce_fusion
  35.6 1.5 copy.36
  37.1 0.0 copy-start.3
  37.1 0.4 fusion
  37.5 0.6 convert_element_type.64
  38.2 3.3 %all-to-all-start = ((bf16[2,2,4096]{2,1,0:T(2,128)(2,1)}), bf16[2,2,4096]{2,1,0:T(2,128)(2,1)S(1)}, u32[]{:S(2)}, u32[]{:S(2)}) async-start(bf16[2,2,4096]{2,1,0:T(2,128)(2,1)} %convert_element_type.64), calls=%async_computation | async-start | bytes 65536 | tf_op jit(solution)/shard_map/all_to_all | solution.py:124
  41.4 0.0 all-reduce.3.cloned.1.call-start
  41.5 3.9 %all-to-all-done = bf16[2,2,4096]{2,1,0:T(2,128)(2,1)S(1)} async-done(((bf16[2,2,4096]{2,1,0:T(2,128)(2,1)}), bf16[2,2,4096]{2,1,0:T(2,128)(2,1)S(1)}, u32[]{:S(2)}, u32[]{:S(2)}) %all-to-all-start) | async-done | bytes 32800 | tf_op jit(solution)/shard_map/all_to_all | solution.py:124
  45.4 0.0 copy-done.2
  45.4 0.2 multiply_reduce_fusion.2
  45.6 0.0 copy-done.7
  45.6 0.1 fusion.17
  45.7 44.5 %all-gather = bf16[16,2,8192]{2,1,0:T(2,128)(2,1)S(1)} all-gather(bf16[1,2,8192]{2,1,0:T(2,128)(2,1)S(1)} %fusion.17), channel_id=1, replica_groups=mesh['wide'=16,'head'=2] {'wide'}, dimensions={0}, use_global_device_ids=true | all-gather | bytes 557056 | tf_op jit(solution)/shard_map/all_gather | solution.py:129
  90.2 0.4 reshape.103
  90.6 0.3 copy.38
  90.9 2.2 gather_fusion.3
  93.1 0.0 copy-done.3
  93.1 6.5 %multiply_reduce_fusion = f32[8,32,128]{2,1,0:T(8,128)S(1)} fusion(bf16[32,8,32,128]{3,0,2,1:T(8,128)(2,1)} %bitcast.84, bf16[8,32,128,128]{3,2,1,0:T(8,128)(2,1)} %param.27, f32[8,32]{1,0:T(8,128)S(1)} %copy-done.3), kind=kOutput, calls=%fused_computation.6 | convolution fusion | flops 270499840 | bytes 10617856 | tf_op jit(solution)/shard_map/rckd,ckdf->rckf/dot_general | solution.py:63
  99.6 0.0 copy-done.1
  99.6 0.0 copy-done.4
  99.6 0.0 slice-start.1
  99.7 0.0 copy-start.5
  99.7 5.9 %multiply_reduce_fusion.1 = f32[8,32,128]{2,1,0:T(8,128)S(1)} fusion(bf16[32,8,32,128]{3,0,2,1:T(8,128)(2,1)S(1)} %bitcast.85, bf16[8,32,128,128]{3,2,1,0:T(8,128)(2,1)} %param.26, f32[8,32]{1,0:T(8,128)S(1)} %copy-done.4), kind=kOutput, calls=%fused_computation.7 | convolution fusion | flops 270499840 | bytes 10617856 | tf_op jit(solution)/shard_map/rckd,ckdf->rckf/dot_general | solution.py:60
  105.5 0.0 slice-done
  105.6 3.2 %convolution_multiply_fusion = f32[8,32,32,128]{3,1,2,0:T(8,128)} fusion(bf16[8,32,128,128]{3,2,1,0:T(8,128)(2,1)S(1)} %bitcast.87, f32[8,32]{1,0:T(8,128)S(1)} %copy-done.5, f32[8,32,128]{2,1,0:T(8,128)S(1)} %multiply_reduce_fusion, f32[8,32,128]{2,1,0:T(8,128)S(1)} %multiply_reduce_fusion.1), kind=kOutput, calls=%fused_computation.8 | convolution fusion | flops 269680640 | bytes 12846080 | tf_op jit(solution)/shard_map/rcf,ckfe->rcke/dot_general | solution.py:68
  108.8 0.1 broadcast_in_dim.48
  108.9 0.0 copy-start.14
  109.0 22.4 %scatter_fusion = f32[32,64,128]{2,0,1:T(8,128)S(1)} fusion(f32[32,64,128]{2,0,1:T(8,128)S(1)} %broadcast_in_dim.48, s32[256]{0:T(256)S(1)} %bitcast.98, f32[256,32,128]{2,1,0:T(8,128)} %bitcast.83), kind=kCustom, calls=%fused_computation.4 | custom fusion | flops 1048576 | bytes 12583936 | tf_op jit(solution)/shard_map/scatter-add | solution.py:90
  131.4 1.1 copy_bitcast_fusion
  132.5 0.0 all-reduce.3.cloned.1.call-update
  132.5 0.6 dynamic-slice
  133.7 88.2 %all-reduce.3.cloned.1.call-done = f32[32,8192]{1,0:T(8,128)} async-done(((f32[32,8192]{1,0:T(8,128)}), f32[32,8192]{1,0:T(8,128)}) %all-reduce.3.cloned.1.call-update) | async-done | bytes 1048592
  222.0 1.6 fusion.8
  (26 shorter events, 0.1 us)
Async XLA Ops:
  6.5 1.6 copy-start
  8.1 8.9 %copy-start.12 = (s32[4]{0:T(128)S(1)}, s32[4]{0:T(128)}, u32[]{:S(2)}) copy-start(s32[4]{0:T(128)} %param.22) | copy-start | bytes 52
  8.1 12.1 %copy-start.8 = (bf16[4,512]{1,0:T(4,128)(2,1)S(1)}, bf16[4,512]{1,0:T(4,128)(2,1)}, u32[]{:S(2)}) copy-start(bf16[4,512]{1,0:T(4,128)(2,1)} %param.18) | copy-start | bytes 12292
  8.1 12.1 %copy-start.9 = (bf16[4,512]{1,0:T(4,128)(2,1)S(1)}, bf16[4,512]{1,0:T(4,128)(2,1)}, u32[]{:S(2)}) copy-start(bf16[4,512]{1,0:T(4,128)(2,1)} %param.19) | copy-start | bytes 12292
  8.1 12.1 %copy-start.11 = (s32[8,32]{1,0:T(8,128)S(1)}, s32[8,32]{1,0:T(8,128)}, u32[]{:S(2)}) copy-start(s32[8,32]{1,0:T(8,128)} %param.28) | copy-start | bytes 3076
  8.2 12.2 %copy-start.10 = (s32[8,32]{1,0:T(8,128)S(1)}, s32[8,32]{1,0:T(8,128)}, u32[]{:S(2)}) copy-start(s32[8,32]{1,0:T(8,128)} %param.32) | copy-start | bytes 3076
  8.2 12.3 %copy-start.13 = (s32[4]{0:T(128)S(1)}, s32[4]{0:T(128)}, u32[]{:S(2)}) copy-start(s32[4]{0:T(128)} %param.23) | copy-start | bytes 52
  8.2 12.3 %copy-start.6 = (bf16[4,4096]{1,0:T(4,128)(2,1)S(1)}, bf16[4,4096]{1,0:T(4,128)(2,1)}, u32[]{:S(2)}) copy-start(bf16[4,4096]{1,0:T(4,128)(2,1)} %param.17) | copy-start | bytes 98308
  13.3 8.5 %collective-permute-start.1 = (bf16[2,4,256,512]{3,2,1,0:T(8,128)(2,1)}, bf16[2,4,256,512]{3,2,1,0:T(8,128)(2,1)}, u32[]{:S(2)}, u32[]{:S(2)}) collective-permute-start(bf16[2,4,256,512]{3,2,1,0:T(8,128)(2,1)} %bitcast.2), channel_id=1, source_target_pairs={{0,2},{2,4},{4,6},{6,8},{8,10},{10,12},{12,14},{14,16},{16,18},{18... | collective-permute-start | bytes 6291464 | tf_op jit(solution)/shard_map/ppermute | solution.py:15
  17.0 4.0 %collective-permute-start = (bf16[4]{0:T(256)(128)(2,1)S(1)}, bf16[4]{0:T(256)(128)(2,1)S(1)}, u32[]{:S(2)}, u32[]{:S(2)}) collective-permute-start(bf16[4]{0:T(256)(128)(2,1)S(1)} %convert_element_type.56), channel_id=1, source_target_pairs={{0,2},{2,4},{4,6},{6,8},{8,10},{10,12},{12,14},{14,16},{16,18},{18... | collective-permute-start | bytes 32 | tf_op jit(solution)/shard_map/ppermute | solution.py:15
  33.6 11.8 %copy-start.2 = (bf16[2,8192]{1,0:T(2,128)(2,1)S(1)}, bf16[2,8192]{1,0:T(2,128)(2,1)}, u32[]{:S(2)}) copy-start(bf16[2,8192]{1,0:T(2,128)(2,1)} %param.24) | copy-start | bytes 98308
  33.6 12.0 %copy-start.7 = (f32[8192]{0:T(1024)S(1)}, f32[8192]{0:T(1024)}, u32[]{:S(2)}) copy-start(f32[8192]{0:T(1024)} %param.25) | copy-start | bytes 98308
  37.1 56.0 %copy-start.3 = (f32[8,32]{1,0:T(8,128)S(1)}, f32[8,32]{1,0:T(8,128)}, u32[]{:S(2)}) copy-start(f32[8,32]{1,0:T(8,128)} %param.30) | copy-start | bytes 3076
  38.2 7.2 %all-to-all-start = ((bf16[2,2,4096]{2,1,0:T(2,128)(2,1)}), bf16[2,2,4096]{2,1,0:T(2,128)(2,1)S(1)}, u32[]{:S(2)}, u32[]{:S(2)}) async-start(bf16[2,2,4096]{2,1,0:T(2,128)(2,1)} %convert_element_type.64), calls=%async_computation | async-start | bytes 65536 | tf_op jit(solution)/shard_map/all_to_all | solution.py:124
  41.4 180.5 %all-reduce.3.cloned.1.call-start = ((), (), s32[]{:S(2)}) async-start(), calls=%async_computation.1 | async-start | bytes 2097152
  93.1 6.5 %copy-start.1 = (bf16[256,32,128]{2,1,0:T(8,128)(2,1)S(1)}, bf16[256,32,128]{2,1,0:T(8,128)(2,1)}, u32[]{:S(2)}) copy-start(bf16[256,32,128]{2,1,0:T(8,128)(2,1)} %gather_fusion.3) | copy-start | bytes 6291460
  93.1 6.5 %copy-start.4 = (f32[8,32]{1,0:T(8,128)S(1)}, f32[8,32]{1,0:T(8,128)}, u32[]{:S(2)}) copy-start(f32[8,32]{1,0:T(8,128)} %param.29) | copy-start | bytes 3076
  93.1 12.4 %slice-start = ((s8[8388608]{0:T(1024)(128)(4,1)}), s8[4194304]{0:T(1024)(128)(4,1)S(1)}, s32[]{:S(2)}) async-start(s8[8388608]{0:T(1024)(128)(4,1)} %bitcast.86), calls=%async_computation.2 | async-start | bytes 8388608
  99.6 5.9 %slice-start.1 = ((s8[8388608]{0:T(1024)(128)(4,1)}), s8[4194304]{0:T(1024)(128)(4,1)S(1)}, s32[]{:S(2)}) async-start(s8[8388608]{0:T(1024)(128)(4,1)} %bitcast.86), calls=%async_computation.3 | async-start | bytes 8388608
  99.7 5.9 %copy-start.5 = (f32[8,32]{1,0:T(8,128)S(1)}, f32[8,32]{1,0:T(8,128)}, u32[]{:S(2)}) copy-start(f32[8,32]{1,0:T(8,128)} %param.33) | copy-start | bytes 3076
  108.9 23.5 %copy-start.14 = (u32[32]{0:T(128)S(1)}, u32[32]{0:T(128)}, u32[]{:S(2)}) copy-start(u32[32]{0:T(128)} %constant.57) | copy-start | bytes 388
Sparse Core Ops, SparseCore 0:
  132.6 89.3 all-reduce.2
where the time goes:
time: 231 us; the launch traced here: 230 us
  waiting for transfers between devices  92.5 us (40%)
  blocking collectives  44.5 us (19%)
  other arithmetic  30.1 us (13%)
  local copies, waits for them, and re-layouts  22.3 us (10%)
  matrix products  16.5 us (7%)
  between operations  14.4 us (6%)
  starting transfers between devices  10.2 us (4%)
    unnamed x2, waiting for transfers between devices  88.2 us
    all_gather x1, blocking collectives, per_device(): gathered = lax.all_gather(normed, 'wide', axis=0, tiled=True)  44.5 us
    scatter-add x1, other arithmetic, feed_forward(): placed = placed.at[:, down_keep.reshape(-1)].add(contrib)  22.4 us
    ppermute x2, starting transfers between devices, shifted(): return lax.ppermute(block, axis, route)  6.88 us
    dot_general x1, matrix products, ffn_terms(): jnp.einsum('rckd,ckdf->rckf', picked, up_blocks, preferred_element_type=j...  6.47 us
    dot_general x1, matrix products, ffn_terms(): jnp.einsum('rckd,ckdf->rckf', picked, gate_blocks, preferred_element_type...  5.88 us
    gather x2, local copies, waits for them, and re-layouts, per_device(): pool_pages[:, page_table]  5.14 us
  transfers between devices with their start and end apart: 4, of which 3 were waited for; matrix products, arithmetic and copies ran while one was open for 1% of the time, Pallas kernels for 0%

commit v1 on v0

v1 whole, which is shorter than its diff:
```python
import functools
import math

import jax
import jax.numpy as jnp
from jax import lax
from jax.experimental import pallas as pl
from jax.experimental.pallas import tpu as pltpu
from jax.sharding import PartitionSpec as P

HD = 128
BLK = 128
DEAD = -1e30
MIB = 1024 * 1024

VMEM = pl.BlockSpec(memory_space=pltpu.VMEM)
SMEM = pl.BlockSpec(memory_space=pltpu.SMEM)
ANY = pl.BlockSpec(memory_space=pl.ANY)


def attend_kernel(
    groups, per_group, page_ref, length_ref, own_ref, next_ref, pool_ref,
    stay_ref, cross_ref, ahead_ref, ahead_cross_ref, mixed,
):
    rows = own_ref.shape[0]
    width = groups * per_group * HD
    kv_width = groups * HD
    pages, page = pool_ref.shape[1], pool_ref.shape[2]
    spots = pages * page
    head = lax.axis_index("head")

    spot = lax.broadcasted_iota(jnp.int32, (1, spots), 1)
    page_of, offset = spot // page, spot % page
    biases = []
    for r in range(rows):
        place = jnp.full((1, spots), 1 << 20, jnp.int32)
        for i in range(page_ref.shape[1]):
            place = jnp.where(page_of == page_ref[r, i], i * page, place)
        biases.append(jnp.where(place + offset < length_ref[r], 0.0, DEAD))

    both = jnp.concatenate(
        [own_ref[...].astype(jnp.float32), next_ref[...].astype(jnp.float32)], axis=0
    )
    shift = lax.broadcasted_iota(jnp.int32, (2 * rows, 1), 0) // rows * rows
    parent = both[:, width + 2 * kv_width : width + 2 * kv_width + 1] + shift.astype(jnp.float32)
    bias = jnp.full((2 * rows, spots), DEAD, jnp.float32)
    for r in range(rows):
        bias = jnp.where(parent == r, biases[r], bias)
    here = (parent >= 0) & (parent < rows)

    factor = 1.0 / math.sqrt(HD)
    for g in range(groups):
        base = g * per_group * HD
        query = jnp.concatenate(
            [both[:, base + j * HD : base + (j + 1) * HD] for j in range(per_group)], axis=0
        )
        key_own = both[:, width + g * HD : width + (g + 1) * HD]
        value_own = both[:, width + kv_width + g * HD : width + kv_width + (g + 1) * HD]
        keys = pool_ref[0, :, :, g * HD : (g + 1) * HD].reshape(spots, HD)
        values = pool_ref[1, :, :, g * HD : (g + 1) * HD].reshape(spots, HD)
        scores = lax.dot_general(
            query.astype(jnp.bfloat16), keys, (((1,), (1,)), ((), ())),
            preferred_element_type=jnp.float32,
        )
        scores = scores.reshape(per_group, 2 * rows, spots) * factor + bias[None]
        query = query.reshape(per_group, 2 * rows, HD)
        own = jnp.sum(query * key_own[None], axis=-1, keepdims=True) * factor
        top = jnp.maximum(jnp.max(scores, axis=-1, keepdims=True), own)
        expo = jnp.exp(scores - top)
        own_expo = jnp.exp(own - top)
        total = jnp.sum(expo, axis=-1, keepdims=True) + own_expo
        weights = (expo / total).astype(jnp.bfloat16)
        own_weight = (own_expo / total).astype(jnp.bfloat16).astype(jnp.float32)
        mixture = jnp.dot(
            weights.reshape(per_group * 2 * rows, spots), values,
            preferred_element_type=jnp.float32,
        )
        mixture = mixture.reshape(per_group, 2 * rows, HD) + own_weight * value_own[None]
        for j in range(per_group):
            mixed[:, base + j * HD : base + (j + 1) * HD] = jnp.where(here, mixture[j], 0.0)

    part = stay_ref.shape[0]
    for start, mine_ref, other_ref in ((0, stay_ref, cross_ref), (rows, ahead_ref, ahead_cross_ref)):
        low = mixed[start : start + part, :]
        high = mixed[start + part : start + 2 * part, :]
        mine_ref[...] = jnp.where(head == 0, low, high).astype(jnp.bfloat16)
        other_ref[...] = jnp.where(head == 0, high, low).astype(jnp.bfloat16)


def norm_kernel(
    stay_ref, cross_ref, behind_ref, behind_cross_ref, residual_ref, gain_ref,
    middle_ref, normed_ref,
):
    head = lax.axis_index("head")
    half = stay_ref.shape[1]
    f32 = jnp.float32
    same = stay_ref[...].astype(f32) + behind_ref[...].astype(f32)
    other = cross_ref[...].astype(f32) + behind_cross_ref[...].astype(f32)
    first = jnp.where(head == 0, same, other)
    second = jnp.where(head == 0, other, same)
    low = residual_ref[:, :half].astype(f32) + first
    high = residual_ref[:, half:].astype(f32) + second
    middle_ref[:, :half] = low
    middle_ref[:, half:] = high
    square = jnp.sum(low * low, axis=-1, keepdims=True)
    square = square + jnp.sum(high * high, axis=-1, keepdims=True)
    scale = lax.rsqrt(square / (2 * half) + 1e-05)
    normed_ref[:, :half] = (low * scale * gain_ref[:, :half]).astype(jnp.bfloat16)
    normed_ref[:, half:] = (high * scale * gain_ref[:, half:]).astype(jnp.bfloat16)


def feed_kernel(
    keep_ref, gate_scale_ref, up_scale_ref, down_keep_ref, down_scale_ref,
    near_ref, far_ref, gate_hbm, up_hbm, down_hbm,
    stay_ref, send_ref,
    gate, up, down, total, sems,
):
    columns, keep = keep_ref.shape
    half = near_ref.shape[0]
    pairs = ((gate_hbm, gate), (up_hbm, up), (down_hbm, down))

    def fetch(which, c):
        source, target = pairs[which]
        return pltpu.make_async_copy(source.at[c], target.at[c], sems.at[which, c])

    def begin(c, carry):
        for which in range(3):
            fetch(which, c).start()
        return carry

    lax.fori_loop(0, columns, begin, 0)
    total[...] = jnp.zeros_like(total)

    def column(c, carry):
        fetch(0, c).wait()
        fetch(1, c).wait()
        gate_sum = jnp.zeros((2 * half, BLK), jnp.float32)
        up_sum = jnp.zeros((2 * half, BLK), jnp.float32)
        for k in range(keep):
            where = pl.ds(pl.multiple_of(keep_ref[c, k] * BLK, BLK), BLK)
            picked = jnp.concatenate([near_ref[:, where], far_ref[:, where]], axis=0)
            gate_sum += gate_scale_ref[c, k] * jnp.dot(
                picked, gate[c, k], preferred_element_type=jnp.float32
            )
            up_sum += up_scale_ref[c, k] * jnp.dot(
                picked, up[c, k], preferred_element_type=jnp.float32
            )
        hidden = (gate_sum / (1.0 + jnp.exp(-gate_sum)) * up_sum).astype(jnp.bfloat16)
        fetch(2, c).wait()
        for k in range(keep):
            where = pl.ds(pl.multiple_of(down_keep_ref[c, k] * BLK, BLK), BLK)
            total[:, where] += down_scale_ref[c, k] * jnp.dot(
                hidden, down[c, k], preferred_element_type=jnp.float32
            )
        return carry

    lax.fori_loop(0, columns, column, 0)
    stay_ref[...] = total[:half, :]
    send_ref[...] = total[half:, :].astype(jnp.bfloat16)


def swapped(block, bit):
    return lax.ppermute(block, "wide", [(i, i ^ bit) for i in range(lax.axis_size("wide"))])


def per_device(
    branch_query, key_new, value_new, pool_pages, page_table, tail_length, parent_row, residual,
    norm_gain, gate_blocks, up_blocks, gate_up_keep, gate_scale, up_scale, down_blocks, down_keep,
    down_scale,
):
    bf16, f32 = jnp.bfloat16, jnp.float32
    wide, heads = lax.axis_size("wide"), lax.axis_size("head")
    rows, width = branch_query.shape
    groups = key_new.shape[1] // HD
    per_group = width // (groups * HD)
    part = residual.shape[0]
    model = residual.shape[1]

    relative = (parent_row - lax.axis_index("wide") * rows).astype(bf16)
    own = jnp.concatenate(
        [branch_query, key_new, value_new, jnp.broadcast_to(relative[:, None], (rows, HD))], axis=1
    )
    following = lax.ppermute(own, "wide", [(i, i - 1) for i in range(1, wide)])
    piece = jax.ShapeDtypeStruct((part, width), bf16)
    stay, cross, ahead, ahead_cross = pl.pallas_call(
        functools.partial(attend_kernel, groups, per_group),
        out_shape=(piece,) * 4,
        in_specs=[SMEM, SMEM, VMEM, VMEM, VMEM],
        out_specs=(VMEM,) * 4,
        scratch_shapes=[pltpu.VMEM((2 * rows, width), f32)],
        compiler_params=pltpu.CompilerParams(vmem_limit_bytes=24 * MIB),
        name="attend",
    )(page_table, tail_length, own, following, pool_pages)

    cross = lax.ppermute(cross, "head", [(h, 1 - h) for h in range(heads)])
    behind = lax.ppermute(ahead, "wide", [(i, i + 1) for i in range(wide - 1)])
    behind_cross = lax.ppermute(
        ahead_cross,
        ("wide", "head"),
        [(i * heads + h, (i + 1) * heads + 1 - h) for i in range(wide - 1) for h in range(heads)],
    )
    middle, normed = pl.pallas_call(
        norm_kernel,
        out_shape=(
            jax.ShapeDtypeStruct((part, model), f32),
            jax.ShapeDtypeStruct((part, model), bf16),
        ),
        in_specs=[VMEM] * 6,
        out_specs=(VMEM,) * 2,
        compiler_params=pltpu.CompilerParams(vmem_limit_bytes=8 * MIB),
        name="norm",
    )(stay, cross, behind, behind_cross, residual, norm_gain.reshape(1, model))

    bits = [1 << b for b in range(wide.bit_length() - 1)]
    gathered = normed
    for bit in bits[:0:-1]:
        gathered = jnp.concatenate([gathered, swapped(gathered, bit)], axis=0)
    far = swapped(gathered, bits[0])

    half = gathered.shape[0]
    weights = [gate_blocks, up_blocks, down_blocks]
    size = 2 * half * model * 4 + half * model * 10 + sum(w.size * 2 for w in weights)
    kept, sent = pl.pallas_call(
        feed_kernel,
        out_shape=(
            jax.ShapeDtypeStruct((half, model), f32),
            jax.ShapeDtypeStruct((half, model), bf16),
        ),
        in_specs=[SMEM] * 5 + [VMEM] * 2 + [ANY] * 3,
        out_specs=(VMEM,) * 2,
        scratch_shapes=[pltpu.VMEM(w.shape, bf16) for w in weights]
        + [pltpu.VMEM((2 * half, model), f32), pltpu.SemaphoreType.DMA((3, gate_blocks.shape[0]))],
        compiler_params=pltpu.CompilerParams(vmem_limit_bytes=size + 8 * MIB),
        name="feed",
    )(
        gate_up_keep, gate_scale, up_scale, down_keep, down_scale,
        gathered, far, gate_blocks, up_blocks, down_blocks,
    )

    for bit in bits:
        summed = kept + swapped(sent, bit).astype(f32)
        if bit != bits[-1]:
            half = half // 2
            kept, sent = summed[:half], summed[half:].astype(bf16)
    return (middle + summed).astype(bf16)


def solution(mesh):
    placed = (
        P("wide", "head"),
        P("wide", "head"),
        P("wide", "head"),
        P(None, "wide", None, "head"),
        P("wide", None),
        P("wide"),
        P("wide"),
        P(("wide", "head"), None),
        P(),
        P("wide", None, None, None),
        P("wide", None, None, None),
        P("wide", None),
        P("wide", None),
        P("wide", None),
        P("wide", None, None, None),
        P("wide", None),
        P("wide", None),
    )
    return jax.shard_map(
        per_device, mesh=mesh, in_specs=placed, out_specs=P(("wide", "head"), None), check_vma=False
    )
```

time: 231 us -> 80.6 us (0.35)
  waiting for transfers between devices: 92.5 us -> 21.7 us
  blocking collectives: 44.5 us -> 0 us
  other arithmetic: 30.1 us -> 2.59 us
  starting transfers between devices: 10.2 us -> 27 us
  matrix products: 16.5 us -> 0 us
  between operations: 14.4 us -> 0.14 us
  Pallas kernels: 0 us -> 13.8 us
  local copies, waits for them, and re-layouts: 22.3 us -> 14.8 us
    unnamed x2 -> x0, waiting for transfers between devices: 88.2 us -> none
    all_gather x1 -> x0, blocking collectives: 44.5 us -> none  [per_device(): gathered = lax.all_gather(normed, 'wide', axis=0, tiled=True)]
    scatter-add x1 -> x0, other arithmetic: 22.4 us -> none  [feed_forward(): placed = placed.at[:, down_keep.reshape(-1)].add(contrib)]
    ppermute x2 -> x12, waiting for transfers between devices: 0.4 us -> 21.7 us  [the longest x8 18.4 us: swapped(): lax.ppermute(block, 'wide', [(i, i ^ bit) for i in range(lax.axis_size('w...]
    ppermute x2 -> x12, starting transfers between devices: 6.88 us -> 27 us  [the longest x8 16.7 us: swapped(): lax.ppermute(block, 'wide', [(i, i ^ bit) for i in range(lax.axis_size('w...]
    dot_general x6 -> x0, matrix products: 16.5 us -> none  [the longest x1 6.47 us: ffn_terms(): jnp.einsum('rckd,ckdf->rckf', picked, up_blocks, preferred_element_type=j...]
    pallas_call x0 -> x3, Pallas kernels: none -> 13.8 us  [the longest x1 11.1 us: per_device(): pl.pallas_call(feed_kernel, out_shape=(jax.ShapeDtypeStruct((half, model)...]
    unnamed x35 -> x24, local copies, waits for them, and re-layouts: 1.35 us -> 14.6 us
  transfers between devices with their start and end apart: 4 -> 12, of which waited for: 3 -> 10; matrix products, arithmetic and copies ran while one was open for 1% -> 0% of each run, Pallas kernels for 0% -> 0%
where the time goes in v1:
time: 80.6 us; the launch traced here: 79.9 us
  starting transfers between devices  27 us (33%)
  waiting for transfers between devices  21.7 us (27%)
  local copies, waits for them, and re-layouts  14.8 us (18%)
  Pallas kernels  13.8 us (17%)
  other arithmetic  2.59 us (3%)
    ppermute x8, waiting for transfers between devices, swapped(): lax.ppermute(block, 'wide', [(i, i ^ bit) for i in range(lax.axis_size('w...  18.4 us
    ppermute x8, starting transfers between devices, swapped(): lax.ppermute(block, 'wide', [(i, i ^ bit) for i in range(lax.axis_size('w...  16.7 us
    unnamed x24, local copies, waits for them, and re-layouts  14.6 us
    pallas_call x1, Pallas kernels, per_device(): pl.pallas_call(feed_kernel, out_shape=(jax.ShapeDtypeStruct((half, model)...  11.1 us
    ppermute x1, starting transfers between devices, per_device(): behind = lax.ppermute(ahead, 'wide', [(i, i + 1) for i in range(wide - 1)])  3.7 us
    ppermute x1, starting transfers between devices, per_device(): cross = lax.ppermute(cross, 'head', [(h, 1 - h) for h in range(heads)])  3.03 us
    pallas_call x1, Pallas kernels, per_device(): pl.pallas_call(functools.partial(attend_kernel, groups, per_group), out_s...  2.46 us
    ppermute x1, starting transfers between devices, per_device(): lax.ppermute(ahead_cross, ('wide', 'head'), [(i * heads + h, (i + 1) * he...  2.29 us
  transfers between devices with their start and end apart: 12, of which 10 were waited for; matrix products, arithmetic and copies ran while one was open for 0% of the time, Pallas kernels for 0%

profile of v1, /device:TPU:0, one launch (start us, length us, event | category | flops | bytes accessed | tf_op | source)
XLA Modules:
  0.0 79.9 jit_solution(8410228958426002727)
XLA Ops:
  0.0 0.7 subtract_convert_fusion
  0.7 0.1 broadcast_in_dim.2
  0.7 0.8 %pad_maximum_fusion.3.own_ref = bf16[4,5248]{1,0:T(4,128)(2,1)S(1)} fusion(bf16[4,128]{1,0:T(4,128)(2,1)S(1)} %broadcast_in_dim.2, bf16[4,512]{1,0:T(4,128)(2,1)} %param.19, bf16[4,512]{1,0:T(4,128)(2,1)} %param.18, bf16[4,4096]{1,0:T(4,128)(2,1)} %param.17), kind=kLoop, calls=%fused_computation.12 | loop fusion | flops 167936 | bytes 83968 | tf_op jit(solution)/shard_map/concatenate | solution.py:180
  1.5 1.3 %collective-permute-start = (bf16[4,5248]{1,0:T(4,128)(2,1)S(1)}, bf16[4,5248]{1,0:T(4,128)(2,1)S(1)}, u32[]{:S(2)}, u32[]{:S(2)}) collective-permute-start(bf16[4,5248]{1,0:T(4,128)(2,1)S(1)} %pad_maximum_fusion.3.own_ref), channel_id=1, source_target_pairs={{2,0},{4,2},{6,4},{8,6},{10,8},{12,10},{14,12},{16,14},{18,16},{20... | collective-permute-start | bytes 125960 | tf_op jit(solution)/shard_map/ppermute | solution.py:183
  2.8 1.8 %collective-permute-done.next_ref = bf16[4,5248]{1,0:T(4,128)(2,1)S(1)} collective-permute-done((bf16[4,5248]{1,0:T(4,128)(2,1)S(1)}, bf16[4,5248]{1,0:T(4,128)(2,1)S(1)}, u32[]{:S(2)}, u32[]{:S(2)}) %collective-permute-start) | collective-permute-done | bytes 42016 | tf_op jit(solution)/shard_map/ppermute | solution.py:183
  4.7 0.0 copy-start.2
  4.7 1.6 %copy-done.2 = bf16[2,64,16,512]{3,2,1,0:T(8,128)(2,1)S(1)} copy-done((bf16[2,64,16,512]{3,2,1,0:T(8,128)(2,1)S(1)}, bf16[2,64,16,512]{3,2,1,0:T(8,128)(2,1)}, u32[]{:S(2)}) %copy-start.2) | copy-done | bytes 2097176
  6.3 0.0 copy-start.10
  6.3 0.7 copy-done.10
  6.9 0.0 copy-start.11
  6.9 0.7 copy-done.11
  7.6 2.5 %attend.1 = (bf16[2,4096]{1,0:T(2,128)(2,1)S(1)}, bf16[2,4096]{1,0:T(2,128)(2,1)S(1)}, bf16[2,4096]{1,0:T(2,128)(2,1)S(1)}, bf16[2,4096]{1,0:T(2,128)(2,1)S(1)}) custom-call(s32[4,16]{1,0:T(4,128)S(1)} %copy-done.10, s32[4]{0:T(128)S(1)} %copy-done.11, bf16[4,5248]{1,0:T(4,128)(2,1)S(1)} %pad_maximum_fusion.3.own_ref, ...), custom_call_target="tpu_custom_call" | custom-call | tf_op jit(solution)/shard_map/attend/pallas_call | solution.py:185
  10.1 3.0 %collective-permute-start.1 = (bf16[2,4096]{1,0:T(2,128)(2,1)S(1)}, bf16[2,4096]{1,0:T(2,128)(2,1)S(1)}, u32[]{:S(2)}, u32[]{:S(2)}) collective-permute-start(bf16[2,4096]{1,0:T(2,128)(2,1)S(1)} %get-tuple-element.14), channel_id=1, source_target_pairs={{0,1},{1,0},{2,3},{3,2},{4,5},{5,4},{6,7},{7,6},{8,9},{9,8},{10,11... | collective-permute-start | bytes 49160 | tf_op jit(solution)/shard_map/ppermute | solution.py:195
  13.1 3.7 %collective-permute-start.2 = (bf16[2,4096]{1,0:T(2,128)(2,1)S(1)}, bf16[2,4096]{1,0:T(2,128)(2,1)S(1)}, u32[]{:S(2)}, u32[]{:S(2)}) collective-permute-start(bf16[2,4096]{1,0:T(2,128)(2,1)S(1)} %get-tuple-element.15), channel_id=1, source_target_pairs={{0,2},{2,4},{4,6},{6,8},{8,10},{10,12},{12,14},{14,16},{16,18},{18... | collective-permute-start | bytes 49160 | tf_op jit(solution)/shard_map/ppermute | solution.py:196
  16.8 2.3 %collective-permute-start.3 = (bf16[2,4096]{1,0:T(2,128)(2,1)S(1)}, bf16[2,4096]{1,0:T(2,128)(2,1)S(1)}, u32[]{:S(2)}, u32[]{:S(2)}) collective-permute-start(bf16[2,4096]{1,0:T(2,128)(2,1)S(1)} %get-tuple-element.16), channel_id=1, source_target_pairs={{0,3},{1,2},{2,5},{3,4},{4,7},{5,6},{6,9},{7,8},{8,11},{9,10},{10,... | collective-permute-start | bytes 49160 | tf_op jit(solution)/shard_map/ppermute | solution.py:197
  19.1 0.0 collective-permute-done.1.cross_ref
  19.1 0.0 collective-permute-done.2.behind_ref
  19.1 1.4 %collective-permute-done.3.behind_cross_ref = bf16[2,4096]{1,0:T(2,128)(2,1)S(1)} collective-permute-done((bf16[2,4096]{1,0:T(2,128)(2,1)S(1)}, bf16[2,4096]{1,0:T(2,128)(2,1)S(1)}, u32[]{:S(2)}, u32[]{:S(2)}) %collective-permute-start.3) | collective-permute-done | bytes 16416 | tf_op jit(solution)/shard_map/ppermute | solution.py:197
  20.5 0.0 copy-start.3
  20.5 0.8 copy-done.3
  21.3 0.0 copy-start.4
  21.3 0.8 copy-done.4
  22.0 0.2 norm.1
  22.2 5.8 %collective-permute-start.4 = (bf16[2,8192]{1,0:T(2,128)(2,1)S(1)}, bf16[2,8192]{1,0:T(2,128)(2,1)S(1)}, u32[]{:S(2)}, u32[]{:S(2)}) collective-permute-start(bf16[2,8192]{1,0:T(2,128)(2,1)S(1)} %get-tuple-element.18), channel_id=1, source_target_pairs={{0,16},{2,18},{4,20},{6,22},{8,24},{10,26},{12,28},{14,30},{16,0},... | collective-permute-start | bytes 98312 | tf_op jit(solution)/shard_map/ppermute | solution.py:163
  28.0 1.9 %collective-permute-done.4 = bf16[2,8192]{1,0:T(2,128)(2,1)S(1)} collective-permute-done((bf16[2,8192]{1,0:T(2,128)(2,1)S(1)}, bf16[2,8192]{1,0:T(2,128)(2,1)S(1)}, u32[]{:S(2)}, u32[]{:S(2)}) %collective-permute-start.4) | collective-permute-done | bytes 32800 | tf_op jit(solution)/shard_map/ppermute | solution.py:163
  29.9 0.1 pad_maximum_fusion.2
  30.0 2.0 %collective-permute-start.5 = (bf16[4,8192]{1,0:T(4,128)(2,1)S(1)}, bf16[4,8192]{1,0:T(4,128)(2,1)S(1)}, u32[]{:S(2)}, u32[]{:S(2)}) collective-permute-start(bf16[4,8192]{1,0:T(4,128)(2,1)S(1)} %pad_maximum_fusion.2), channel_id=1, source_target_pairs={{0,8},{2,10},{4,12},{6,14},{8,0},{10,2},{12,4},{14,6},{16,24},{18,... | collective-permute-start | bytes 196616 | tf_op jit(solution)/shard_map/ppermute | solution.py:163
  32.0 2.4 %collective-permute-done.5 = bf16[4,8192]{1,0:T(4,128)(2,1)S(1)} collective-permute-done((bf16[4,8192]{1,0:T(4,128)(2,1)S(1)}, bf16[4,8192]{1,0:T(4,128)(2,1)S(1)}, u32[]{:S(2)}, u32[]{:S(2)}) %collective-permute-start.5) | collective-permute-done | bytes 65568 | tf_op jit(solution)/shard_map/ppermute | solution.py:163
  34.3 0.1 pad_maximum_fusion.1
  34.4 1.9 %collective-permute-start.6 = (bf16[8,8192]{1,0:T(8,128)(2,1)S(1)}, bf16[8,8192]{1,0:T(8,128)(2,1)S(1)}, u32[]{:S(2)}, u32[]{:S(2)}) collective-permute-start(bf16[8,8192]{1,0:T(8,128)(2,1)S(1)} %pad_maximum_fusion.1), channel_id=1, source_target_pairs={{0,4},{2,6},{4,0},{6,2},{8,12},{10,14},{12,8},{14,10},{16,20},{18,... | collective-permute-start | bytes 393224 | tf_op jit(solution)/shard_map/ppermute | solution.py:163
  36.3 3.2 %collective-permute-done.6 = bf16[8,8192]{1,0:T(8,128)(2,1)S(1)} collective-permute-done((bf16[8,8192]{1,0:T(8,128)(2,1)S(1)}, bf16[8,8192]{1,0:T(8,128)(2,1)S(1)}, u32[]{:S(2)}, u32[]{:S(2)}) %collective-permute-start.6) | collective-permute-done | bytes 131104 | tf_op jit(solution)/shard_map/ppermute | solution.py:163
  39.5 0.2 pad_maximum_fusion.near_ref
  39.6 0.1 collective-permute-start.7
  39.7 1.5 %collective-permute-done.7.far_ref = bf16[16,8192]{1,0:T(8,128)(2,1)S(1)} collective-permute-done((bf16[16,8192]{1,0:T(8,128)(2,1)S(1)}, bf16[16,8192]{1,0:T(8,128)(2,1)S(1)}, u32[]{:S(2)}, u32[]{:S(2)}) %collective-permute-start.7) | collective-permute-done | bytes 262176 | tf_op jit(solution)/shard_map/ppermute | solution.py:163
  41.2 0.0 copy-start
  41.2 3.4 %copy-done = bf16[8,32,128,128]{3,2,1,0:T(8,128)(2,1)S(1)} copy-done((bf16[8,32,128,128]{3,2,1,0:T(8,128)(2,1)S(1)}, bf16[8,32,128,128]{3,2,1,0:T(8,128)(2,1)}, u32[]{:S(2)}) %copy-start) | copy-done | bytes 8388632
  44.6 0.0 copy-start.1
  44.6 3.4 %copy-done.1 = bf16[8,32,128,128]{3,2,1,0:T(8,128)(2,1)S(1)} copy-done((bf16[8,32,128,128]{3,2,1,0:T(8,128)(2,1)S(1)}, bf16[8,32,128,128]{3,2,1,0:T(8,128)(2,1)}, u32[]{:S(2)}) %copy-start.1) | copy-done | bytes 8388632
  48.0 0.0 copy-start.5
  48.0 0.7 copy-done.5
  48.7 0.0 copy-start.6
  48.7 0.7 copy-done.6
  49.4 0.0 copy-start.7
  49.4 0.7 copy-done.7
  50.1 0.0 copy-start.8
  50.1 0.7 copy-done.8
  50.8 0.0 copy-start.9
  50.8 0.7 copy-done.9
  51.4 11.1 %feed.1 = (f32[16,8192]{1,0:T(8,128)S(1)}, bf16[16,8192]{1,0:T(8,128)(2,1)S(1)}) custom-call(s32[8,32]{1,0:T(8,128)S(1)} %copy-done.5, f32[8,32]{1,0:T(8,128)S(1)} %copy-done.6, f32[8,32]{1,0:T(8,128)S(1)} %copy-done.7, s32[8,32]{1,0:T(8,128)S(1)} %copy-done.8, f32[8,32]{1,0:T(8,128)S(1)} %copy-done.9, bf16[16,8192]{1,0:T(8,128)(2,1)S(1)} %pad_maximum_fusion.near_ref, ...), custom_call_target="tpu_custom_call" | custom-call | tf_op jit(solution)/shard_map/feed/pallas_call | solution.py:223
  62.6 0.2 collective-permute-start.8
  62.8 1.4 %collective-permute-done.8 = bf16[16,8192]{1,0:T(8,128)(2,1)S(1)} collective-permute-done((bf16[16,8192]{1,0:T(8,128)(2,1)S(1)}, bf16[16,8192]{1,0:T(8,128)(2,1)S(1)}, u32[]{:S(2)}, u32[]{:S(2)}) %collective-permute-start.8) | collective-permute-done | bytes 262176 | tf_op jit(solution)/shard_map/ppermute | solution.py:163
  64.2 1.9 %collective-permute-start.9 = (bf16[8,8192]{1,0:T(8,128)(2,1)S(1)}, bf16[8,8192]{1,0:T(8,128)(2,1)S(1)}, u32[]{:S(2)}, u32[]{:S(2)}) collective-permute-start(bf16[8,8192]{1,0:T(8,128)(2,1)S(1)} %slice.43), channel_id=1, source_target_pairs={{0,4},{2,6},{4,0},{6,2},{8,12},{10,14},{12,8},{14,10},{16,20},{18,... | collective-permute-start | bytes 393224 | tf_op jit(solution)/shard_map/ppermute | solution.py:163
  66.1 3.8 %collective-permute-done.9 = bf16[8,8192]{1,0:T(8,128)(2,1)S(1)} collective-permute-done((bf16[8,8192]{1,0:T(8,128)(2,1)S(1)}, bf16[8,8192]{1,0:T(8,128)(2,1)S(1)}, u32[]{:S(2)}, u32[]{:S(2)}) %collective-permute-start.9) | collective-permute-done | bytes 131104 | tf_op jit(solution)/shard_map/ppermute | solution.py:163
  70.0 1.9 %collective-permute-start.10 = (bf16[4,8192]{1,0:T(4,128)(2,1)S(1)}, bf16[4,8192]{1,0:T(4,128)(2,1)S(1)}, u32[]{:S(2)}, u32[]{:S(2)}) collective-permute-start(bf16[4,8192]{1,0:T(4,128)(2,1)S(1)} %slice.44), channel_id=1, source_target_pairs={{0,8},{2,10},{4,12},{6,14},{8,0},{10,2},{12,4},{14,6},{16,24},{18,... | collective-permute-start | bytes 196616 | tf_op jit(solution)/shard_map/ppermute | solution.py:163
  71.9 2.4 %collective-permute-done.10 = bf16[4,8192]{1,0:T(4,128)(2,1)S(1)} collective-permute-done((bf16[4,8192]{1,0:T(4,128)(2,1)S(1)}, bf16[4,8192]{1,0:T(4,128)(2,1)S(1)}, u32[]{:S(2)}, u32[]{:S(2)}) %collective-permute-start.10) | collective-permute-done | bytes 65568 | tf_op jit(solution)/shard_map/ppermute | solution.py:163
  74.4 3.0 %collective-permute-start.11 = (bf16[2,8192]{1,0:T(2,128)(2,1)S(1)}, bf16[2,8192]{1,0:T(2,128)(2,1)S(1)}, u32[]{:S(2)}, u32[]{:S(2)}) collective-permute-start(bf16[2,8192]{1,0:T(2,128)(2,1)S(1)} %slice.45), channel_id=1, source_target_pairs={{0,16},{2,18},{4,20},{6,22},{8,24},{10,26},{12,28},{14,30},{16,0},... | collective-permute-start | bytes 98312 | tf_op jit(solution)/shard_map/ppermute | solution.py:163
  77.4 1.9 %collective-permute-done.11 = bf16[2,8192]{1,0:T(2,128)(2,1)S(1)} collective-permute-done((bf16[2,8192]{1,0:T(2,128)(2,1)S(1)}, bf16[2,8192]{1,0:T(2,128)(2,1)S(1)}, u32[]{:S(2)}, u32[]{:S(2)}) %collective-permute-start.11) | collective-permute-done | bytes 32800 | tf_op jit(solution)/shard_map/ppermute | solution.py:163
  79.3 0.7 fusion.1
  (6 shorter events, 0.2 us)
Async XLA Ops:
  1.5 3.1 %collective-permute-start = (bf16[4,5248]{1,0:T(4,128)(2,1)S(1)}, bf16[4,5248]{1,0:T(4,128)(2,1)S(1)}, u32[]{:S(2)}, u32[]{:S(2)}) collective-permute-start(bf16[4,5248]{1,0:T(4,128)(2,1)S(1)} %pad_maximum_fusion.3.own_ref), channel_id=1, source_target_pairs={{2,0},{4,2},{6,4},{8,6},{10,8},{12,10},{14,12},{16,14},{18,16},{20... | collective-permute-start | bytes 125960 | tf_op jit(solution)/shard_map/ppermute | solution.py:183
  4.7 1.6 %copy-start.2 = (bf16[2,64,16,512]{3,2,1,0:T(8,128)(2,1)S(1)}, bf16[2,64,16,512]{3,2,1,0:T(8,128)(2,1)}, u32[]{:S(2)}) copy-start(bf16[2,64,16,512]{3,2,1,0:T(8,128)(2,1)} %pool_ref.1) | copy-start | bytes 6291460
  6.3 0.7 copy-start.10
  6.9 0.7 copy-start.11
  10.1 9.0 %collective-permute-start.1 = (bf16[2,4096]{1,0:T(2,128)(2,1)S(1)}, bf16[2,4096]{1,0:T(2,128)(2,1)S(1)}, u32[]{:S(2)}, u32[]{:S(2)}) collective-permute-start(bf16[2,4096]{1,0:T(2,128)(2,1)S(1)} %get-tuple-element.14), channel_id=1, source_target_pairs={{0,1},{1,0},{2,3},{3,2},{4,5},{5,4},{6,7},{7,6},{8,9},{9,8},{10,11... | collective-permute-start | bytes 49160 | tf_op jit(solution)/shard_map/ppermute | solution.py:195
  13.1 6.0 %collective-permute-start.2 = (bf16[2,4096]{1,0:T(2,128)(2,1)S(1)}, bf16[2,4096]{1,0:T(2,128)(2,1)S(1)}, u32[]{:S(2)}, u32[]{:S(2)}) collective-permute-start(bf16[2,4096]{1,0:T(2,128)(2,1)S(1)} %get-tuple-element.15), channel_id=1, source_target_pairs={{0,2},{2,4},{4,6},{6,8},{8,10},{10,12},{12,14},{14,16},{16,18},{18... | collective-permute-start | bytes 49160 | tf_op jit(solution)/shard_map/ppermute | solution.py:196
  16.8 3.7 %collective-permute-start.3 = (bf16[2,4096]{1,0:T(2,128)(2,1)S(1)}, bf16[2,4096]{1,0:T(2,128)(2,1)S(1)}, u32[]{:S(2)}, u32[]{:S(2)}) collective-permute-start(bf16[2,4096]{1,0:T(2,128)(2,1)S(1)} %get-tuple-element.16), channel_id=1, source_target_pairs={{0,3},{1,2},{2,5},{3,4},{4,7},{5,6},{6,9},{7,8},{8,11},{9,10},{10,... | collective-permute-start | bytes 49160 | tf_op jit(solution)/shard_map/ppermute | solution.py:197
  20.5 0.8 copy-start.3
  21.3 0.8 copy-start.4
  22.2 7.7 %collective-permute-start.4 = (bf16[2,8192]{1,0:T(2,128)(2,1)S(1)}, bf16[2,8192]{1,0:T(2,128)(2,1)S(1)}, u32[]{:S(2)}, u32[]{:S(2)}) collective-permute-start(bf16[2,8192]{1,0:T(2,128)(2,1)S(1)} %get-tuple-element.18), channel_id=1, source_target_pairs={{0,16},{2,18},{4,20},{6,22},{8,24},{10,26},{12,28},{14,30},{16,0},... | collective-permute-start | bytes 98312 | tf_op jit(solution)/shard_map/ppermute | solution.py:163
  30.0 4.3 %collective-permute-start.5 = (bf16[4,8192]{1,0:T(4,128)(2,1)S(1)}, bf16[4,8192]{1,0:T(4,128)(2,1)S(1)}, u32[]{:S(2)}, u32[]{:S(2)}) collective-permute-start(bf16[4,8192]{1,0:T(4,128)(2,1)S(1)} %pad_maximum_fusion.2), channel_id=1, source_target_pairs={{0,8},{2,10},{4,12},{6,14},{8,0},{10,2},{12,4},{14,6},{16,24},{18,... | collective-permute-start | bytes 196616 | tf_op jit(solution)/shard_map/ppermute | solution.py:163
  34.4 5.0 %collective-permute-start.6 = (bf16[8,8192]{1,0:T(8,128)(2,1)S(1)}, bf16[8,8192]{1,0:T(8,128)(2,1)S(1)}, u32[]{:S(2)}, u32[]{:S(2)}) collective-permute-start(bf16[8,8192]{1,0:T(8,128)(2,1)S(1)} %pad_maximum_fusion.1), channel_id=1, source_target_pairs={{0,4},{2,6},{4,0},{6,2},{8,12},{10,14},{12,8},{14,10},{16,20},{18,... | collective-permute-start | bytes 393224 | tf_op jit(solution)/shard_map/ppermute | solution.py:163
  39.6 1.6 %collective-permute-start.7 = (bf16[16,8192]{1,0:T(8,128)(2,1)S(1)}, bf16[16,8192]{1,0:T(8,128)(2,1)S(1)}, u32[]{:S(2)}, u32[]{:S(2)}) collective-permute-start(bf16[16,8192]{1,0:T(8,128)(2,1)S(1)} %pad_maximum_fusion.near_ref), channel_id=1, source_target_pairs={{0,2},{2,0},{4,6},{6,4},{8,10},{10,8},{12,14},{14,12},{16,18},{18,... | collective-permute-start | bytes 786440 | tf_op jit(solution)/shard_map/ppermute | solution.py:163
  41.2 3.4 %copy-start = (bf16[8,32,128,128]{3,2,1,0:T(8,128)(2,1)S(1)}, bf16[8,32,128,128]{3,2,1,0:T(8,128)(2,1)}, u32[]{:S(2)}) copy-start(bf16[8,32,128,128]{3,2,1,0:T(8,128)(2,1)} %gate_hbm.1) | copy-start | bytes 25165828
  44.6 3.4 %copy-start.1 = (bf16[8,32,128,128]{3,2,1,0:T(8,128)(2,1)S(1)}, bf16[8,32,128,128]{3,2,1,0:T(8,128)(2,1)}, u32[]{:S(2)}) copy-start(bf16[8,32,128,128]{3,2,1,0:T(8,128)(2,1)} %up_hbm.1) | copy-start | bytes 25165828
  48.0 0.7 copy-start.5
  48.7 0.7 copy-start.6
  49.4 0.7 copy-start.7
  50.1 0.7 copy-start.8
  50.8 0.7 copy-start.9
  62.6 1.6 %collective-permute-start.8 = (bf16[16,8192]{1,0:T(8,128)(2,1)S(1)}, bf16[16,8192]{1,0:T(8,128)(2,1)S(1)}, u32[]{:S(2)}, u32[]{:S(2)}) collective-permute-start(bf16[16,8192]{1,0:T(8,128)(2,1)S(1)} %get-tuple-element.20), channel_id=1, source_target_pairs={{0,2},{2,0},{4,6},{6,4},{8,10},{10,8},{12,14},{14,12},{16,18},{18,... | collective-permute-start | bytes 786440 | tf_op jit(solution)/shard_map/ppermute | solution.py:163
  64.2 5.7 %collective-permute-start.9 = (bf16[8,8192]{1,0:T(8,128)(2,1)S(1)}, bf16[8,8192]{1,0:T(8,128)(2,1)S(1)}, u32[]{:S(2)}, u32[]{:S(2)}) collective-permute-start(bf16[8,8192]{1,0:T(8,128)(2,1)S(1)} %slice.43), channel_id=1, source_target_pairs={{0,4},{2,6},{4,0},{6,2},{8,12},{10,14},{12,8},{14,10},{16,20},{18,... | collective-permute-start | bytes 393224 | tf_op jit(solution)/shard_map/ppermute | solution.py:163
  70.0 4.3 %collective-permute-start.10 = (bf16[4,8192]{1,0:T(4,128)(2,1)S(1)}, bf16[4,8192]{1,0:T(4,128)(2,1)S(1)}, u32[]{:S(2)}, u32[]{:S(2)}) collective-permute-start(bf16[4,8192]{1,0:T(4,128)(2,1)S(1)} %slice.44), channel_id=1, source_target_pairs={{0,8},{2,10},{4,12},{6,14},{8,0},{10,2},{12,4},{14,6},{16,24},{18,... | collective-permute-start | bytes 196616 | tf_op jit(solution)/shard_map/ppermute | solution.py:163
  74.4 4.9 %collective-permute-start.11 = (bf16[2,8192]{1,0:T(2,128)(2,1)S(1)}, bf16[2,8192]{1,0:T(2,128)(2,1)S(1)}, u32[]{:S(2)}, u32[]{:S(2)}) collective-permute-start(bf16[2,8192]{1,0:T(2,128)(2,1)S(1)} %slice.45), channel_id=1, source_target_pairs={{0,16},{2,18},{4,20},{6,22},{8,24},{10,26},{12,28},{14,30},{16,0},... | collective-permute-start | bytes 98312 | tf_op jit(solution)/shard_map/ppermute | solution.py:163

commit v2 on v1

--- a/solution.py
+++ b/solution.py
@@ -15,28 +15,55 @@
 
 VMEM = pl.BlockSpec(memory_space=pltpu.VMEM)
 SMEM = pl.BlockSpec(memory_space=pltpu.SMEM)
-ANY = pl.BlockSpec(memory_space=pl.ANY)
-
-
-def attend_kernel(
-    groups, per_group, page_ref, length_ref, own_ref, next_ref, pool_ref,
-    stay_ref, cross_ref, ahead_ref, ahead_cross_ref, mixed,
-):
+HBM = pl.BlockSpec(memory_space=pltpu.HBM)
+
+
+def copies(pairs, sems):
+    return [
+        pltpu.make_async_copy(source, target, sems.at[i])
+        for i, (source, target) in enumerate(pairs)
+    ]
+
+
+def prepare_kernel(count, *refs):
+    page_hbm, length_hbm, sources = refs[0], refs[1], refs[2 : 2 + count]
+    targets = refs[2 + count : 2 + 2 * count]
+    bias_ref, page_ref, length_ref, sems = refs[2 + 2 * count :]
+    spots = bias_ref.shape[1]
+    page = spots // sources[0].shape[1]
+    lists = copies(((page_hbm, page_ref), (length_hbm, length_ref)), sems.at[pl.ds(0, 2)])
+    moves = copies(
+        [(s if s.shape == t.shape else s.at[pl.ds(0, t.shape[0])], t) for s, t in zip(sources, targets)],
+        sems.at[pl.ds(2, count)],
+    )
+    for move in lists + moves:
+        move.start()
+    for move in lists:
+        move.wait()
+    spot = lax.broadcasted_iota(jnp.int32, (1, spots), 1)
+    page_of, offset = spot // page, spot % page
+    for r in range(bias_ref.shape[0]):
+        place = jnp.full((1, spots), 1 << 20, jnp.int32)
+        for i in range(page_ref.shape[1]):
+            place = jnp.where(page_of == page_ref[r, i], i * page, place)
+        bias_ref[r : r + 1, :] = jnp.where(place + offset < length_ref[r], 0.0, DEAD)
+    for move in moves:
+        move.wait()
+
+
+def attend_kernel(groups, per_group, skip, own_ref, next_ref, pool_ref, bias_ref, *refs):
+    extra = (len(refs) - 6) // 2
+    sources, targets = refs[:extra], refs[extra + 4 : 2 * extra + 4]
+    stay_ref, cross_ref, ahead_ref, ahead_cross_ref = refs[extra : extra + 4]
+    mixed, sems = refs[-2:]
+    moves = copies([(s.at[pl.ds(skip, t.shape[0])], t) for s, t in zip(sources, targets)], sems)
+    for move in moves:
+        move.start()
     rows = own_ref.shape[0]
     width = groups * per_group * HD
     kv_width = groups * HD
-    pages, page = pool_ref.shape[1], pool_ref.shape[2]
-    spots = pages * page
+    spots = bias_ref.shape[1]
     head = lax.axis_index("head")
-
-    spot = lax.broadcasted_iota(jnp.int32, (1, spots), 1)
-    page_of, offset = spot // page, spot % page
-    biases = []
-    for r in range(rows):
-        place = jnp.full((1, spots), 1 << 20, jnp.int32)
-        for i in range(page_ref.shape[1]):
-            place = jnp.where(page_of == page_ref[r, i], i * page, place)
-        biases.append(jnp.where(place + offset < length_ref[r], 0.0, DEAD))
 
     both = jnp.concatenate(
         [own_ref[...].astype(jnp.float32), next_ref[...].astype(jnp.float32)], axis=0
@@ -45,7 +72,7 @@
     parent = both[:, width + 2 * kv_width : width + 2 * kv_width + 1] + shift.astype(jnp.float32)
     bias = jnp.full((2 * rows, spots), DEAD, jnp.float32)
     for r in range(rows):
-        bias = jnp.where(parent == r, biases[r], bias)
+        bias = jnp.where(parent == r, bias_ref[r : r + 1, :], bias)
     here = (parent >= 0) & (parent < rows)
 
     factor = 1.0 / math.sqrt(HD)
@@ -85,6 +112,8 @@
         high = mixed[start + part : start + 2 * part, :]
         mine_ref[...] = jnp.where(head == 0, low, high).astype(jnp.bfloat16)
         other_ref[...] = jnp.where(head == 0, high, low).astype(jnp.bfloat16)
+    for move in moves:
+        move.wait()
 
 
 def norm_kernel(
@@ -110,53 +139,62 @@
 
 
 def feed_kernel(
-    keep_ref, gate_scale_ref, up_scale_ref, down_keep_ref, down_scale_ref,
-    near_ref, far_ref, gate_hbm, up_hbm, down_hbm,
-    stay_ref, send_ref,
-    gate, up, down, total, sems,
+    brought, keep_ref, gate_scale_ref, up_scale_ref, down_keep_ref, down_scale_ref,
+    near_ref, far_ref, gate_hbm, up_hbm, down_hbm, *refs,
 ):
     columns, keep = keep_ref.shape
     half = near_ref.shape[0]
-    pairs = ((gate_hbm, gate), (up_hbm, up), (down_hbm, down))
-
-    def fetch(which, c):
-        source, target = pairs[which]
-        return pltpu.make_async_copy(source.at[c], target.at[c], sems.at[which, c])
-
-    def begin(c, carry):
-        for which in range(3):
-            fetch(which, c).start()
-        return carry
-
-    lax.fori_loop(0, columns, begin, 0)
+    stay_ref, send_ref, gate_rest, up_rest, down, hidden, total, sems = refs[-8:]
+    pieces = refs[:-8]
+    gates, ups = [], []
+    for gate_piece, up_piece in zip(pieces[0::2], pieces[1::2]):
+        gates += [gate_piece.at[i] for i in range(gate_piece.shape[0])]
+        ups += [up_piece.at[i] for i in range(up_piece.shape[0])]
+    rest = columns - brought
+    gates += [gate_rest.at[i] for i in range(rest)]
+    ups += [up_rest.at[i] for i in range(rest)]
+    gate_moves = copies([(gate_hbm.at[brought + i], gate_rest.at[i]) for i in range(rest)], sems.at[0])
+    up_moves = copies([(up_hbm.at[brought + i], up_rest.at[i]) for i in range(rest)], sems.at[1])
+    down_moves = copies([(down_hbm.at[i], down.at[i]) for i in range(columns)], sems.at[2])
+    for gate_move, up_move in zip(gate_moves, up_moves):
+        gate_move.start()
+        up_move.start()
+    for move in down_moves:
+        move.start()
     total[...] = jnp.zeros_like(total)
 
-    def column(c, carry):
-        fetch(0, c).wait()
-        fetch(1, c).wait()
+    for c in range(columns):
+        if c >= brought:
+            gate_moves[c - brought].wait()
+            up_moves[c - brought].wait()
         gate_sum = jnp.zeros((2 * half, BLK), jnp.float32)
         up_sum = jnp.zeros((2 * half, BLK), jnp.float32)
         for k in range(keep):
             where = pl.ds(pl.multiple_of(keep_ref[c, k] * BLK, BLK), BLK)
             picked = jnp.concatenate([near_ref[:, where], far_ref[:, where]], axis=0)
-            gate_sum += gate_scale_ref[c, k] * jnp.dot(
-                picked, gate[c, k], preferred_element_type=jnp.float32
+            both = jnp.dot(
+                picked, jnp.concatenate([gates[c][k], ups[c][k]], axis=1),
+                preferred_element_type=jnp.float32,
             )
-            up_sum += up_scale_ref[c, k] * jnp.dot(
-                picked, up[c, k], preferred_element_type=jnp.float32
+            gate_sum += gate_scale_ref[c, k] * both[:, :BLK]
+            up_sum += up_scale_ref[c, k] * both[:, BLK:]
+        hidden[c] = (gate_sum / (1.0 + jnp.exp(-gate_sum)) * up_sum).astype(jnp.bfloat16)
+    for c in range(columns):
+        down_moves[c].wait()
+        for k in range(0, keep, 2):
+            both = jnp.dot(
+                hidden[c], jnp.concatenate([down[c, k], down[c, k + 1]], axis=1),
+                preferred_element_type=jnp.float32,
             )
-        hidden = (gate_sum / (1.0 + jnp.exp(-gate_sum)) * up_sum).astype(jnp.bfloat16)
-        fetch(2, c).wait()
-        for k in range(keep):
-            where = pl.ds(pl.multiple_of(down_keep_ref[c, k] * BLK, BLK), BLK)
-            total[:, where] += down_scale_ref[c, k] * jnp.dot(
-                hidden, down[c, k], preferred_element_type=jnp.float32
-            )
-        return carry
-
-    lax.fori_loop(0, columns, column, 0)
+            for j in range(2):
+                where = pl.ds(pl.multiple_of(down_keep_ref[c, k + j] * BLK, BLK), BLK)
+                total[:, where] += down_scale_ref[c, k + j] * both[:, j * BLK : (j + 1) * BLK]
     stay_ref[...] = total[:half, :]
     send_ref[...] = total[half:, :].astype(jnp.bfloat16)
+
+
+def in_hbm(arrays):
+    return [pltpu.with_memory_space_constraint(a, pltpu.HBM) for a in arrays]
 
 
 def swapped(block, bit):
@@ -181,16 +219,46 @@
         [branch_query, key_new, value_new, jnp.broadcast_to(relative[:, None], (rows, HD))], axis=1
     )
     following = lax.ppermute(own, "wide", [(i, i - 1) for i in range(1, wide)])
+    gain = norm_gain.reshape(1, model)
+    columns = gate_blocks.shape[0]
+    quarter = columns // 4
+    portion = [jax.ShapeDtypeStruct((quarter, *gate_blocks.shape[1:]), bf16)] * (2 if quarter else 0)
+    stored = [pool_pages, residual, gain, gate_up_keep, gate_scale, up_scale, down_keep, down_scale]
+    shapes = [jax.ShapeDtypeStruct(a.shape, a.dtype) for a in stored] + portion
+    moved = stored + [gate_blocks, up_blocks][: len(portion)]
+    spots = pool_pages.shape[1] * pool_pages.shape[2]
+    prepared = pl.pallas_call(
+        functools.partial(prepare_kernel, len(moved)),
+        out_shape=(*shapes, jax.ShapeDtypeStruct((rows, spots), f32)),
+        in_specs=[HBM] * (2 + len(moved)),
+        out_specs=(VMEM,) * (len(moved) + 1),
+        scratch_shapes=[
+            pltpu.SMEM(page_table.shape, jnp.int32),
+            pltpu.SMEM(tail_length.shape, jnp.int32),
+            pltpu.SemaphoreType.DMA((2 + len(moved),)),
+        ],
+        compiler_params=pltpu.CompilerParams(vmem_limit_bytes=4 * MIB),
+        cost_estimate=pl.CostEstimate(flops=0, bytes_accessed=8 * MIB, transcendentals=0),
+        name="prepare",
+    )(*in_hbm([page_table, tail_length, *moved]))
+    pool, residual, gain, *lists = prepared[: len(stored)]
+    pieces = list(prepared[len(stored) : -1])
+    bias = prepared[-1]
+
     piece = jax.ShapeDtypeStruct((part, width), bf16)
-    stay, cross, ahead, ahead_cross = pl.pallas_call(
-        functools.partial(attend_kernel, groups, per_group),
-        out_shape=(piece,) * 4,
-        in_specs=[SMEM, SMEM, VMEM, VMEM, VMEM],
-        out_specs=(VMEM,) * 4,
-        scratch_shapes=[pltpu.VMEM((2 * rows, width), f32)],
-        compiler_params=pltpu.CompilerParams(vmem_limit_bytes=24 * MIB),
+    stay, cross, ahead, ahead_cross, *more = pl.pallas_call(
+        functools.partial(attend_kernel, groups, per_group, quarter),
+        out_shape=(*(piece,) * 4, *portion),
+        in_specs=[VMEM] * 4 + [HBM] * len(portion),
+        out_specs=(VMEM,) * (4 + len(portion)),
+        scratch_shapes=[
+            pltpu.VMEM((2 * rows, width), f32),
+            pltpu.SemaphoreType.DMA((max(len(portion), 1),)),
+        ],
+        compiler_params=pltpu.CompilerParams(vmem_limit_bytes=8 * MIB),
         name="attend",
-    )(page_table, tail_length, own, following, pool_pages)
+    )(own, following, pool, bias, *in_hbm([gate_blocks, up_blocks][: len(portion)]))
+    pieces += more
 
     cross = lax.ppermute(cross, "head", [(h, 1 - h) for h in range(heads)])
     behind = lax.ppermute(ahead, "wide", [(i, i + 1) for i in range(wide - 1)])
@@ -209,7 +277,7 @@
         out_specs=(VMEM,) * 2,
         compiler_params=pltpu.CompilerParams(vmem_limit_bytes=8 * MIB),
         name="norm",
-    )(stay, cross, behind, behind_cross, residual, norm_gain.reshape(1, model))
+    )(stay, cross, behind, behind_cross, residual, gain)
 
     bits = [1 << b for b in range(wide.bit_length() - 1)]
     gathered = normed
@@ -218,24 +286,27 @@
     far = swapped(gathered, bits[0])
 
     half = gathered.shape[0]
-    weights = [gate_blocks, up_blocks, down_blocks]
-    size = 2 * half * model * 4 + half * model * 10 + sum(w.size * 2 for w in weights)
+    rest = jax.ShapeDtypeStruct((columns - 2 * quarter, *gate_blocks.shape[1:]), bf16)
+    size = 2 * half * model * 4 + half * model * 10 + 2 * (2 * rest.size + down_blocks.size)
     kept, sent = pl.pallas_call(
-        feed_kernel,
+        functools.partial(feed_kernel, 2 * quarter),
         out_shape=(
             jax.ShapeDtypeStruct((half, model), f32),
             jax.ShapeDtypeStruct((half, model), bf16),
         ),
-        in_specs=[SMEM] * 5 + [VMEM] * 2 + [ANY] * 3,
+        in_specs=[SMEM] * 5 + [VMEM] * 2 + [HBM] * 3 + [VMEM] * len(pieces),
         out_specs=(VMEM,) * 2,
-        scratch_shapes=[pltpu.VMEM(w.shape, bf16) for w in weights]
-        + [pltpu.VMEM((2 * half, model), f32), pltpu.SemaphoreType.DMA((3, gate_blocks.shape[0]))],
-        compiler_params=pltpu.CompilerParams(vmem_limit_bytes=size + 8 * MIB),
+        scratch_shapes=[
+            pltpu.VMEM(rest.shape, bf16),
+            pltpu.VMEM(rest.shape, bf16),
+            pltpu.VMEM(down_blocks.shape, bf16),
+            pltpu.VMEM((columns, 2 * half, BLK), bf16),
+            pltpu.VMEM((2 * half, model), f32),
+            pltpu.SemaphoreType.DMA((3, columns)),
+        ],
+        compiler_params=pltpu.CompilerParams(vmem_limit_bytes=size + 4 * MIB),
         name="feed",
-    )(
-        gate_up_keep, gate_scale, up_scale, down_keep, down_scale,
-        gathered, far, gate_blocks, up_blocks, down_blocks,
-    )
+    )(*lists, gathered, far, *in_hbm([gate_blocks, up_blocks, down_blocks]), *pieces)
 
     for bit in bits:
         summed = kept + swapped(sent, bit).astype(f32)

time: 80.6 us -> 65.3 us (0.81)
  local copies, waits for them, and re-layouts: 14.8 us -> 0.16 us
  Pallas kernels: 13.8 us -> 15.7 us
  starting transfers between devices: 27 us -> 25.1 us
    unnamed x24 -> x0, local copies, waits for them, and re-layouts: 14.6 us -> none
    ppermute x8, starting transfers between devices: 16.7 us -> 14.7 us  [swapped(): lax.ppermute(block, 'wide', [(i, i ^ bit) for i in range(lax.axis_size('w...]
    pallas_call x2 -> x3, Pallas kernels: 13.6 us -> 15.5 us  [the longest x1 8.78 us: per_device(): pl.pallas_call(functools.partial(feed_kernel, 2 * quarter), out_shape=(ja...]
    ppermute x1, waiting for transfers between devices: 1.81 us -> 0.01 us  [per_device(): following = lax.ppermute(own, 'wide', [(i, i - 1) for i in range(1, wide)])]
    ppermute x8, waiting for transfers between devices: 18.4 us -> 19.9 us  [swapped(): lax.ppermute(block, 'wide', [(i, i ^ bit) for i in range(lax.axis_size('w...]
    ppermute x1, starting transfers between devices: 2.29 us -> 3.41 us  [per_device(): lax.ppermute(ahead_cross, ('wide', 'head'), [(i * heads + h, (i + 1) * he...]
    ppermute x1, starting transfers between devices: 3.7 us -> 2.74 us  [per_device(): behind = lax.ppermute(ahead, 'wide', [(i, i + 1) for i in range(wide - 1)])]
  transfers between devices with their start and end apart: 12 -> 12, of which waited for: 10 -> 9; matrix products, arithmetic and copies ran while one was open for 0% -> 0% of each run, Pallas kernels for 0% -> 5%
where the time goes in v2:
time: 65.3 us; the launch traced here: 65 us
  starting transfers between devices  25.1 us (38%)
  waiting for transfers between devices  21.3 us (33%)
  Pallas kernels  15.7 us (24%)
  other arithmetic  2.59 us (4%)
    ppermute x8, waiting for transfers between devices, swapped(): lax.ppermute(block, 'wide', [(i, i ^ bit) for i in range(lax.axis_size('w...  19.9 us
    ppermute x8, starting transfers between devices, swapped(): lax.ppermute(block, 'wide', [(i, i ^ bit) for i in range(lax.axis_size('w...  14.7 us
    pallas_call x1, Pallas kernels, per_device(): pl.pallas_call(functools.partial(feed_kernel, 2 * quarter), out_shape=(ja...  8.78 us
    pallas_call x1, Pallas kernels, per_device(): pl.pallas_call(functools.partial(attend_kernel, groups, per_group, quarte...  3.63 us
    ppermute x1, starting transfers between devices, per_device(): lax.ppermute(ahead_cross, ('wide', 'head'), [(i * heads + h, (i + 1) * he...  3.41 us
    pallas_call x1, Pallas kernels, per_device(): pl.pallas_call(functools.partial(prepare_kernel, len(moved)), out_shape=(...  3.1 us
    ppermute x1, starting transfers between devices, per_device(): cross = lax.ppermute(cross, 'head', [(h, 1 - h) for h in range(heads)])  3.03 us
    ppermute x1, starting transfers between devices, per_device(): behind = lax.ppermute(ahead, 'wide', [(i, i + 1) for i in range(wide - 1)])  2.74 us
  transfers between devices with their start and end apart: 12, of which 9 were waited for; matrix products, arithmetic and copies ran while one was open for 0% of the time, Pallas kernels for 5%

profile of v2, /device:TPU:0, one launch (start us, length us, event | category | flops | bytes accessed | tf_op | source)
XLA Modules:
  0.0 65.0 jit_solution(4066080127121378263)
XLA Ops:
  0.0 0.7 %subtract_convert_fusion = bf16[4]{0:T(256)(128)(2,1)S(1)} fusion(s32[4]{0:T(128)} %param.23, s32[]{:T(128)S(6)} %mul.3), kind=kLoop, calls=%fused_computation.13 | loop fusion | flops 8 | bytes 28 | tf_op jit(solution)/shard_map/convert_element_type | solution.py:217
  0.7 0.1 broadcast_in_dim.2
  0.7 0.8 %pad_maximum_fusion.3.own_ref = bf16[4,5248]{1,0:T(4,128)(2,1)S(1)} fusion(bf16[4,128]{1,0:T(4,128)(2,1)S(1)} %broadcast_in_dim.2, bf16[4,512]{1,0:T(4,128)(2,1)} %param.19, bf16[4,512]{1,0:T(4,128)(2,1)} %param.18, bf16[4,4096]{1,0:T(4,128)(2,1)} %param.17), kind=kLoop, calls=%fused_computation.12 | loop fusion | flops 167936 | bytes 83968 | tf_op jit(solution)/shard_map/concatenate | solution.py:218
  1.5 1.3 %collective-permute-start = (bf16[4,5248]{1,0:T(4,128)(2,1)S(1)}, bf16[4,5248]{1,0:T(4,128)(2,1)S(1)}, u32[]{:S(2)}, u32[]{:S(2)}) collective-permute-start(bf16[4,5248]{1,0:T(4,128)(2,1)S(1)} %pad_maximum_fusion.3.own_ref), channel_id=1, source_target_pairs={{2,0},{4,2},{6,4},{8,6},{10,8},{12,10},{14,12},{16,14},{18,16},{20... | collective-permute-start | bytes 125960 | tf_op jit(solution)/shard_map/ppermute | solution.py:221
  2.8 3.1 %prepare.1 = (bf16[2,64,16,512]{3,2,1,0:T(8,128)(2,1)S(1)}, bf16[2,8192]{1,0:T(2,128)(2,1)S(1)}, f32[1,8192]{1,0:T(1,128)S(1)}, s32[8,32]{1,0:T(8,128)S(1)}, f32...) custom-call(s32[4,16]{1,0:T(4,128)} %refs_0_.2, ...), custom_call_target="tpu_custom_call" | custom-call | bytes 8388608 | tf_op jit(solution)/shard_map/prepare/pallas_call | solution.py:230
  6.0 0.0 collective-permute-done.next_ref
  6.0 3.6 %attend.1 = (bf16[2,4096]{1,0:T(2,128)(2,1)S(1)}, bf16[2,4096]{1,0:T(2,128)(2,1)S(1)}, bf16[2,4096]{1,0:T(2,128)(2,1)S(1)}, bf16[2,4096]{1,0:T(2,128)(2,1)S(1)},...) custom-call(bf16[4,5248]{1,0:T(4,128)(2,1)S(1)} %pad_maximum_fusion.3.own_ref, ...), custom_call_target="tpu_custom_call" | custom-call | tf_op jit(solution)/shard_map/attend/pallas_call | solution.py:249
  9.6 3.0 %collective-permute-start.1 = (bf16[2,4096]{1,0:T(2,128)(2,1)S(1)}, bf16[2,4096]{1,0:T(2,128)(2,1)S(1)}, u32[]{:S(2)}, u32[]{:S(2)}) collective-permute-start(bf16[2,4096]{1,0:T(2,128)(2,1)S(1)} %get-tuple-element.29), channel_id=1, source_target_pairs={{0,1},{1,0},{2,3},{3,2},{4,5},{5,4},{6,7},{7,6},{8,9},{9,8},{10,11... | collective-permute-start | bytes 49160 | tf_op jit(solution)/shard_map/ppermute | solution.py:263
  12.6 2.7 %collective-permute-start.2 = (bf16[2,4096]{1,0:T(2,128)(2,1)S(1)}, bf16[2,4096]{1,0:T(2,128)(2,1)S(1)}, u32[]{:S(2)}, u32[]{:S(2)}) collective-permute-start(bf16[2,4096]{1,0:T(2,128)(2,1)S(1)} %get-tuple-element.30), channel_id=1, source_target_pairs={{0,2},{2,4},{4,6},{6,8},{8,10},{10,12},{12,14},{14,16},{16,18},{18... | collective-permute-start | bytes 49160 | tf_op jit(solution)/shard_map/ppermute | solution.py:264
  15.4 3.4 %collective-permute-start.3 = (bf16[2,4096]{1,0:T(2,128)(2,1)S(1)}, bf16[2,4096]{1,0:T(2,128)(2,1)S(1)}, u32[]{:S(2)}, u32[]{:S(2)}) collective-permute-start(bf16[2,4096]{1,0:T(2,128)(2,1)S(1)} %get-tuple-element.31), channel_id=1, source_target_pairs={{0,3},{1,2},{2,5},{3,4},{4,7},{5,6},{6,9},{7,8},{8,11},{9,10},{10,... | collective-permute-start | bytes 49160 | tf_op jit(solution)/shard_map/ppermute | solution.py:265
  18.8 0.0 collective-permute-done.1.cross_ref
  18.8 0.0 collective-permute-done.2.behind_ref
  18.8 1.4 %collective-permute-done.3.behind_cross_ref = bf16[2,4096]{1,0:T(2,128)(2,1)S(1)} collective-permute-done((bf16[2,4096]{1,0:T(2,128)(2,1)S(1)}, bf16[2,4096]{1,0:T(2,128)(2,1)S(1)}, u32[]{:S(2)}, u32[]{:S(2)}) %collective-permute-start.3) | collective-permute-done | bytes 16416 | tf_op jit(solution)/shard_map/ppermute | solution.py:265
  20.2 0.2 norm.1
  20.4 5.3 %collective-permute-start.4 = (bf16[2,8192]{1,0:T(2,128)(2,1)S(1)}, bf16[2,8192]{1,0:T(2,128)(2,1)S(1)}, u32[]{:S(2)}, u32[]{:S(2)}) collective-permute-start(bf16[2,8192]{1,0:T(2,128)(2,1)S(1)} %get-tuple-element.40), channel_id=1, source_target_pairs={{0,16},{2,18},{4,20},{6,22},{8,24},{10,26},{12,28},{14,30},{16,0},... | collective-permute-start | bytes 98312 | tf_op jit(solution)/shard_map/ppermute | solution.py:201
  25.7 1.9 %collective-permute-done.4 = bf16[2,8192]{1,0:T(2,128)(2,1)S(1)} collective-permute-done((bf16[2,8192]{1,0:T(2,128)(2,1)S(1)}, bf16[2,8192]{1,0:T(2,128)(2,1)S(1)}, u32[]{:S(2)}, u32[]{:S(2)}) %collective-permute-start.4) | collective-permute-done | bytes 32800 | tf_op jit(solution)/shard_map/ppermute | solution.py:201
  27.6 0.1 pad_maximum_fusion.2
  27.7 2.0 %collective-permute-start.5 = (bf16[4,8192]{1,0:T(4,128)(2,1)S(1)}, bf16[4,8192]{1,0:T(4,128)(2,1)S(1)}, u32[]{:S(2)}, u32[]{:S(2)}) collective-permute-start(bf16[4,8192]{1,0:T(4,128)(2,1)S(1)} %pad_maximum_fusion.2), channel_id=1, source_target_pairs={{0,8},{2,10},{4,12},{6,14},{8,0},{10,2},{12,4},{14,6},{16,24},{18,... | collective-permute-start | bytes 196616 | tf_op jit(solution)/shard_map/ppermute | solution.py:201
  29.6 2.4 %collective-permute-done.5 = bf16[4,8192]{1,0:T(4,128)(2,1)S(1)} collective-permute-done((bf16[4,8192]{1,0:T(4,128)(2,1)S(1)}, bf16[4,8192]{1,0:T(4,128)(2,1)S(1)}, u32[]{:S(2)}, u32[]{:S(2)}) %collective-permute-start.5) | collective-permute-done | bytes 65568 | tf_op jit(solution)/shard_map/ppermute | solution.py:201
  32.0 0.1 pad_maximum_fusion.1
  32.1 1.1 %collective-permute-start.6 = (bf16[8,8192]{1,0:T(8,128)(2,1)S(1)}, bf16[8,8192]{1,0:T(8,128)(2,1)S(1)}, u32[]{:S(2)}, u32[]{:S(2)}) collective-permute-start(bf16[8,8192]{1,0:T(8,128)(2,1)S(1)} %pad_maximum_fusion.1), channel_id=1, source_target_pairs={{0,4},{2,6},{4,0},{6,2},{8,12},{10,14},{12,8},{14,10},{16,20},{18,... | collective-permute-start | bytes 393224 | tf_op jit(solution)/shard_map/ppermute | solution.py:201
  33.2 3.9 %collective-permute-done.6 = bf16[8,8192]{1,0:T(8,128)(2,1)S(1)} collective-permute-done((bf16[8,8192]{1,0:T(8,128)(2,1)S(1)}, bf16[8,8192]{1,0:T(8,128)(2,1)S(1)}, u32[]{:S(2)}, u32[]{:S(2)}) %collective-permute-start.6) | collective-permute-done | bytes 131104 | tf_op jit(solution)/shard_map/ppermute | solution.py:201
  37.1 0.2 pad_maximum_fusion.near_ref
  37.3 0.1 collective-permute-start.7
  37.4 1.5 %collective-permute-done.7.far_ref = bf16[16,8192]{1,0:T(8,128)(2,1)S(1)} collective-permute-done((bf16[16,8192]{1,0:T(8,128)(2,1)S(1)}, bf16[16,8192]{1,0:T(8,128)(2,1)S(1)}, u32[]{:S(2)}, u32[]{:S(2)}) %collective-permute-start.7) | collective-permute-done | bytes 262176 | tf_op jit(solution)/shard_map/ppermute | solution.py:201
  38.9 8.8 %feed.1 = (f32[16,8192]{1,0:T(8,128)S(1)}, bf16[16,8192]{1,0:T(8,128)(2,1)S(1)}) custom-call(s32[8,32]{1,0:T(8,128)S(1)} %get-tuple-element.35.keep_ref, f32[8,32]{1,0:T(8,128)S(1)} %get-tuple-element.36.gate_scale_ref, f32[8,32]{1,0:T(8,128)S(1)} %get-tuple-element.37.up_scale_ref, s32[8,32]{1,0:T(8,128)S(1)} %get-tuple-element.38.down_keep_ref, ...), custom_call_target="tpu_custom_call" | custom-call | tf_op jit(solution)/shard_map/feed/pallas_call | solution.py:291
  47.7 0.2 collective-permute-start.8
  47.9 1.4 %collective-permute-done.8 = bf16[16,8192]{1,0:T(8,128)(2,1)S(1)} collective-permute-done((bf16[16,8192]{1,0:T(8,128)(2,1)S(1)}, bf16[16,8192]{1,0:T(8,128)(2,1)S(1)}, u32[]{:S(2)}, u32[]{:S(2)}) %collective-permute-start.8) | collective-permute-done | bytes 262176 | tf_op jit(solution)/shard_map/ppermute | solution.py:201
  49.4 1.1 %collective-permute-start.9 = (bf16[8,8192]{1,0:T(8,128)(2,1)S(1)}, bf16[8,8192]{1,0:T(8,128)(2,1)S(1)}, u32[]{:S(2)}, u32[]{:S(2)}) collective-permute-start(bf16[8,8192]{1,0:T(8,128)(2,1)S(1)} %slice.43), channel_id=1, source_target_pairs={{0,4},{2,6},{4,0},{6,2},{8,12},{10,14},{12,8},{14,10},{16,20},{18,... | collective-permute-start | bytes 393224 | tf_op jit(solution)/shard_map/ppermute | solution.py:201
  50.5 4.5 %collective-permute-done.9 = bf16[8,8192]{1,0:T(8,128)(2,1)S(1)} collective-permute-done((bf16[8,8192]{1,0:T(8,128)(2,1)S(1)}, bf16[8,8192]{1,0:T(8,128)(2,1)S(1)}, u32[]{:S(2)}, u32[]{:S(2)}) %collective-permute-start.9) | collective-permute-done | bytes 131104 | tf_op jit(solution)/shard_map/ppermute | solution.py:201
  55.1 2.0 %collective-permute-start.10 = (bf16[4,8192]{1,0:T(4,128)(2,1)S(1)}, bf16[4,8192]{1,0:T(4,128)(2,1)S(1)}, u32[]{:S(2)}, u32[]{:S(2)}) collective-permute-start(bf16[4,8192]{1,0:T(4,128)(2,1)S(1)} %slice.44), channel_id=1, source_target_pairs={{0,8},{2,10},{4,12},{6,14},{8,0},{10,2},{12,4},{14,6},{16,24},{18,... | collective-permute-start | bytes 196616 | tf_op jit(solution)/shard_map/ppermute | solution.py:201
  57.0 2.4 %collective-permute-done.10 = bf16[4,8192]{1,0:T(4,128)(2,1)S(1)} collective-permute-done((bf16[4,8192]{1,0:T(4,128)(2,1)S(1)}, bf16[4,8192]{1,0:T(4,128)(2,1)S(1)}, u32[]{:S(2)}, u32[]{:S(2)}) %collective-permute-start.10) | collective-permute-done | bytes 65568 | tf_op jit(solution)/shard_map/ppermute | solution.py:201
  59.5 3.0 %collective-permute-start.11 = (bf16[2,8192]{1,0:T(2,128)(2,1)S(1)}, bf16[2,8192]{1,0:T(2,128)(2,1)S(1)}, u32[]{:S(2)}, u32[]{:S(2)}) collective-permute-start(bf16[2,8192]{1,0:T(2,128)(2,1)S(1)} %slice.45), channel_id=1, source_target_pairs={{0,16},{2,18},{4,20},{6,22},{8,24},{10,26},{12,28},{14,30},{16,0},... | collective-permute-start | bytes 98312 | tf_op jit(solution)/shard_map/ppermute | solution.py:201
  62.5 1.9 %collective-permute-done.11 = bf16[2,8192]{1,0:T(2,128)(2,1)S(1)} collective-permute-done((bf16[2,8192]{1,0:T(2,128)(2,1)S(1)}, bf16[2,8192]{1,0:T(2,128)(2,1)S(1)}, u32[]{:S(2)}, u32[]{:S(2)}) %collective-permute-start.11) | collective-permute-done | bytes 32800 | tf_op jit(solution)/shard_map/ppermute | solution.py:201
  64.4 0.7 %fusion.1 = bf16[2,8192]{1,0:T(2,128)(2,1)} fusion(f32[2,8192]{1,0:T(2,128)S(1)} %get-tuple-element.34, f32[4,8192]{1,0:T(4,128)S(1)} %slice_add_fusion.1, bf16[2,8192]{1,0:T(2,128)(2,1)S(1)} %collective-permute-done.11), kind=kLoop, calls=%fused_computation.10 | loop fusion | flops 65536 | bytes 196608 | tf_op jit(solution)/shard_map/convert_element_type | solution.py:316
  (6 shorter events, 0.2 us)
Async XLA Ops:
  1.5 4.4 %collective-permute-start = (bf16[4,5248]{1,0:T(4,128)(2,1)S(1)}, bf16[4,5248]{1,0:T(4,128)(2,1)S(1)}, u32[]{:S(2)}, u32[]{:S(2)}) collective-permute-start(bf16[4,5248]{1,0:T(4,128)(2,1)S(1)} %pad_maximum_fusion.3.own_ref), channel_id=1, source_target_pairs={{2,0},{4,2},{6,4},{8,6},{10,8},{12,10},{14,12},{16,14},{18,16},{20... | collective-permute-start | bytes 125960 | tf_op jit(solution)/shard_map/ppermute | solution.py:221
  9.6 9.2 %collective-permute-start.1 = (bf16[2,4096]{1,0:T(2,128)(2,1)S(1)}, bf16[2,4096]{1,0:T(2,128)(2,1)S(1)}, u32[]{:S(2)}, u32[]{:S(2)}) collective-permute-start(bf16[2,4096]{1,0:T(2,128)(2,1)S(1)} %get-tuple-element.29), channel_id=1, source_target_pairs={{0,1},{1,0},{2,3},{3,2},{4,5},{5,4},{6,7},{7,6},{8,9},{9,8},{10,11... | collective-permute-start | bytes 49160 | tf_op jit(solution)/shard_map/ppermute | solution.py:263
  12.6 6.2 %collective-permute-start.2 = (bf16[2,4096]{1,0:T(2,128)(2,1)S(1)}, bf16[2,4096]{1,0:T(2,128)(2,1)S(1)}, u32[]{:S(2)}, u32[]{:S(2)}) collective-permute-start(bf16[2,4096]{1,0:T(2,128)(2,1)S(1)} %get-tuple-element.30), channel_id=1, source_target_pairs={{0,2},{2,4},{4,6},{6,8},{8,10},{10,12},{12,14},{14,16},{16,18},{18... | collective-permute-start | bytes 49160 | tf_op jit(solution)/shard_map/ppermute | solution.py:264
  15.4 4.8 %collective-permute-start.3 = (bf16[2,4096]{1,0:T(2,128)(2,1)S(1)}, bf16[2,4096]{1,0:T(2,128)(2,1)S(1)}, u32[]{:S(2)}, u32[]{:S(2)}) collective-permute-start(bf16[2,4096]{1,0:T(2,128)(2,1)S(1)} %get-tuple-element.31), channel_id=1, source_target_pairs={{0,3},{1,2},{2,5},{3,4},{4,7},{5,6},{6,9},{7,8},{8,11},{9,10},{10,... | collective-permute-start | bytes 49160 | tf_op jit(solution)/shard_map/ppermute | solution.py:265
  20.4 7.2 %collective-permute-start.4 = (bf16[2,8192]{1,0:T(2,128)(2,1)S(1)}, bf16[2,8192]{1,0:T(2,128)(2,1)S(1)}, u32[]{:S(2)}, u32[]{:S(2)}) collective-permute-start(bf16[2,8192]{1,0:T(2,128)(2,1)S(1)} %get-tuple-element.40), channel_id=1, source_target_pairs={{0,16},{2,18},{4,20},{6,22},{8,24},{10,26},{12,28},{14,30},{16,0},... | collective-permute-start | bytes 98312 | tf_op jit(solution)/shard_map/ppermute | solution.py:201
  27.7 4.3 %collective-permute-start.5 = (bf16[4,8192]{1,0:T(4,128)(2,1)S(1)}, bf16[4,8192]{1,0:T(4,128)(2,1)S(1)}, u32[]{:S(2)}, u32[]{:S(2)}) collective-permute-start(bf16[4,8192]{1,0:T(4,128)(2,1)S(1)} %pad_maximum_fusion.2), channel_id=1, source_target_pairs={{0,8},{2,10},{4,12},{6,14},{8,0},{10,2},{12,4},{14,6},{16,24},{18,... | collective-permute-start | bytes 196616 | tf_op jit(solution)/shard_map/ppermute | solution.py:201
  32.1 5.0 %collective-permute-start.6 = (bf16[8,8192]{1,0:T(8,128)(2,1)S(1)}, bf16[8,8192]{1,0:T(8,128)(2,1)S(1)}, u32[]{:S(2)}, u32[]{:S(2)}) collective-permute-start(bf16[8,8192]{1,0:T(8,128)(2,1)S(1)} %pad_maximum_fusion.1), channel_id=1, source_target_pairs={{0,4},{2,6},{4,0},{6,2},{8,12},{10,14},{12,8},{14,10},{16,20},{18,... | collective-permute-start | bytes 393224 | tf_op jit(solution)/shard_map/ppermute | solution.py:201
  37.3 1.6 %collective-permute-start.7 = (bf16[16,8192]{1,0:T(8,128)(2,1)S(1)}, bf16[16,8192]{1,0:T(8,128)(2,1)S(1)}, u32[]{:S(2)}, u32[]{:S(2)}) collective-permute-start(bf16[16,8192]{1,0:T(8,128)(2,1)S(1)} %pad_maximum_fusion.near_ref), channel_id=1, source_target_pairs={{0,2},{2,0},{4,6},{6,4},{8,10},{10,8},{12,14},{14,12},{16,18},{18,... | collective-permute-start | bytes 786440 | tf_op jit(solution)/shard_map/ppermute | solution.py:201
  47.7 1.6 %collective-permute-start.8 = (bf16[16,8192]{1,0:T(8,128)(2,1)S(1)}, bf16[16,8192]{1,0:T(8,128)(2,1)S(1)}, u32[]{:S(2)}, u32[]{:S(2)}) collective-permute-start(bf16[16,8192]{1,0:T(8,128)(2,1)S(1)} %get-tuple-element.46), channel_id=1, source_target_pairs={{0,2},{2,0},{4,6},{6,4},{8,10},{10,8},{12,14},{14,12},{16,18},{18,... | collective-permute-start | bytes 786440 | tf_op jit(solution)/shard_map/ppermute | solution.py:201
  49.4 5.6 %collective-permute-start.9 = (bf16[8,8192]{1,0:T(8,128)(2,1)S(1)}, bf16[8,8192]{1,0:T(8,128)(2,1)S(1)}, u32[]{:S(2)}, u32[]{:S(2)}) collective-permute-start(bf16[8,8192]{1,0:T(8,128)(2,1)S(1)} %slice.43), channel_id=1, source_target_pairs={{0,4},{2,6},{4,0},{6,2},{8,12},{10,14},{12,8},{14,10},{16,20},{18,... | collective-permute-start | bytes 393224 | tf_op jit(solution)/shard_map/ppermute | solution.py:201
  55.1 4.3 %collective-permute-start.10 = (bf16[4,8192]{1,0:T(4,128)(2,1)S(1)}, bf16[4,8192]{1,0:T(4,128)(2,1)S(1)}, u32[]{:S(2)}, u32[]{:S(2)}) collective-permute-start(bf16[4,8192]{1,0:T(4,128)(2,1)S(1)} %slice.44), channel_id=1, source_target_pairs={{0,8},{2,10},{4,12},{6,14},{8,0},{10,2},{12,4},{14,6},{16,24},{18,... | collective-permute-start | bytes 196616 | tf_op jit(solution)/shard_map/ppermute | solution.py:201
  59.5 4.9 %collective-permute-start.11 = (bf16[2,8192]{1,0:T(2,128)(2,1)S(1)}, bf16[2,8192]{1,0:T(2,128)(2,1)S(1)}, u32[]{:S(2)}, u32[]{:S(2)}) collective-permute-start(bf16[2,8192]{1,0:T(2,128)(2,1)S(1)} %slice.45), channel_id=1, source_target_pairs={{0,16},{2,18},{4,20},{6,22},{8,24},{10,26},{12,28},{14,30},{16,0},... | collective-permute-start | bytes 98312 | tf_op jit(solution)/shard_map/ppermute | solution.py:201

commit v3 on v2

v3 whole, which is shorter than its diff:
```python
import functools
import math

import jax
import jax.numpy as jnp
from jax import lax
from jax.experimental import pallas as pl
from jax.experimental.pallas import tpu as pltpu
from jax.sharding import PartitionSpec as P

HD = 128
BLK = 128
TILE = 8
DEAD = -1e30
MIB = 1024 * 1024

VMEM = pl.BlockSpec(memory_space=pltpu.VMEM)
SMEM = pl.BlockSpec(memory_space=pltpu.SMEM)
HBM = pl.BlockSpec(memory_space=pltpu.HBM)


def in_hbm(arrays):
    return [pltpu.with_memory_space_constraint(a, pltpu.HBM) for a in arrays]


def like(array):
    return jax.ShapeDtypeStruct(array.shape, array.dtype)


def copies(pairs, sems):
    return [
        pltpu.make_async_copy(source, target, sems.at[i])
        for i, (source, target) in enumerate(pairs)
    ]


def pack_kernel(query_hbm, key_hbm, value_hbm, parent_hbm, packed_ref, parent_ref, sems):
    rows, width = query_hbm.shape
    kv_width = key_hbm.shape[1]
    moves = copies(
        (
            (parent_hbm, parent_ref),
            (query_hbm, packed_ref.at[:, pl.ds(0, width)]),
            (key_hbm, packed_ref.at[:, pl.ds(width, kv_width)]),
            (value_hbm, packed_ref.at[:, pl.ds(width + kv_width, kv_width)]),
        ),
        sems,
    )
    for move in moves:
        move.start()
    moves[0].wait()
    first = lax.axis_index("wide") * rows
    row = lax.broadcasted_iota(jnp.int32, (rows, HD), 0)
    parent = jnp.zeros((rows, HD), jnp.int32)
    for r in range(rows):
        parent = jnp.where(row == r, parent_ref[r] - first, parent)
    packed_ref[:, width + 2 * kv_width :] = parent.astype(jnp.float32).astype(jnp.bfloat16)
    for move in moves[1:]:
        move.wait()


def attend_kernel(groups, per_group, shift, packed_ref, pool_ref, bias_ref, *refs):
    out_ref = refs[-1]
    rows = packed_ref.shape[0]
    width = groups * per_group * HD
    kv_width = groups * HD
    spots = bias_ref.shape[1]
    fold = TILE // rows

    def tiled(block):
        return jnp.concatenate([block] * fold, axis=0)

    packed = packed_ref[...].astype(jnp.float32)
    parent = packed[:, width + 2 * kv_width : width + 2 * kv_width + 1] + shift
    bias = jnp.full((rows, spots), DEAD, jnp.float32)
    for r in range(rows):
        bias = jnp.where(parent == r, bias_ref[r : r + 1, :], bias)
    bias = tiled(bias)
    here = (parent >= 0) & (parent < rows)

    factor = 1.0 / math.sqrt(HD)
    for g in range(groups):
        base = g * per_group * HD
        query = jnp.concatenate(
            [packed[:, base + j * HD : base + (j + 1) * HD] for j in range(per_group)], axis=0
        )
        key_own = tiled(packed[:, width + g * HD : width + (g + 1) * HD])
        value_own = tiled(packed[:, width + kv_width + g * HD : width + kv_width + (g + 1) * HD])
        keys = pool_ref[0, :, :, g * HD : (g + 1) * HD].reshape(spots, HD)
        values = pool_ref[1, :, :, g * HD : (g + 1) * HD].reshape(spots, HD)
        scores = lax.dot_general(
            query.astype(jnp.bfloat16), keys, (((1,), (1,)), ((), ())),
            preferred_element_type=jnp.float32,
        )
        scores = scores.reshape(-1, TILE, spots) * factor + bias[None]
        query = query.reshape(-1, TILE, HD)
        own = jnp.sum(query * key_own[None], axis=-1, keepdims=True) * factor
        top = jnp.maximum(jnp.max(scores, axis=-1, keepdims=True), own)
        expo = jnp.exp(scores - top)
        own_expo = jnp.exp(own - top)
        total = jnp.sum(expo, axis=-1, keepdims=True) + own_expo
        weights = (expo / total).astype(jnp.bfloat16)
        own_weight = (own_expo / total).astype(jnp.bfloat16).astype(jnp.float32)
        mixture = jnp.dot(
            weights.reshape(per_group * rows, spots), values, preferred_element_type=jnp.float32
        )
        mixture = mixture.reshape(-1, TILE, HD) + own_weight * value_own[None]
        mixture = mixture.reshape(per_group * rows, HD)
        for j in range(per_group):
            out_ref[:, base + j * HD : base + (j + 1) * HD] = jnp.where(
                here, mixture[j * rows : (j + 1) * rows], 0.0
            ).astype(jnp.bfloat16)


def prepare_kernel(count, *refs):
    page_hbm, length_hbm, sources = refs[0], refs[1], refs[2 : 2 + count]
    bias_ref, targets = refs[2 + count], refs[3 + count : 3 + 2 * count]
    page_ref, length_ref, sems = refs[3 + 2 * count :]
    moves = copies(
        ((page_hbm, page_ref), (length_hbm, length_ref), *zip(sources, targets)), sems
    )
    for move in moves:
        move.start()
    moves[0].wait()
    moves[1].wait()
    spots = bias_ref.shape[1]
    page = spots // sources[0].shape[1]
    spot = lax.broadcasted_iota(jnp.int32, (1, spots), 1)
    page_of, offset = spot // page, spot % page
    for r in range(bias_ref.shape[0]):
        place = jnp.full((1, spots), 1 << 20, jnp.int32)
        for i in range(page_ref.shape[1]):
            place = jnp.where(page_of == page_ref[r, i], i * page, place)
        bias_ref[r : r + 1, :] = jnp.where(place + offset < length_ref[r], 0.0, DEAD)
    for move in moves[2:]:
        move.wait()


def load_kernel(skip, after_ref, gate_hbm, up_hbm, token_ref, gate_ref, up_ref, sems):
    del after_ref
    moves = copies(
        [
            (source.at[pl.ds(skip, target.shape[0])], target)
            for source, target in ((gate_hbm, gate_ref), (up_hbm, up_ref))
        ],
        sems,
    )
    for move in moves:
        move.start()
    token_ref[...] = jnp.zeros_like(token_ref)
    for move in moves:
        move.wait()


def merge_kernel(own_ref, behind_ref, *refs):
    stay_ref, cross_ref = refs[-2:]
    head = lax.axis_index("head")
    part = stay_ref.shape[0]
    both = own_ref[...].astype(jnp.float32) + behind_ref[...].astype(jnp.float32)
    low, high = both[:part], both[part : 2 * part]
    stay_ref[...] = jnp.where(head == 0, low, high).astype(jnp.bfloat16)
    cross_ref[...] = jnp.where(head == 0, high, low).astype(jnp.bfloat16)


def norm_kernel(stay_ref, cross_ref, residual_ref, gain_ref, *refs):
    middle_ref, normed_ref = refs[-2:]
    head = lax.axis_index("head")
    half = stay_ref.shape[1]
    f32 = jnp.float32
    same, other = stay_ref[...].astype(f32), cross_ref[...].astype(f32)
    low = residual_ref[:, :half].astype(f32) + jnp.where(head == 0, same, other)
    high = residual_ref[:, half:].astype(f32) + jnp.where(head == 0, other, same)
    middle_ref[:, :half] = low
    middle_ref[:, half:] = high
    square = jnp.sum(low * low, axis=-1, keepdims=True)
    square = square + jnp.sum(high * high, axis=-1, keepdims=True)
    scale = lax.rsqrt(square / (2 * half) + 1e-05)
    normed_ref[:, :half] = (low * scale * gain_ref[:, :half]).astype(jnp.bfloat16)
    normed_ref[:, half:] = (high * scale * gain_ref[:, half:]).astype(jnp.bfloat16)


def feed_kernel(
    brought, keep_ref, gate_scale_ref, up_scale_ref, down_keep_ref, down_scale_ref,
    near_ref, far_ref, gate_hbm, up_hbm, down_hbm, *refs,
):
    columns, keep = keep_ref.shape
    half = near_ref.shape[0]
    rest = columns - brought
    stay_ref, send_ref, gate_rest, up_rest, down, hidden, total, sems = refs[-8:]
    gates, ups = [], []
    pieces = refs[: 2 if brought else 0]
    for gate_piece, up_piece in zip(pieces[0::2], pieces[1::2]):
        gates += [gate_piece.at[i] for i in range(gate_piece.shape[0])]
        ups += [up_piece.at[i] for i in range(up_piece.shape[0])]
    gates += [gate_rest.at[i] for i in range(rest)]
    ups += [up_rest.at[i] for i in range(rest)]
    moves = copies(
        (
            (gate_hbm.at[pl.ds(brought, rest)], gate_rest),
            (up_hbm.at[pl.ds(brought, rest)], up_rest),
        ),
        sems.at[0],
    )
    late = columns // 4
    ends = [0, columns - late, columns] if late else [0, columns]
    down_moves = copies(
        [
            (down_hbm.at[pl.ds(start, end - start)], down.at[pl.ds(start, end - start)])
            for start, end in zip(ends, ends[1:])
        ],
        sems.at[1],
    )
    for move in moves + down_moves:
        move.start()
    total[...] = jnp.zeros_like(total)

    for c in range(columns):
        if c == brought:
            for move in moves:
                move.wait()
        gate_sum = jnp.zeros((2 * half, BLK), jnp.float32)
        up_sum = jnp.zeros((2 * half, BLK), jnp.float32)
        for k in range(keep):
            where = pl.ds(pl.multiple_of(keep_ref[c, k] * BLK, BLK), BLK)
            picked = jnp.concatenate([near_ref[:, where], far_ref[:, where]], axis=0)
            both = jnp.dot(
                picked, jnp.concatenate([gates[c][k], ups[c][k]], axis=1),
                preferred_element_type=jnp.float32,
            )
            gate_sum += gate_scale_ref[c, k] * both[:, :BLK]
            up_sum += up_scale_ref[c, k] * both[:, BLK:]
        hidden[c] = (gate_sum / (1.0 + jnp.exp(-gate_sum)) * up_sum).astype(jnp.bfloat16)
    for c in range(columns):
        if c in ends:
            down_moves[ends.index(c)].wait()
        for k in range(0, keep, 2):
            both = jnp.dot(
                hidden[c], jnp.concatenate([down[c, k], down[c, k + 1]], axis=1),
                preferred_element_type=jnp.float32,
            )
            for j in range(2):
                where = pl.ds(pl.multiple_of(down_keep_ref[c, k + j] * BLK, BLK), BLK)
                total[:, where] += down_scale_ref[c, k + j] * both[:, j * BLK : (j + 1) * BLK]
    stay_ref[...] = total[:half, :]
    send_ref[...] = total[half:, :].astype(jnp.bfloat16)


def join_kernel(count, *refs):
    out_ref = refs[-1]
    height = refs[0].shape[0]
    for i, ref in enumerate(refs[:count]):
        out_ref[i * height : (i + 1) * height, :] = ref[...]


def joined(blocks, tokens):
    height, width = blocks[0].shape
    return pl.pallas_call(
        functools.partial(join_kernel, len(blocks)),
        out_shape=jax.ShapeDtypeStruct((len(blocks) * height, width), blocks[0].dtype),
        in_specs=[VMEM] * (len(blocks) + len(tokens)),
        out_specs=VMEM,
        compiler_params=pltpu.CompilerParams(vmem_limit_bytes=2 * MIB),
        name="join",
    )(*blocks, *tokens)


def swapped(block, bits):
    return lax.ppermute(block, "wide", [(i, i ^ bits) for i in range(lax.axis_size("wide"))])


def combined(bits):
    sums = [0]
    for bit in bits:
        sums += [s + bit for s in sums]
    return sums[1:]


def per_device(
    branch_query, key_new, value_new, pool_pages, page_table, tail_length, parent_row, residual,
    norm_gain, gate_blocks, up_blocks, gate_up_keep, gate_scale, up_scale, down_blocks, down_keep,
    down_scale,
):
    bf16, f32 = jnp.bfloat16, jnp.float32
    wide, heads = lax.axis_size("wide"), lax.axis_size("head")
    rows, width = branch_query.shape
    kv_width = key_new.shape[1]
    groups = kv_width // HD
    per_group = width // kv_width
    part, model = residual.shape
    columns = gate_blocks.shape[0]

    own = pl.pallas_call(
        pack_kernel,
        out_shape=jax.ShapeDtypeStruct((rows, width + 2 * kv_width + HD), bf16),
        in_specs=[HBM] * 4,
        out_specs=VMEM,
        scratch_shapes=[
            pltpu.SMEM(parent_row.shape, jnp.int32),
            pltpu.SemaphoreType.DMA((4,)),
        ],
        compiler_params=pltpu.CompilerParams(vmem_limit_bytes=2 * MIB),
        name="pack",
    )(*in_hbm([branch_query, key_new, value_new, parent_row]))
    following = lax.ppermute(own, "wide", [(i, i - 1) for i in range(1, wide)])

    stored = [pool_pages, residual, norm_gain.reshape(1, model)]
    stored += [gate_up_keep, gate_scale, up_scale, down_keep, down_scale]
    spots = pool_pages.shape[1] * pool_pages.shape[2]
    bias, pool, residual, gain, *lists = pl.pallas_call(
        functools.partial(prepare_kernel, len(stored)),
        out_shape=(jax.ShapeDtypeStruct((rows, spots), f32), *[like(a) for a in stored]),
        in_specs=[HBM] * (2 + len(stored)),
        out_specs=(VMEM,) * (1 + len(stored)),
        scratch_shapes=[
            pltpu.SMEM(page_table.shape, jnp.int32),
            pltpu.SMEM(tail_length.shape, jnp.int32),
            pltpu.SemaphoreType.DMA((2 + len(stored),)),
        ],
        compiler_params=pltpu.CompilerParams(vmem_limit_bytes=2 * MIB),
        cost_estimate=pl.CostEstimate(flops=0, bytes_accessed=8 * MIB, transcendentals=0),
        name="prepare",
    )(*in_hbm([page_table, tail_length, *stored]))

    def attended(packed, shift, *after):
        return pl.pallas_call(
            functools.partial(attend_kernel, groups, per_group, shift),
            out_shape=jax.ShapeDtypeStruct((rows, width), bf16),
            in_specs=[VMEM] * (3 + len(after)),
            out_specs=VMEM,
            compiler_params=pltpu.CompilerParams(vmem_limit_bytes=6 * MIB),
            name="attend",
        )(packed, pool, bias, *after)

    ahead = attended(following, rows)
    behind = lax.ppermute(ahead, "wide", [(i, i + 1) for i in range(wide - 1)])
    mixed = attended(own, 0, ahead)
    per_load = columns // 2
    portion = pltpu.VMEM((per_load, *gate_blocks.shape[1:]), bf16)
    pieces = []

    def load(after):
        if not per_load:
            return []
        token, gate_piece, up_piece = pl.pallas_call(
            functools.partial(load_kernel, len(pieces) // 2 * per_load),
            out_shape=(jax.ShapeDtypeStruct((8, HD), f32), portion, portion),
            in_specs=[VMEM, HBM, HBM],
            out_specs=(VMEM,) * 3,
            scratch_shapes=[pltpu.SemaphoreType.DMA((2,))],
            compiler_params=pltpu.CompilerParams(vmem_limit_bytes=2 * MIB),
            cost_estimate=pl.CostEstimate(
                flops=0, bytes_accessed=4 * gate_blocks.size // 2, transcendentals=0
            ),
            name="load",
        )(after, *in_hbm([gate_blocks, up_blocks]))
        pieces.extend([gate_piece, up_piece])
        return [token]

    stay, cross = pl.pallas_call(
        merge_kernel,
        out_shape=(jax.ShapeDtypeStruct((part, width), bf16),) * 2,
        in_specs=[VMEM] * 2,
        out_specs=(VMEM,) * 2,
        compiler_params=pltpu.CompilerParams(vmem_limit_bytes=2 * MIB),
        name="merge",
    )(mixed, behind)
    crossed = lax.ppermute(cross, "head", [(h, 1 - h) for h in range(heads)])
    middle, normed = pl.pallas_call(
        norm_kernel,
        out_shape=(
            jax.ShapeDtypeStruct((part, model), f32),
            jax.ShapeDtypeStruct((part, model), bf16),
        ),
        in_specs=[VMEM] * 4,
        out_specs=(VMEM,) * 2,
        compiler_params=pltpu.CompilerParams(vmem_limit_bytes=2 * MIB),
        name="norm",
    )(stay, crossed, residual, gain)

    bits = [1 << b for b in range(wide.bit_length() - 1)]
    stages = [(bits[0],), tuple(bits[1:3]), *[(bit,) for bit in bits[3:]]]
    gathered = normed
    for stage in stages[:0:-1]:
        blocks = [gathered] + [swapped(gathered, s) for s in combined(stage)]
        tokens = load(gathered) if len(stage) > 1 else []
        gathered = joined(blocks, tokens)
    far = swapped(gathered, bits[0])

    half = gathered.shape[0]
    rest = columns - len(pieces) // 2 * per_load
    kept_back = [pltpu.VMEM((rest, *gate_blocks.shape[1:]), bf16)] * 2
    size = 2 * half * model * 4 + half * model * 6 + 2 * down_blocks.size
    size += 4 * rest * gate_blocks.size // columns
    kept, sent = pl.pallas_call(
        functools.partial(feed_kernel, columns - rest),
        out_shape=(
            jax.ShapeDtypeStruct((half, model), f32),
            jax.ShapeDtypeStruct((half, model), bf16),
        ),
        in_specs=[SMEM] * 5 + [VMEM] * 2 + [HBM] * 3 + [VMEM] * len(pieces),
        out_specs=(VMEM,) * 2,
        scratch_shapes=kept_back
        + [
            pltpu.VMEM(down_blocks.shape, bf16),
            pltpu.VMEM((columns, 2 * half, BLK), bf16),
            pltpu.VMEM((2 * half, model), f32),
            pltpu.SemaphoreType.DMA((2, 2)),
        ],
        compiler_params=pltpu.CompilerParams(vmem_limit_bytes=size + 4 * MIB),
        name="feed",
    )(*lists, gathered, far, *in_hbm([gate_blocks, up_blocks, down_blocks]), *pieces)

    total = kept + swapped(sent, bits[0]).astype(f32)
    for stage in stages[1:]:
        half = half >> len(stage)
        kept, sent = total[:half], total[half:].astype(bf16)
        total = kept
        for i, s in enumerate(combined(stage)):
            total = total + swapped(sent[i * half : (i + 1) * half], s).astype(f32)
    return (middle + total).astype(bf16)


def solution(mesh):
    placed = (
        P("wide", "head"),
        P("wide", "head"),
        P("wide", "head"),
        P(None, "wide", None, "head"),
        P("wide", None),
        P("wide"),
        P("wide"),
        P(("wide", "head"), None),
        P(),
        P("wide", None, None, None),
        P("wide", None, None, None),
        P("wide", None),
        P("wide", None),
        P("wide", None),
        P("wide", None, None, None),
        P("wide", None),
        P("wide", None),
    )
    return jax.shard_map(
        per_device, mesh=mesh, in_specs=placed, out_specs=P(("wide", "head"), None), check_vma=False
    )
```

time: 65.3 us -> 56.7 us (0.87)
  waiting for transfers between devices: 21.3 us -> 13.2 us
  Pallas kernels: 15.7 us -> 19.2 us
  starting transfers between devices: 25.1 us -> 22.9 us
  other arithmetic: 2.59 us -> 0.77 us
    ppermute x10 -> x11, waiting for transfers between devices: 21.3 us -> 13.1 us  [the longest x10 10.9 us: swapped(): lax.ppermute(block, 'wide', [(i, i ^ bits) for i in range(lax.axis_size('...]
    ppermute x10 -> x11, starting transfers between devices: 21.1 us -> 16.2 us  [the longest x10 14.6 us: swapped(): lax.ppermute(block, 'wide', [(i, i ^ bits) for i in range(lax.axis_size('...]
    pallas_call x3 -> x9, Pallas kernels: 15.5 us -> 19 us  [the longest x1 9.41 us: per_device(): pl.pallas_call(functools.partial(feed_kernel, columns - rest), out_shape=...]
    ppermute x1, starting transfers between devices: 2.74 us -> 5.44 us  [per_device(): behind = lax.ppermute(ahead, 'wide', [(i, i + 1) for i in range(wide - 1)])]
    concatenate x4 -> x0, other arithmetic: 1.17 us -> none  [the longest x1 0.81 us: per_device(): jnp.concatenate([branch_query, key_new, value_new, jnp.broadcast_to(relat...]
    convert_element_type x2 -> x1, other arithmetic: 1.32 us -> 0.66 us  [per_device(): return (middle + total).astype(bf16)]
  transfers between devices with their start and end apart: 12 -> 13, of which waited for: 9 -> 9; matrix products, arithmetic and copies ran while one was open for 0% -> 0% of each run, Pallas kernels for 5% -> 12%
where the time goes in v3:
time: 56.7 us; the launch traced here: 56.4 us
  starting transfers between devices  22.9 us (40%)
  Pallas kernels  19.2 us (34%)
  waiting for transfers between devices  13.2 us (23%)
  other arithmetic  0.77 us (1%)
    ppermute x10, starting transfers between devices, swapped(): lax.ppermute(block, 'wide', [(i, i ^ bits) for i in range(lax.axis_size('...  14.6 us
    ppermute x10, waiting for transfers between devices, swapped(): lax.ppermute(block, 'wide', [(i, i ^ bits) for i in range(lax.axis_size('...  10.9 us
    pallas_call x1, Pallas kernels, per_device(): pl.pallas_call(functools.partial(feed_kernel, columns - rest), out_shape=...  9.41 us
    ppermute x1, starting transfers between devices, per_device(): behind = lax.ppermute(ahead, 'wide', [(i, i + 1) for i in range(wide - 1)])  5.44 us
    pallas_call x2, Pallas kernels, attended(): pl.pallas_call(functools.partial(attend_kernel, groups, per_group, shift)...  3.5 us
    pallas_call x1, Pallas kernels, load(): pl.pallas_call(functools.partial(load_kernel, len(pieces) // 2 * per_load...  3.48 us
    ppermute x1, waiting for transfers between devices, per_device(): crossed = lax.ppermute(cross, 'head', [(h, 1 - h) for h in range(heads)])  2.22 us
    pallas_call x1, Pallas kernels, per_device(): pl.pallas_call(functools.partial(prepare_kernel, len(stored)), out_shape=...  1.71 us
  transfers between devices with their start and end apart: 13, of which 9 were waited for; matrix products, arithmetic and copies ran while one was open for 0% of the time, Pallas kernels for 12%

profile of v3, /device:TPU:0, one launch (start us, length us, event | category | flops | bytes accessed | tf_op | source)
XLA Modules:
  0.0 56.4 jit_solution(8882800322981455138)
XLA Ops:
  0.0 0.8 %pack.1.packed_ref = bf16[4,5248]{1,0:T(4,128)(2,1)S(1)} custom-call(bf16[4,4096]{1,0:T(4,128)(2,1)} %query_hbm.1, bf16[4,512]{1,0:T(4,128)(2,1)} %key_hbm.1, bf16[4,512]{1,0:T(4,128)(2,1)} %value_hbm.1, s32[4]{0:T(128)} %parent_hbm.1), custom_call_target="tpu_custom_call" | custom-call | tf_op jit(solution)/shard_map/pack/pallas_call | solution.py:292
  0.8 1.3 %collective-permute-start = (bf16[4,5248]{1,0:T(4,128)(2,1)S(1)}, bf16[4,5248]{1,0:T(4,128)(2,1)S(1)}, u32[]{:S(2)}, u32[]{:S(2)}) collective-permute-start(bf16[4,5248]{1,0:T(4,128)(2,1)S(1)} %pack.1.packed_ref), channel_id=1, source_target_pairs={{2,0},{4,2},{6,4},{8,6},{10,8},{12,10},{14,12},{16,14},{18,16},{20... | collective-permute-start | bytes 125960 | tf_op jit(solution)/shard_map/ppermute | solution.py:304
  2.1 1.7 %prepare.1 = (f32[4,1024]{1,0:T(4,128)S(1)}, bf16[2,64,16,512]{3,2,1,0:T(8,128)(2,1)S(1)}, bf16[2,8192]{1,0:T(2,128)(2,1)S(1)}, f32[1,8192]{1,0:T(1,128)S(1)}, s...) custom-call(s32[4,16]{1,0:T(4,128)} %refs_0_.1, ...), custom_call_target="tpu_custom_call" | custom-call | bytes 8388608 | tf_op jit(solution)/shard_map/prepare/pallas_call | solution.py:309
  3.8 0.1 collective-permute-done.packed_ref
  3.9 1.7 %attend.2.refs_0_ = bf16[4,4096]{1,0:T(4,128)(2,1)S(1)} custom-call(bf16[4,5248]{1,0:T(4,128)(2,1)S(1)} %collective-permute-done.packed_ref, bf16[2,64,16,512]{3,2,1,0:T(8,128)(2,1)S(1)} %get-tuple-element.23.pool_ref, f32[4,1024]{1,0:T(4,128)S(1)} %get-tuple-element.24.bias_ref), custom_call_target="tpu_custom_call" | custom-call | tf_op jit(solution)/shard_map/attend/pallas_call | solution.py:325
  5.7 5.4 %collective-permute-start.1 = (bf16[4,4096]{1,0:T(4,128)(2,1)S(1)}, bf16[4,4096]{1,0:T(4,128)(2,1)S(1)}, u32[]{:S(2)}, u32[]{:S(2)}) collective-permute-start(bf16[4,4096]{1,0:T(4,128)(2,1)S(1)} %attend.2.refs_0_), channel_id=1, source_target_pairs={{0,2},{2,4},{4,6},{6,8},{8,10},{10,12},{12,14},{14,16},{16,18},{18... | collective-permute-start | bytes 98312 | tf_op jit(solution)/shard_map/ppermute | solution.py:335
  11.1 1.8 %attend.3.own_ref = bf16[4,4096]{1,0:T(4,128)(2,1)S(1)} custom-call(bf16[4,5248]{1,0:T(4,128)(2,1)S(1)} %pack.1.packed_ref, bf16[2,64,16,512]{3,2,1,0:T(8,128)(2,1)S(1)} %get-tuple-element.23.pool_ref, f32[4,1024]{1,0:T(4,128)S(1)} %get-tuple-element.24.bias_ref, bf16[4,4096]{1,0:T(4,128)(2,1)S(1)} %attend.2.refs_0_), custom_call_target="tpu_custom_call" | custom-call | tf_op jit(solution)/shard_map/attend/pallas_call | solution.py:325
  12.9 0.0 collective-permute-done.1.behind_ref
  12.9 1.6 %collective-permute-start.2 = (bf16[2,4096]{1,0:T(2,128)(2,1)S(1)}, bf16[2,4096]{1,0:T(2,128)(2,1)S(1)}, u32[]{:S(2)}, u32[]{:S(2)}) collective-permute-start(bf16[2,4096]{1,0:T(2,128)(2,1)S(1)} %get-tuple-element.26), channel_id=1, source_target_pairs={{0,1},{1,0},{2,3},{3,2},{4,5},{5,4},{6,7},{7,6},{8,9},{9,8},{10,11... | collective-permute-start | bytes 49160 | tf_op jit(solution)/shard_map/ppermute | solution.py:367
  14.5 2.2 %collective-permute-done.2.cross_ref = bf16[2,4096]{1,0:T(2,128)(2,1)S(1)} collective-permute-done((bf16[2,4096]{1,0:T(2,128)(2,1)S(1)}, bf16[2,4096]{1,0:T(2,128)(2,1)S(1)}, u32[]{:S(2)}, u32[]{:S(2)}) %collective-permute-start.2) | collective-permute-done | bytes 16416 | tf_op jit(solution)/shard_map/ppermute | solution.py:367
  16.7 0.2 norm.1
  16.9 4.4 %collective-permute-start.3 = (bf16[2,8192]{1,0:T(2,128)(2,1)S(1)}, bf16[2,8192]{1,0:T(2,128)(2,1)S(1)}, u32[]{:S(2)}, u32[]{:S(2)}) collective-permute-start(bf16[2,8192]{1,0:T(2,128)(2,1)S(1)} %get-tuple-element.35.refs_0_), channel_id=1, source_target_pairs={{0,16},{2,18},{4,20},{6,22},{8,24},{10,26},{12,28},{14,30},{16,0},... | collective-permute-start | bytes 98312 | tf_op jit(solution)/shard_map/ppermute | solution.py:268
  21.3 1.9 %collective-permute-done.3.refs_1_ = bf16[2,8192]{1,0:T(2,128)(2,1)S(1)} collective-permute-done((bf16[2,8192]{1,0:T(2,128)(2,1)S(1)}, bf16[2,8192]{1,0:T(2,128)(2,1)S(1)}, u32[]{:S(2)}, u32[]{:S(2)}) %collective-permute-start.3) | collective-permute-done | bytes 32800 | tf_op jit(solution)/shard_map/ppermute | solution.py:268
  23.2 2.1 %collective-permute-start.6 = (bf16[4,8192]{1,0:T(4,128)(2,1)S(1)}, bf16[4,8192]{1,0:T(4,128)(2,1)S(1)}, u32[]{:S(2)}, u32[]{:S(2)}) collective-permute-start(bf16[4,8192]{1,0:T(4,128)(2,1)S(1)} %join.2.after_ref.refs_0_), channel_id=1, source_target_pairs={{0,12},{2,14},{4,8},{6,10},{8,4},{10,6},{12,0},{14,2},{16,28},{18,... | collective-permute-start | bytes 196616 | tf_op jit(solution)/shard_map/ppermute | solution.py:268
  25.3 0.4 collective-permute-start.5
  25.7 1.0 %collective-permute-start.4 = (bf16[4,8192]{1,0:T(4,128)(2,1)S(1)}, bf16[4,8192]{1,0:T(4,128)(2,1)S(1)}, u32[]{:S(2)}, u32[]{:S(2)}) collective-permute-start(bf16[4,8192]{1,0:T(4,128)(2,1)S(1)} %join.2.after_ref.refs_0_), channel_id=1, source_target_pairs={{0,4},{2,6},{4,0},{6,2},{8,12},{10,14},{12,8},{14,10},{16,20},{18,... | collective-permute-start | bytes 196616 | tf_op jit(solution)/shard_map/ppermute | solution.py:268
  26.8 3.5 %load.1 = (f32[8,128]{1,0:T(8,128)S(1)}, bf16[4,32,128,128]{3,2,1,0:T(8,128)(2,1)S(1)}, bf16[4,32,128,128]{3,2,1,0:T(8,128)(2,1)S(1)}) custom-call(bf16[4,8192]{1,0:T(4,128)(2,1)S(1)} %join.2.after_ref.refs_0_, bf16[8,32,128,128]{3,2,1,0:T(8,128)(2,1)} %gate_hbm.3, bf16[8,32,128,128]{3,2,1,0:T(8,128)(2,1)} %up_hbm.3), custom_call_target="tpu_custom_call" | custom-call | bytes 8388608 | tf_op jit(solution)/shard_map/load/pallas_call | solution.py:344
  30.2 0.0 collective-permute-done.6.refs_3_
  30.3 0.0 collective-permute-done.5.refs_2_
  30.3 0.0 collective-permute-done.4.refs_1_
  30.3 0.1 join.3.near_ref
  30.4 0.1 collective-permute-start.7
  30.4 1.5 %collective-permute-done.7.far_ref = bf16[16,8192]{1,0:T(8,128)(2,1)S(1)} collective-permute-done((bf16[16,8192]{1,0:T(8,128)(2,1)S(1)}, bf16[16,8192]{1,0:T(8,128)(2,1)S(1)}, u32[]{:S(2)}, u32[]{:S(2)}) %collective-permute-start.7) | collective-permute-done | bytes 262176 | tf_op jit(solution)/shard_map/ppermute | solution.py:268
  32.0 9.4 %feed.1 = (f32[16,8192]{1,0:T(8,128)S(1)}, bf16[16,8192]{1,0:T(8,128)(2,1)S(1)}) custom-call(s32[8,32]{1,0:T(8,128)S(1)} %get-tuple-element.30.keep_ref, f32[8,32]{1,0:T(8,128)S(1)} %get-tuple-element.31.gate_scale_ref, f32[8,32]{1,0:T(8,128)S(1)} %get-tuple-element.32.up_scale_ref, s32[8,32]{1,0:T(8,128)S(1)} %get-tuple-element.33.down_keep_ref, ...), custom_call_target="tpu_custom_call" | custom-call | tf_op jit(solution)/shard_map/feed/pallas_call | solution.py:394
  41.4 0.2 collective-permute-start.8
  41.6 1.4 %collective-permute-done.8 = bf16[16,8192]{1,0:T(8,128)(2,1)S(1)} collective-permute-done((bf16[16,8192]{1,0:T(8,128)(2,1)S(1)}, bf16[16,8192]{1,0:T(8,128)(2,1)S(1)}, u32[]{:S(2)}, u32[]{:S(2)}) %collective-permute-start.8) | collective-permute-done | bytes 262176 | tf_op jit(solution)/shard_map/ppermute | solution.py:268
  43.0 0.1 fusion.4
  43.0 0.1 fusion.5
  43.1 1.1 %collective-permute-start.9 = (bf16[4,8192]{1,0:T(4,128)(2,1)S(1)}, bf16[4,8192]{1,0:T(4,128)(2,1)S(1)}, u32[]{:S(2)}, u32[]{:S(2)}) collective-permute-start(bf16[4,8192]{1,0:T(4,128)(2,1)S(1)} %get-tuple-element.43), channel_id=1, source_target_pairs={{0,4},{2,6},{4,0},{6,2},{8,12},{10,14},{12,8},{14,10},{16,20},{18,... | collective-permute-start | bytes 196616 | tf_op jit(solution)/shard_map/ppermute | solution.py:268
  44.2 2.3 %collective-permute-start.11 = (bf16[4,8192]{1,0:T(4,128)(2,1)S(1)}, bf16[4,8192]{1,0:T(4,128)(2,1)S(1)}, u32[]{:S(2)}, u32[]{:S(2)}) collective-permute-start(bf16[4,8192]{1,0:T(4,128)(2,1)S(1)} %get-tuple-element.44), channel_id=1, source_target_pairs={{0,12},{2,14},{4,8},{6,10},{8,4},{10,6},{12,0},{14,2},{16,28},{18,... | collective-permute-start | bytes 196616 | tf_op jit(solution)/shard_map/ppermute | solution.py:268
  46.5 0.2 collective-permute-start.10
  46.7 0.8 %collective-permute-done.9 = bf16[4,8192]{1,0:T(4,128)(2,1)S(1)} collective-permute-done((bf16[4,8192]{1,0:T(4,128)(2,1)S(1)}, bf16[4,8192]{1,0:T(4,128)(2,1)S(1)}, u32[]{:S(2)}, u32[]{:S(2)}) %collective-permute-start.9) | collective-permute-done | bytes 65568 | tf_op jit(solution)/shard_map/ppermute | solution.py:268
  47.5 2.3 %collective-permute-done.11 = bf16[4,8192]{1,0:T(4,128)(2,1)S(1)} collective-permute-done((bf16[4,8192]{1,0:T(4,128)(2,1)S(1)}, bf16[4,8192]{1,0:T(4,128)(2,1)S(1)}, u32[]{:S(2)}, u32[]{:S(2)}) %collective-permute-start.11) | collective-permute-done | bytes 65568 | tf_op jit(solution)/shard_map/ppermute | solution.py:268
  49.8 1.0 %collective-permute-done.10 = bf16[4,8192]{1,0:T(4,128)(2,1)S(1)} collective-permute-done((bf16[4,8192]{1,0:T(4,128)(2,1)S(1)}, bf16[4,8192]{1,0:T(4,128)(2,1)S(1)}, u32[]{:S(2)}, u32[]{:S(2)}) %collective-permute-start.10) | collective-permute-done | bytes 65568 | tf_op jit(solution)/shard_map/ppermute | solution.py:268
  50.8 0.1 fusion.1
  50.9 2.9 %collective-permute-start.12 = (bf16[2,8192]{1,0:T(2,128)(2,1)S(1)}, bf16[2,8192]{1,0:T(2,128)(2,1)S(1)}, u32[]{:S(2)}, u32[]{:S(2)}) collective-permute-start(bf16[2,8192]{1,0:T(2,128)(2,1)S(1)} %slice.47), channel_id=1, source_target_pairs={{0,16},{2,18},{4,20},{6,22},{8,24},{10,26},{12,28},{14,30},{16,0},... | collective-permute-start | bytes 98312 | tf_op jit(solution)/shard_map/ppermute | solution.py:268
  53.8 2.0 %collective-permute-done.12 = bf16[2,8192]{1,0:T(2,128)(2,1)S(1)} collective-permute-done((bf16[2,8192]{1,0:T(2,128)(2,1)S(1)}, bf16[2,8192]{1,0:T(2,128)(2,1)S(1)}, u32[]{:S(2)}, u32[]{:S(2)}) %collective-permute-start.12) | collective-permute-done | bytes 32800 | tf_op jit(solution)/shard_map/ppermute | solution.py:268
  55.8 0.7 %fusion.3 = bf16[2,8192]{1,0:T(2,128)(2,1)} fusion(f32[2,8192]{1,0:T(2,128)S(1)} %get-tuple-element.29, f32[4,8192]{1,0:T(4,128)S(1)} %fusion.1, bf16[2,8192]{1,0:T(2,128)(2,1)S(1)} %collective-permute-done.12), kind=kLoop, calls=%fused_computation.7 | loop fusion | flops 65536 | bytes 196608 | tf_op jit(solution)/shard_map/convert_element_type | solution.py:420
  (3 shorter events, 0.1 us)
Async XLA Ops:
  0.8 3.1 %collective-permute-start = (bf16[4,5248]{1,0:T(4,128)(2,1)S(1)}, bf16[4,5248]{1,0:T(4,128)(2,1)S(1)}, u32[]{:S(2)}, u32[]{:S(2)}) collective-permute-start(bf16[4,5248]{1,0:T(4,128)(2,1)S(1)} %pack.1.packed_ref), channel_id=1, source_target_pairs={{2,0},{4,2},{6,4},{8,6},{10,8},{12,10},{14,12},{16,14},{18,16},{20... | collective-permute-start | bytes 125960 | tf_op jit(solution)/shard_map/ppermute | solution.py:304
  5.7 7.2 %collective-permute-start.1 = (bf16[4,4096]{1,0:T(4,128)(2,1)S(1)}, bf16[4,4096]{1,0:T(4,128)(2,1)S(1)}, u32[]{:S(2)}, u32[]{:S(2)}) collective-permute-start(bf16[4,4096]{1,0:T(4,128)(2,1)S(1)} %attend.2.refs_0_), channel_id=1, source_target_pairs={{0,2},{2,4},{4,6},{6,8},{8,10},{10,12},{12,14},{14,16},{16,18},{18... | collective-permute-start | bytes 98312 | tf_op jit(solution)/shard_map/ppermute | solution.py:335
  12.9 3.8 %collective-permute-start.2 = (bf16[2,4096]{1,0:T(2,128)(2,1)S(1)}, bf16[2,4096]{1,0:T(2,128)(2,1)S(1)}, u32[]{:S(2)}, u32[]{:S(2)}) collective-permute-start(bf16[2,4096]{1,0:T(2,128)(2,1)S(1)} %get-tuple-element.26), channel_id=1, source_target_pairs={{0,1},{1,0},{2,3},{3,2},{4,5},{5,4},{6,7},{7,6},{8,9},{9,8},{10,11... | collective-permute-start | bytes 49160 | tf_op jit(solution)/shard_map/ppermute | solution.py:367
  16.9 6.2 %collective-permute-start.3 = (bf16[2,8192]{1,0:T(2,128)(2,1)S(1)}, bf16[2,8192]{1,0:T(2,128)(2,1)S(1)}, u32[]{:S(2)}, u32[]{:S(2)}) collective-permute-start(bf16[2,8192]{1,0:T(2,128)(2,1)S(1)} %get-tuple-element.35.refs_0_), channel_id=1, source_target_pairs={{0,16},{2,18},{4,20},{6,22},{8,24},{10,26},{12,28},{14,30},{16,0},... | collective-permute-start | bytes 98312 | tf_op jit(solution)/shard_map/ppermute | solution.py:268
  23.2 7.0 %collective-permute-start.6 = (bf16[4,8192]{1,0:T(4,128)(2,1)S(1)}, bf16[4,8192]{1,0:T(4,128)(2,1)S(1)}, u32[]{:S(2)}, u32[]{:S(2)}) collective-permute-start(bf16[4,8192]{1,0:T(4,128)(2,1)S(1)} %join.2.after_ref.refs_0_), channel_id=1, source_target_pairs={{0,12},{2,14},{4,8},{6,10},{8,4},{10,6},{12,0},{14,2},{16,28},{18,... | collective-permute-start | bytes 196616 | tf_op jit(solution)/shard_map/ppermute | solution.py:268
  25.3 5.0 %collective-permute-start.5 = (bf16[4,8192]{1,0:T(4,128)(2,1)S(1)}, bf16[4,8192]{1,0:T(4,128)(2,1)S(1)}, u32[]{:S(2)}, u32[]{:S(2)}) collective-permute-start(bf16[4,8192]{1,0:T(4,128)(2,1)S(1)} %join.2.after_ref.refs_0_), channel_id=1, source_target_pairs={{0,8},{2,10},{4,12},{6,14},{8,0},{10,2},{12,4},{14,6},{16,24},{18,... | collective-permute-start | bytes 196616 | tf_op jit(solution)/shard_map/ppermute | solution.py:268
  25.7 4.6 %collective-permute-start.4 = (bf16[4,8192]{1,0:T(4,128)(2,1)S(1)}, bf16[4,8192]{1,0:T(4,128)(2,1)S(1)}, u32[]{:S(2)}, u32[]{:S(2)}) collective-permute-start(bf16[4,8192]{1,0:T(4,128)(2,1)S(1)} %join.2.after_ref.refs_0_), channel_id=1, source_target_pairs={{0,4},{2,6},{4,0},{6,2},{8,12},{10,14},{12,8},{14,10},{16,20},{18,... | collective-permute-start | bytes 196616 | tf_op jit(solution)/shard_map/ppermute | solution.py:268
  30.4 1.6 %collective-permute-start.7 = (bf16[16,8192]{1,0:T(8,128)(2,1)S(1)}, bf16[16,8192]{1,0:T(8,128)(2,1)S(1)}, u32[]{:S(2)}, u32[]{:S(2)}) collective-permute-start(bf16[16,8192]{1,0:T(8,128)(2,1)S(1)} %join.3.near_ref), channel_id=1, source_target_pairs={{0,2},{2,0},{4,6},{6,4},{8,10},{10,8},{12,14},{14,12},{16,18},{18,... | collective-permute-start | bytes 786440 | tf_op jit(solution)/shard_map/ppermute | solution.py:268
  41.4 1.6 %collective-permute-start.8 = (bf16[16,8192]{1,0:T(8,128)(2,1)S(1)}, bf16[16,8192]{1,0:T(8,128)(2,1)S(1)}, u32[]{:S(2)}, u32[]{:S(2)}) collective-permute-start(bf16[16,8192]{1,0:T(8,128)(2,1)S(1)} %get-tuple-element.40), channel_id=1, source_target_pairs={{0,2},{2,0},{4,6},{6,4},{8,10},{10,8},{12,14},{14,12},{16,18},{18,... | collective-permute-start | bytes 786440 | tf_op jit(solution)/shard_map/ppermute | solution.py:268
  43.1 4.3 %collective-permute-start.9 = (bf16[4,8192]{1,0:T(4,128)(2,1)S(1)}, bf16[4,8192]{1,0:T(4,128)(2,1)S(1)}, u32[]{:S(2)}, u32[]{:S(2)}) collective-permute-start(bf16[4,8192]{1,0:T(4,128)(2,1)S(1)} %get-tuple-element.43), channel_id=1, source_target_pairs={{0,4},{2,6},{4,0},{6,2},{8,12},{10,14},{12,8},{14,10},{16,20},{18,... | collective-permute-start | bytes 196616 | tf_op jit(solution)/shard_map/ppermute | solution.py:268
  44.2 5.6 %collective-permute-start.11 = (bf16[4,8192]{1,0:T(4,128)(2,1)S(1)}, bf16[4,8192]{1,0:T(4,128)(2,1)S(1)}, u32[]{:S(2)}, u32[]{:S(2)}) collective-permute-start(bf16[4,8192]{1,0:T(4,128)(2,1)S(1)} %get-tuple-element.44), channel_id=1, source_target_pairs={{0,12},{2,14},{4,8},{6,10},{8,4},{10,6},{12,0},{14,2},{16,28},{18,... | collective-permute-start | bytes 196616 | tf_op jit(solution)/shard_map/ppermute | solution.py:268
  46.5 4.3 %collective-permute-start.10 = (bf16[4,8192]{1,0:T(4,128)(2,1)S(1)}, bf16[4,8192]{1,0:T(4,128)(2,1)S(1)}, u32[]{:S(2)}, u32[]{:S(2)}) collective-permute-start(bf16[4,8192]{1,0:T(4,128)(2,1)S(1)} %get-tuple-element.45), channel_id=1, source_target_pairs={{0,8},{2,10},{4,12},{6,14},{8,0},{10,2},{12,4},{14,6},{16,24},{18,... | collective-permute-start | bytes 196616 | tf_op jit(solution)/shard_map/ppermute | solution.py:268
  50.9 4.9 %collective-permute-start.12 = (bf16[2,8192]{1,0:T(2,128)(2,1)S(1)}, bf16[2,8192]{1,0:T(2,128)(2,1)S(1)}, u32[]{:S(2)}, u32[]{:S(2)}) collective-permute-start(bf16[2,8192]{1,0:T(2,128)(2,1)S(1)} %slice.47), channel_id=1, source_target_pairs={{0,16},{2,18},{4,20},{6,22},{8,24},{10,26},{12,28},{14,30},{16,0},... | collective-permute-start | bytes 98312 | tf_op jit(solution)/shard_map/ppermute | solution.py:268

commit v4 on v3

--- a/solution.py
+++ b/solution.py
@@ -13,6 +13,7 @@
 TILE = 8
 DEAD = -1e30
 MIB = 1024 * 1024
+WHILE_EXCHANGING = pl.CostEstimate(flops=20 * 10**9, bytes_accessed=64 * MIB, transcendentals=0)
 
 VMEM = pl.BlockSpec(memory_space=pltpu.VMEM)
 SMEM = pl.BlockSpec(memory_space=pltpu.SMEM)
@@ -136,106 +137,60 @@
         move.wait()
 
 
-def load_kernel(skip, after_ref, gate_hbm, up_hbm, token_ref, gate_ref, up_ref, sems):
-    del after_ref
-    moves = copies(
-        [
-            (source.at[pl.ds(skip, target.shape[0])], target)
-            for source, target in ((gate_hbm, gate_ref), (up_hbm, up_ref))
-        ],
-        sems,
-    )
-    for move in moves:
-        move.start()
-    token_ref[...] = jnp.zeros_like(token_ref)
-    for move in moves:
-        move.wait()
-
-
-def merge_kernel(own_ref, behind_ref, *refs):
-    stay_ref, cross_ref = refs[-2:]
+def merge_kernel(own_ref, behind_ref, residual_ref, cross_ref, stay_ref):
     head = lax.axis_index("head")
-    part = stay_ref.shape[0]
+    part, width = cross_ref.shape
     both = own_ref[...].astype(jnp.float32) + behind_ref[...].astype(jnp.float32)
     low, high = both[:part], both[part : 2 * part]
-    stay_ref[...] = jnp.where(head == 0, low, high).astype(jnp.bfloat16)
     cross_ref[...] = jnp.where(head == 0, high, low).astype(jnp.bfloat16)
-
-
-def norm_kernel(stay_ref, cross_ref, residual_ref, gain_ref, *refs):
-    middle_ref, normed_ref = refs[-2:]
+    stay_ref[:, :width] = jnp.where(head == 0, low, high).astype(jnp.bfloat16)
+    stay_ref[:, width:] = residual_ref[...]
+
+
+def norm_kernel(stay_ref, cross_ref, far_stay_ref, far_cross_ref, gain_ref, middle_ref, normed_ref):
     head = lax.axis_index("head")
-    half = stay_ref.shape[1]
+    part, half = cross_ref.shape
     f32 = jnp.float32
-    same, other = stay_ref[...].astype(f32), cross_ref[...].astype(f32)
-    low = residual_ref[:, :half].astype(f32) + jnp.where(head == 0, same, other)
-    high = residual_ref[:, half:].astype(f32) + jnp.where(head == 0, other, same)
-    middle_ref[:, :half] = low
-    middle_ref[:, half:] = high
-    square = jnp.sum(low * low, axis=-1, keepdims=True)
-    square = square + jnp.sum(high * high, axis=-1, keepdims=True)
-    scale = lax.rsqrt(square / (2 * half) + 1e-05)
-    normed_ref[:, :half] = (low * scale * gain_ref[:, :half]).astype(jnp.bfloat16)
-    normed_ref[:, half:] = (high * scale * gain_ref[:, half:]).astype(jnp.bfloat16)
+    for i, (stay, cross) in enumerate(((stay_ref, cross_ref), (far_stay_ref, far_cross_ref))):
+        same, other = stay[:, :half].astype(f32), cross[...].astype(f32)
+        low = stay[:, half : 2 * half].astype(f32) + jnp.where(head == 0, same, other)
+        high = stay[:, 2 * half :].astype(f32) + jnp.where(head == 0, other, same)
+        if i == 0:
+            middle_ref[:, :half] = low
+            middle_ref[:, half:] = high
+        square = jnp.sum(low * low, axis=-1, keepdims=True)
+        square = square + jnp.sum(high * high, axis=-1, keepdims=True)
+        scale = lax.rsqrt(square / (2 * half) + 1e-05)
+        rows = slice(i * part, (i + 1) * part)
+        normed_ref[rows, :half] = (low * scale * gain_ref[:, :half]).astype(jnp.bfloat16)
+        normed_ref[rows, half:] = (high * scale * gain_ref[:, half:]).astype(jnp.bfloat16)
 
 
 def feed_kernel(
-    brought, keep_ref, gate_scale_ref, up_scale_ref, down_keep_ref, down_scale_ref,
-    near_ref, far_ref, gate_hbm, up_hbm, down_hbm, *refs,
+    keep_ref, gate_scale_ref, up_scale_ref, down_keep_ref, down_scale_ref,
+    near_ref, far_ref, gate_ref, up_ref, down_ref, stay_ref, send_ref, hidden, total,
 ):
     columns, keep = keep_ref.shape
     half = near_ref.shape[0]
-    rest = columns - brought
-    stay_ref, send_ref, gate_rest, up_rest, down, hidden, total, sems = refs[-8:]
-    gates, ups = [], []
-    pieces = refs[: 2 if brought else 0]
-    for gate_piece, up_piece in zip(pieces[0::2], pieces[1::2]):
-        gates += [gate_piece.at[i] for i in range(gate_piece.shape[0])]
-        ups += [up_piece.at[i] for i in range(up_piece.shape[0])]
-    gates += [gate_rest.at[i] for i in range(rest)]
-    ups += [up_rest.at[i] for i in range(rest)]
-    moves = copies(
-        (
-            (gate_hbm.at[pl.ds(brought, rest)], gate_rest),
-            (up_hbm.at[pl.ds(brought, rest)], up_rest),
-        ),
-        sems.at[0],
-    )
-    late = columns // 4
-    ends = [0, columns - late, columns] if late else [0, columns]
-    down_moves = copies(
-        [
-            (down_hbm.at[pl.ds(start, end - start)], down.at[pl.ds(start, end - start)])
-            for start, end in zip(ends, ends[1:])
-        ],
-        sems.at[1],
-    )
-    for move in moves + down_moves:
-        move.start()
     total[...] = jnp.zeros_like(total)
 
     for c in range(columns):
-        if c == brought:
-            for move in moves:
-                move.wait()
         gate_sum = jnp.zeros((2 * half, BLK), jnp.float32)
         up_sum = jnp.zeros((2 * half, BLK), jnp.float32)
         for k in range(keep):
             where = pl.ds(pl.multiple_of(keep_ref[c, k] * BLK, BLK), BLK)
             picked = jnp.concatenate([near_ref[:, where], far_ref[:, where]], axis=0)
             both = jnp.dot(
-                picked, jnp.concatenate([gates[c][k], ups[c][k]], axis=1),
+                picked, jnp.concatenate([gate_ref[c, k], up_ref[c, k]], axis=1),
                 preferred_element_type=jnp.float32,
             )
             gate_sum += gate_scale_ref[c, k] * both[:, :BLK]
             up_sum += up_scale_ref[c, k] * both[:, BLK:]
         hidden[c] = (gate_sum / (1.0 + jnp.exp(-gate_sum)) * up_sum).astype(jnp.bfloat16)
     for c in range(columns):
-        if c in ends:
-            down_moves[ends.index(c)].wait()
         for k in range(0, keep, 2):
             both = jnp.dot(
-                hidden[c], jnp.concatenate([down[c, k], down[c, k + 1]], axis=1),
+                hidden[c], jnp.concatenate([down_ref[c, k], down_ref[c, k + 1]], axis=1),
                 preferred_element_type=jnp.float32,
             )
             for j in range(2):
@@ -245,23 +200,24 @@
     send_ref[...] = total[half:, :].astype(jnp.bfloat16)
 
 
-def join_kernel(count, *refs):
+def join_kernel(*refs):
     out_ref = refs[-1]
     height = refs[0].shape[0]
-    for i, ref in enumerate(refs[:count]):
+    for i, ref in enumerate(refs[:-1]):
         out_ref[i * height : (i + 1) * height, :] = ref[...]
 
 
-def joined(blocks, tokens):
+def joined(blocks):
     height, width = blocks[0].shape
     return pl.pallas_call(
-        functools.partial(join_kernel, len(blocks)),
+        join_kernel,
         out_shape=jax.ShapeDtypeStruct((len(blocks) * height, width), blocks[0].dtype),
-        in_specs=[VMEM] * (len(blocks) + len(tokens)),
+        in_specs=[VMEM] * len(blocks),
         out_specs=VMEM,
         compiler_params=pltpu.CompilerParams(vmem_limit_bytes=2 * MIB),
+        cost_estimate=WHILE_EXCHANGING,
         name="join",
-    )(*blocks, *tokens)
+    )(*blocks)
 
 
 def swapped(block, bits):
@@ -334,81 +290,61 @@
     ahead = attended(following, rows)
     behind = lax.ppermute(ahead, "wide", [(i, i + 1) for i in range(wide - 1)])
     mixed = attended(own, 0, ahead)
-    per_load = columns // 2
-    portion = pltpu.VMEM((per_load, *gate_blocks.shape[1:]), bf16)
-    pieces = []
-
-    def load(after):
-        if not per_load:
-            return []
-        token, gate_piece, up_piece = pl.pallas_call(
-            functools.partial(load_kernel, len(pieces) // 2 * per_load),
-            out_shape=(jax.ShapeDtypeStruct((8, HD), f32), portion, portion),
-            in_specs=[VMEM, HBM, HBM],
-            out_specs=(VMEM,) * 3,
-            scratch_shapes=[pltpu.SemaphoreType.DMA((2,))],
-            compiler_params=pltpu.CompilerParams(vmem_limit_bytes=2 * MIB),
-            cost_estimate=pl.CostEstimate(
-                flops=0, bytes_accessed=4 * gate_blocks.size // 2, transcendentals=0
-            ),
-            name="load",
-        )(after, *in_hbm([gate_blocks, up_blocks]))
-        pieces.extend([gate_piece, up_piece])
-        return [token]
-
-    stay, cross = pl.pallas_call(
+    bits = [1 << b for b in range(wide.bit_length() - 1)]
+    stages = [(bits[0],), tuple(bits[1:3]), *[(bit,) for bit in bits[3:]]]
+    high = bits[-1]
+    cross, stay = pl.pallas_call(
         merge_kernel,
-        out_shape=(jax.ShapeDtypeStruct((part, width), bf16),) * 2,
-        in_specs=[VMEM] * 2,
+        out_shape=(
+            jax.ShapeDtypeStruct((part, width), bf16),
+            jax.ShapeDtypeStruct((part, width + model), bf16),
+        ),
+        in_specs=[VMEM] * 3,
         out_specs=(VMEM,) * 2,
         compiler_params=pltpu.CompilerParams(vmem_limit_bytes=2 * MIB),
         name="merge",
-    )(mixed, behind)
-    crossed = lax.ppermute(cross, "head", [(h, 1 - h) for h in range(heads)])
-    middle, normed = pl.pallas_call(
+    )(mixed, behind, residual)
+    far_cross = lax.ppermute(
+        cross,
+        ("wide", "head"),
+        [(i * heads + h, (i ^ high) * heads + 1 - h) for i in range(wide) for h in range(heads)],
+    )
+    far_stay = swapped(stay, high)
+    near_cross = lax.ppermute(cross, "head", [(h, 1 - h) for h in range(heads)])
+    middle, gathered = pl.pallas_call(
         norm_kernel,
         out_shape=(
             jax.ShapeDtypeStruct((part, model), f32),
-            jax.ShapeDtypeStruct((part, model), bf16),
-        ),
-        in_specs=[VMEM] * 4,
+            jax.ShapeDtypeStruct((2 * part, model), bf16),
+        ),
+        in_specs=[VMEM] * 5,
         out_specs=(VMEM,) * 2,
         compiler_params=pltpu.CompilerParams(vmem_limit_bytes=2 * MIB),
+        cost_estimate=WHILE_EXCHANGING,
         name="norm",
-    )(stay, crossed, residual, gain)
-
-    bits = [1 << b for b in range(wide.bit_length() - 1)]
-    stages = [(bits[0],), tuple(bits[1:3]), *[(bit,) for bit in bits[3:]]]
-    gathered = normed
-    for stage in stages[:0:-1]:
-        blocks = [gathered] + [swapped(gathered, s) for s in combined(stage)]
-        tokens = load(gathered) if len(stage) > 1 else []
-        gathered = joined(blocks, tokens)
+    )(stay, near_cross, far_stay, far_cross, gain)
+    for stage in stages[-2:0:-1]:
+        gathered = joined([gathered] + [swapped(gathered, s) for s in combined(stage)])
     far = swapped(gathered, bits[0])
 
     half = gathered.shape[0]
-    rest = columns - len(pieces) // 2 * per_load
-    kept_back = [pltpu.VMEM((rest, *gate_blocks.shape[1:]), bf16)] * 2
-    size = 2 * half * model * 4 + half * model * 6 + 2 * down_blocks.size
-    size += 4 * rest * gate_blocks.size // columns
     kept, sent = pl.pallas_call(
-        functools.partial(feed_kernel, columns - rest),
+        feed_kernel,
         out_shape=(
             jax.ShapeDtypeStruct((half, model), f32),
             jax.ShapeDtypeStruct((half, model), bf16),
         ),
-        in_specs=[SMEM] * 5 + [VMEM] * 2 + [HBM] * 3 + [VMEM] * len(pieces),
+        in_specs=[SMEM] * 5 + [VMEM] * 5,
         out_specs=(VMEM,) * 2,
-        scratch_shapes=kept_back
-        + [
-            pltpu.VMEM(down_blocks.shape, bf16),
+        scratch_shapes=[
             pltpu.VMEM((columns, 2 * half, BLK), bf16),
             pltpu.VMEM((2 * half, model), f32),
-            pltpu.SemaphoreType.DMA((2, 2)),
         ],
-        compiler_params=pltpu.CompilerParams(vmem_limit_bytes=size + 4 * MIB),
+        compiler_params=pltpu.CompilerParams(
+            vmem_limit_bytes=2 * half * model * 4 + half * model * 6 + 4 * MIB
+        ),
         name="feed",
-    )(*lists, gathered, far, *in_hbm([gate_blocks, up_blocks, down_blocks]), *pieces)
+    )(*lists, gathered, far, gate_blocks, up_blocks, down_blocks)
 
     total = kept + swapped(sent, bits[0]).astype(f32)
     for stage in stages[1:]:

time: 56.7 us -> 51.9 us (0.915)
  Pallas kernels: 19.2 us -> 11.8 us
  waiting for transfers between devices: 13.2 us -> 16.5 us
  starting transfers between devices: 22.9 us -> 22.1 us
    pallas_call x4 -> x2, Pallas kernels: 13 us -> 5.58 us  [the longest x1 5.51 us: per_device(): pl.pallas_call(feed_kernel, out_shape=(jax.ShapeDtypeStruct((half, model)...]
    ppermute x1 -> x2, waiting for transfers between devices: 2.22 us -> 4 us  [the longest x1 3.99 us: per_device(): lax.ppermute(cross, ('wide', 'head'), [(i * heads + h, (i ^ high) * heads...]
    ppermute x10, waiting for transfers between devices: 10.9 us -> 12.4 us  [swapped(): lax.ppermute(block, 'wide', [(i, i ^ bits) for i in range(lax.axis_size('...]
    ppermute x10, starting transfers between devices: 14.6 us -> 13.8 us  [swapped(): lax.ppermute(block, 'wide', [(i, i ^ bits) for i in range(lax.axis_size('...]
    ppermute x1 -> x2, starting transfers between devices: 1.58 us -> 1.54 us  [the longest x1 1.03 us: per_device(): lax.ppermute(cross, ('wide', 'head'), [(i * heads + h, (i ^ high) * heads...]
  transfers between devices with their start and end apart: 13 -> 14, of which waited for: 9 -> 11; matrix products, arithmetic and copies ran while one was open for 0% -> 0% of each run, Pallas kernels for 12% -> 7%
where the time goes in v4:
time: 51.9 us; the launch traced here: 51.6 us
  starting transfers between devices  22.1 us (43%)
  waiting for transfers between devices  16.5 us (32%)
  Pallas kernels  11.8 us (23%)
  other arithmetic  0.77 us (1%)
    ppermute x10, starting transfers between devices, swapped(): lax.ppermute(block, 'wide', [(i, i ^ bits) for i in range(lax.axis_size('...  13.8 us
    ppermute x10, waiting for transfers between devices, swapped(): lax.ppermute(block, 'wide', [(i, i ^ bits) for i in range(lax.axis_size('...  12.4 us
    pallas_call x1, Pallas kernels, per_device(): pl.pallas_call(feed_kernel, out_shape=(jax.ShapeDtypeStruct((half, model)...  5.51 us
    ppermute x1, starting transfers between devices, per_device(): behind = lax.ppermute(ahead, 'wide', [(i, i + 1) for i in range(wide - 1)])  5.44 us
    ppermute x1, waiting for transfers between devices, per_device(): lax.ppermute(cross, ('wide', 'head'), [(i * heads + h, (i ^ high) * heads...  3.99 us
    pallas_call x2, Pallas kernels, attended(): pl.pallas_call(functools.partial(attend_kernel, groups, per_group, shift)...  3.5 us
    pallas_call x1, Pallas kernels, per_device(): pl.pallas_call(functools.partial(prepare_kernel, len(stored)), out_shape=...  1.71 us
    ppermute x1, starting transfers between devices, per_device(): following = lax.ppermute(own, 'wide', [(i, i - 1) for i in range(1, wide)])  1.29 us
  transfers between devices with their start and end apart: 14, of which 11 were waited for; matrix products, arithmetic and copies ran while one was open for 0% of the time, Pallas kernels for 7%

profile of v4, /device:TPU:0, one launch (start us, length us, event | category | flops | bytes accessed | tf_op | source)
XLA Modules:
  0.0 51.6 jit_solution(10298536984938367510)
XLA Ops:
  0.0 0.8 %pack.1.packed_ref = bf16[4,5248]{1,0:T(4,128)(2,1)S(1)} custom-call(bf16[4,4096]{1,0:T(4,128)(2,1)} %query_hbm.1, bf16[4,512]{1,0:T(4,128)(2,1)} %key_hbm.1, bf16[4,512]{1,0:T(4,128)(2,1)} %value_hbm.1, s32[4]{0:T(128)} %parent_hbm.1), custom_call_target="tpu_custom_call" | custom-call | tf_op jit(solution)/shard_map/pack/pallas_call | solution.py:248
  0.8 1.3 %collective-permute-start = (bf16[4,5248]{1,0:T(4,128)(2,1)S(1)}, bf16[4,5248]{1,0:T(4,128)(2,1)S(1)}, u32[]{:S(2)}, u32[]{:S(2)}) collective-permute-start(bf16[4,5248]{1,0:T(4,128)(2,1)S(1)} %pack.1.packed_ref), channel_id=1, source_target_pairs={{2,0},{4,2},{6,4},{8,6},{10,8},{12,10},{14,12},{16,14},{18,16},{20... | collective-permute-start | bytes 125960 | tf_op jit(solution)/shard_map/ppermute | solution.py:260
  2.1 1.7 %prepare.1 = (f32[4,1024]{1,0:T(4,128)S(1)}, bf16[2,64,16,512]{3,2,1,0:T(8,128)(2,1)S(1)}, bf16[2,8192]{1,0:T(2,128)(2,1)S(1)}, f32[1,8192]{1,0:T(1,128)S(1)}, s...) custom-call(s32[4,16]{1,0:T(4,128)} %refs_0_.1, ...), custom_call_target="tpu_custom_call" | custom-call | bytes 8388608 | tf_op jit(solution)/shard_map/prepare/pallas_call | solution.py:265
  3.8 0.1 collective-permute-done.packed_ref
  3.9 1.7 %attend.2.refs_0_ = bf16[4,4096]{1,0:T(4,128)(2,1)S(1)} custom-call(bf16[4,5248]{1,0:T(4,128)(2,1)S(1)} %collective-permute-done.packed_ref, bf16[2,64,16,512]{3,2,1,0:T(8,128)(2,1)S(1)} %get-tuple-element.20.pool_ref, f32[4,1024]{1,0:T(4,128)S(1)} %get-tuple-element.21.bias_ref), custom_call_target="tpu_custom_call" | custom-call | tf_op jit(solution)/shard_map/attend/pallas_call | solution.py:281
  5.7 5.4 %collective-permute-start.1 = (bf16[4,4096]{1,0:T(4,128)(2,1)S(1)}, bf16[4,4096]{1,0:T(4,128)(2,1)S(1)}, u32[]{:S(2)}, u32[]{:S(2)}) collective-permute-start(bf16[4,4096]{1,0:T(4,128)(2,1)S(1)} %attend.2.refs_0_), channel_id=1, source_target_pairs={{0,2},{2,4},{4,6},{6,8},{8,10},{10,12},{12,14},{14,16},{16,18},{18... | collective-permute-start | bytes 98312 | tf_op jit(solution)/shard_map/ppermute | solution.py:291
  11.1 1.8 %attend.3.own_ref = bf16[4,4096]{1,0:T(4,128)(2,1)S(1)} custom-call(bf16[4,5248]{1,0:T(4,128)(2,1)S(1)} %pack.1.packed_ref, bf16[2,64,16,512]{3,2,1,0:T(8,128)(2,1)S(1)} %get-tuple-element.20.pool_ref, f32[4,1024]{1,0:T(4,128)S(1)} %get-tuple-element.21.bias_ref, bf16[4,4096]{1,0:T(4,128)(2,1)S(1)} %attend.2.refs_0_), custom_call_target="tpu_custom_call" | custom-call | tf_op jit(solution)/shard_map/attend/pallas_call | solution.py:281
  12.9 0.0 collective-permute-done.1.behind_ref
  12.9 4.4 %collective-permute-start.3 = (bf16[2,12288]{1,0:T(2,128)(2,1)S(1)}, bf16[2,12288]{1,0:T(2,128)(2,1)S(1)}, u32[]{:S(2)}, u32[]{:S(2)}) collective-permute-start(bf16[2,12288]{1,0:T(2,128)(2,1)S(1)} %get-tuple-element.23.stay_ref), channel_id=1, source_target_pairs={{0,16},{2,18},{4,20},{6,22},{8,24},{10,26},{12,28},{14,30},{16,0},... | collective-permute-start | bytes 147464 | tf_op jit(solution)/shard_map/ppermute | solution.py:224
  17.3 1.0 %collective-permute-start.4 = (bf16[2,4096]{1,0:T(2,128)(2,1)S(1)}, bf16[2,4096]{1,0:T(2,128)(2,1)S(1)}, u32[]{:S(2)}, u32[]{:S(2)}) collective-permute-start(bf16[2,4096]{1,0:T(2,128)(2,1)S(1)} %get-tuple-element.24), channel_id=1, source_target_pairs={{0,17},{1,16},{2,19},{3,18},{4,21},{5,20},{6,23},{7,22},{8,25},{9,... | collective-permute-start | bytes 49160 | tf_op jit(solution)/shard_map/ppermute | solution.py:307
  18.3 0.5 collective-permute-start.2
  18.8 4.0 %collective-permute-done.4.far_cross_ref = bf16[2,4096]{1,0:T(2,128)(2,1)S(1)} collective-permute-done((bf16[2,4096]{1,0:T(2,128)(2,1)S(1)}, bf16[2,4096]{1,0:T(2,128)(2,1)S(1)}, u32[]{:S(2)}, u32[]{:S(2)}) %collective-permute-start.4) | collective-permute-done | bytes 16416 | tf_op jit(solution)/shard_map/ppermute | solution.py:307
  22.8 0.0 collective-permute-done.2.cross_ref
  22.8 0.0 collective-permute-done.3.far_stay_ref
  22.8 0.2 norm.1
  23.1 0.0 slice-start
  23.1 0.0 slice-start.2
  23.1 0.0 slice-start.4
  23.1 0.0 slice-start.1
  23.1 0.0 slice-start.3
  23.1 0.0 slice-start.5
  23.1 1.2 %collective-permute-start.7 = (bf16[4,8192]{1,0:T(4,128)(2,1)S(1)}, bf16[4,8192]{1,0:T(4,128)(2,1)S(1)}, u32[]{:S(2)}, u32[]{:S(2)}) collective-permute-start(bf16[4,8192]{1,0:T(4,128)(2,1)S(1)} %get-tuple-element.32.refs_0_), channel_id=1, source_target_pairs={{0,12},{2,14},{4,8},{6,10},{8,4},{10,6},{12,0},{14,2},{16,28},{18,... | collective-permute-start | bytes 196616 | tf_op jit(solution)/shard_map/ppermute | solution.py:224
  24.4 1.0 %collective-permute-start.6 = (bf16[4,8192]{1,0:T(4,128)(2,1)S(1)}, bf16[4,8192]{1,0:T(4,128)(2,1)S(1)}, u32[]{:S(2)}, u32[]{:S(2)}) collective-permute-start(bf16[4,8192]{1,0:T(4,128)(2,1)S(1)} %get-tuple-element.32.refs_0_), channel_id=1, source_target_pairs={{0,8},{2,10},{4,12},{6,14},{8,0},{10,2},{12,4},{14,6},{16,24},{18,... | collective-permute-start | bytes 196616 | tf_op jit(solution)/shard_map/ppermute | solution.py:224
  25.3 1.4 %collective-permute-start.5 = (bf16[4,8192]{1,0:T(4,128)(2,1)S(1)}, bf16[4,8192]{1,0:T(4,128)(2,1)S(1)}, u32[]{:S(2)}, u32[]{:S(2)}) collective-permute-start(bf16[4,8192]{1,0:T(4,128)(2,1)S(1)} %get-tuple-element.32.refs_0_), channel_id=1, source_target_pairs={{0,4},{2,6},{4,0},{6,2},{8,12},{10,14},{12,8},{14,10},{16,20},{18,... | collective-permute-start | bytes 196616 | tf_op jit(solution)/shard_map/ppermute | solution.py:224
  26.7 1.7 %collective-permute-done.7.refs_3_ = bf16[4,8192]{1,0:T(4,128)(2,1)S(1)} collective-permute-done((bf16[4,8192]{1,0:T(4,128)(2,1)S(1)}, bf16[4,8192]{1,0:T(4,128)(2,1)S(1)}, u32[]{:S(2)}, u32[]{:S(2)}) %collective-permute-start.7) | collective-permute-done | bytes 65568 | tf_op jit(solution)/shard_map/ppermute | solution.py:224
  28.4 0.3 collective-permute-done.6.refs_2_
  28.6 1.0 %collective-permute-done.5.refs_1_ = bf16[4,8192]{1,0:T(4,128)(2,1)S(1)} collective-permute-done((bf16[4,8192]{1,0:T(4,128)(2,1)S(1)}, bf16[4,8192]{1,0:T(4,128)(2,1)S(1)}, u32[]{:S(2)}, u32[]{:S(2)}) %collective-permute-start.5) | collective-permute-done | bytes 65568 | tf_op jit(solution)/shard_map/ppermute | solution.py:224
  29.6 0.1 join.1.near_ref
  29.7 0.1 collective-permute-start.8
  29.8 1.5 %collective-permute-done.8.far_ref = bf16[16,8192]{1,0:T(8,128)(2,1)S(1)} collective-permute-done((bf16[16,8192]{1,0:T(8,128)(2,1)S(1)}, bf16[16,8192]{1,0:T(8,128)(2,1)S(1)}, u32[]{:S(2)}, u32[]{:S(2)}) %collective-permute-start.8) | collective-permute-done | bytes 262176 | tf_op jit(solution)/shard_map/ppermute | solution.py:224
  31.3 0.0 slice-done
  31.3 0.0 slice-done.2
  31.3 0.0 slice-done.4
  31.3 0.0 slice-done.1
  31.3 0.0 slice-done.3
  31.3 0.0 slice-done.5
  31.3 5.5 %feed.1 = (f32[16,8192]{1,0:T(8,128)S(1)}, bf16[16,8192]{1,0:T(8,128)(2,1)S(1)}) custom-call(s32[8,32]{1,0:T(8,128)S(1)} %get-tuple-element.27.keep_ref, f32[8,32]{1,0:T(8,128)S(1)} %get-tuple-element.28.gate_scale_ref, f32[8,32]{1,0:T(8,128)S(1)} %get-tuple-element.29.up_scale_ref, s32[8,32]{1,0:T(8,128)S(1)} %get-tuple-element.30.down_keep_ref, ...), custom_call_target="tpu_custom_call" | custom-call | tf_op jit(solution)/shard_map/feed/pallas_call | solution.py:331
  36.9 0.2 collective-permute-start.9
  37.1 1.4 %collective-permute-done.9 = bf16[16,8192]{1,0:T(8,128)(2,1)S(1)} collective-permute-done((bf16[16,8192]{1,0:T(8,128)(2,1)S(1)}, bf16[16,8192]{1,0:T(8,128)(2,1)S(1)}, u32[]{:S(2)}, u32[]{:S(2)}) %collective-permute-start.9) | collective-permute-done | bytes 262176 | tf_op jit(solution)/shard_map/ppermute | solution.py:224
  38.5 0.1 fusion.4
  38.5 0.1 fusion.5
  38.6 1.4 %collective-permute-start.10 = (bf16[4,8192]{1,0:T(4,128)(2,1)S(1)}, bf16[4,8192]{1,0:T(4,128)(2,1)S(1)}, u32[]{:S(2)}, u32[]{:S(2)}) collective-permute-start(bf16[4,8192]{1,0:T(4,128)(2,1)S(1)} %get-tuple-element.37), channel_id=1, source_target_pairs={{0,4},{2,6},{4,0},{6,2},{8,12},{10,14},{12,8},{14,10},{16,20},{18,... | collective-permute-start | bytes 196616 | tf_op jit(solution)/shard_map/ppermute | solution.py:224
  40.0 1.7 %collective-permute-start.12 = (bf16[4,8192]{1,0:T(4,128)(2,1)S(1)}, bf16[4,8192]{1,0:T(4,128)(2,1)S(1)}, u32[]{:S(2)}, u32[]{:S(2)}) collective-permute-start(bf16[4,8192]{1,0:T(4,128)(2,1)S(1)} %get-tuple-element.38), channel_id=1, source_target_pairs={{0,12},{2,14},{4,8},{6,10},{8,4},{10,6},{12,0},{14,2},{16,28},{18,... | collective-permute-start | bytes 196616 | tf_op jit(solution)/shard_map/ppermute | solution.py:224
  41.7 0.4 collective-permute-start.11
  42.2 0.8 %collective-permute-done.10 = bf16[4,8192]{1,0:T(4,128)(2,1)S(1)} collective-permute-done((bf16[4,8192]{1,0:T(4,128)(2,1)S(1)}, bf16[4,8192]{1,0:T(4,128)(2,1)S(1)}, u32[]{:S(2)}, u32[]{:S(2)}) %collective-permute-start.10) | collective-permute-done | bytes 65568 | tf_op jit(solution)/shard_map/ppermute | solution.py:224
  42.9 2.8 %collective-permute-done.12 = bf16[4,8192]{1,0:T(4,128)(2,1)S(1)} collective-permute-done((bf16[4,8192]{1,0:T(4,128)(2,1)S(1)}, bf16[4,8192]{1,0:T(4,128)(2,1)S(1)}, u32[]{:S(2)}, u32[]{:S(2)}) %collective-permute-start.12) | collective-permute-done | bytes 65568 | tf_op jit(solution)/shard_map/ppermute | solution.py:224
  45.7 0.3 collective-permute-done.11
  46.0 0.1 fusion.1
  46.1 2.1 %collective-permute-start.13 = (bf16[2,8192]{1,0:T(2,128)(2,1)S(1)}, bf16[2,8192]{1,0:T(2,128)(2,1)S(1)}, u32[]{:S(2)}, u32[]{:S(2)}) collective-permute-start(bf16[2,8192]{1,0:T(2,128)(2,1)S(1)} %slice.47), channel_id=1, source_target_pairs={{0,16},{2,18},{4,20},{6,22},{8,24},{10,26},{12,28},{14,30},{16,0},... | collective-permute-start | bytes 98312 | tf_op jit(solution)/shard_map/ppermute | solution.py:224
  48.2 2.8 %collective-permute-done.13 = bf16[2,8192]{1,0:T(2,128)(2,1)S(1)} collective-permute-done((bf16[2,8192]{1,0:T(2,128)(2,1)S(1)}, bf16[2,8192]{1,0:T(2,128)(2,1)S(1)}, u32[]{:S(2)}, u32[]{:S(2)}) %collective-permute-start.13) | collective-permute-done | bytes 32800 | tf_op jit(solution)/shard_map/ppermute | solution.py:224
  51.0 0.7 %fusion.3 = bf16[2,8192]{1,0:T(2,128)(2,1)} fusion(f32[2,8192]{1,0:T(2,128)S(1)} %get-tuple-element.26, f32[4,8192]{1,0:T(4,128)S(1)} %fusion.1, bf16[2,8192]{1,0:T(2,128)(2,1)S(1)} %collective-permute-done.13), kind=kLoop, calls=%fused_computation.7 | loop fusion | flops 65536 | bytes 196608 | tf_op jit(solution)/shard_map/convert_element_type | solution.py:356
  (5 shorter events, 0.1 us)
Async XLA Ops:
  0.8 3.1 %collective-permute-start = (bf16[4,5248]{1,0:T(4,128)(2,1)S(1)}, bf16[4,5248]{1,0:T(4,128)(2,1)S(1)}, u32[]{:S(2)}, u32[]{:S(2)}) collective-permute-start(bf16[4,5248]{1,0:T(4,128)(2,1)S(1)} %pack.1.packed_ref), channel_id=1, source_target_pairs={{2,0},{4,2},{6,4},{8,6},{10,8},{12,10},{14,12},{16,14},{18,16},{20... | collective-permute-start | bytes 125960 | tf_op jit(solution)/shard_map/ppermute | solution.py:260
  5.7 7.2 %collective-permute-start.1 = (bf16[4,4096]{1,0:T(4,128)(2,1)S(1)}, bf16[4,4096]{1,0:T(4,128)(2,1)S(1)}, u32[]{:S(2)}, u32[]{:S(2)}) collective-permute-start(bf16[4,4096]{1,0:T(4,128)(2,1)S(1)} %attend.2.refs_0_), channel_id=1, source_target_pairs={{0,2},{2,4},{4,6},{6,8},{8,10},{10,12},{12,14},{14,16},{16,18},{18... | collective-permute-start | bytes 98312 | tf_op jit(solution)/shard_map/ppermute | solution.py:291
  12.9 9.9 %collective-permute-start.3 = (bf16[2,12288]{1,0:T(2,128)(2,1)S(1)}, bf16[2,12288]{1,0:T(2,128)(2,1)S(1)}, u32[]{:S(2)}, u32[]{:S(2)}) collective-permute-start(bf16[2,12288]{1,0:T(2,128)(2,1)S(1)} %get-tuple-element.23.stay_ref), channel_id=1, source_target_pairs={{0,16},{2,18},{4,20},{6,22},{8,24},{10,26},{12,28},{14,30},{16,0},... | collective-permute-start | bytes 147464 | tf_op jit(solution)/shard_map/ppermute | solution.py:224
  17.3 5.5 %collective-permute-start.4 = (bf16[2,4096]{1,0:T(2,128)(2,1)S(1)}, bf16[2,4096]{1,0:T(2,128)(2,1)S(1)}, u32[]{:S(2)}, u32[]{:S(2)}) collective-permute-start(bf16[2,4096]{1,0:T(2,128)(2,1)S(1)} %get-tuple-element.24), channel_id=1, source_target_pairs={{0,17},{1,16},{2,19},{3,18},{4,21},{5,20},{6,23},{7,22},{8,25},{9,... | collective-permute-start | bytes 49160 | tf_op jit(solution)/shard_map/ppermute | solution.py:307
  18.3 4.5 %collective-permute-start.2 = (bf16[2,4096]{1,0:T(2,128)(2,1)S(1)}, bf16[2,4096]{1,0:T(2,128)(2,1)S(1)}, u32[]{:S(2)}, u32[]{:S(2)}) collective-permute-start(bf16[2,4096]{1,0:T(2,128)(2,1)S(1)} %get-tuple-element.24), channel_id=1, source_target_pairs={{0,1},{1,0},{2,3},{3,2},{4,5},{5,4},{6,7},{7,6},{8,9},{9,8},{10,11... | collective-permute-start | bytes 49160 | tf_op jit(solution)/shard_map/ppermute | solution.py:313
  23.1 8.2 %slice-start = ((s8[8388608]{0:T(1024)(128)(4,1)}), s8[4194304]{0:T(1024)(128)(4,1)S(1)}, s32[]{:S(2)}) async-start(s8[8388608]{0:T(1024)(128)(4,1)} %bitcast.1), calls=%async_computation | async-start | bytes 8388608
  23.1 8.2 %slice-start.2 = ((s8[8388608]{0:T(1024)(128)(4,1)}), s8[4194304]{0:T(1024)(128)(4,1)S(1)}, s32[]{:S(2)}) async-start(s8[8388608]{0:T(1024)(128)(4,1)} %bitcast.3), calls=%async_computation.2 | async-start | bytes 8388608
  23.1 8.2 %slice-start.4 = ((s8[8388608]{0:T(1024)(128)(4,1)}), s8[4194304]{0:T(1024)(128)(4,1)S(1)}, s32[]{:S(2)}) async-start(s8[8388608]{0:T(1024)(128)(4,1)} %bitcast.5), calls=%async_computation.4 | async-start | bytes 8388608
  23.1 8.2 %slice-start.1 = ((s8[8388608]{0:T(1024)(128)(4,1)}), s8[4194304]{0:T(1024)(128)(4,1)S(1)}, s32[]{:S(2)}) async-start(s8[8388608]{0:T(1024)(128)(4,1)} %bitcast.1), calls=%async_computation.1 | async-start | bytes 8388608
  23.1 8.2 %slice-start.3 = ((s8[8388608]{0:T(1024)(128)(4,1)}), s8[4194304]{0:T(1024)(128)(4,1)S(1)}, s32[]{:S(2)}) async-start(s8[8388608]{0:T(1024)(128)(4,1)} %bitcast.3), calls=%async_computation.3 | async-start | bytes 8388608
  23.1 8.2 %slice-start.5 = ((s8[8388608]{0:T(1024)(128)(4,1)}), s8[4194304]{0:T(1024)(128)(4,1)S(1)}, s32[]{:S(2)}) async-start(s8[8388608]{0:T(1024)(128)(4,1)} %bitcast.5), calls=%async_computation.5 | async-start | bytes 8388608
  23.1 5.2 %collective-permute-start.7 = (bf16[4,8192]{1,0:T(4,128)(2,1)S(1)}, bf16[4,8192]{1,0:T(4,128)(2,1)S(1)}, u32[]{:S(2)}, u32[]{:S(2)}) collective-permute-start(bf16[4,8192]{1,0:T(4,128)(2,1)S(1)} %get-tuple-element.32.refs_0_), channel_id=1, source_target_pairs={{0,12},{2,14},{4,8},{6,10},{8,4},{10,6},{12,0},{14,2},{16,28},{18,... | collective-permute-start | bytes 196616 | tf_op jit(solution)/shard_map/ppermute | solution.py:224
  24.4 4.3 %collective-permute-start.6 = (bf16[4,8192]{1,0:T(4,128)(2,1)S(1)}, bf16[4,8192]{1,0:T(4,128)(2,1)S(1)}, u32[]{:S(2)}, u32[]{:S(2)}) collective-permute-start(bf16[4,8192]{1,0:T(4,128)(2,1)S(1)} %get-tuple-element.32.refs_0_), channel_id=1, source_target_pairs={{0,8},{2,10},{4,12},{6,14},{8,0},{10,2},{12,4},{14,6},{16,24},{18,... | collective-permute-start | bytes 196616 | tf_op jit(solution)/shard_map/ppermute | solution.py:224
  25.3 4.3 %collective-permute-start.5 = (bf16[4,8192]{1,0:T(4,128)(2,1)S(1)}, bf16[4,8192]{1,0:T(4,128)(2,1)S(1)}, u32[]{:S(2)}, u32[]{:S(2)}) collective-permute-start(bf16[4,8192]{1,0:T(4,128)(2,1)S(1)} %get-tuple-element.32.refs_0_), channel_id=1, source_target_pairs={{0,4},{2,6},{4,0},{6,2},{8,12},{10,14},{12,8},{14,10},{16,20},{18,... | collective-permute-start | bytes 196616 | tf_op jit(solution)/shard_map/ppermute | solution.py:224
  29.7 1.6 %collective-permute-start.8 = (bf16[16,8192]{1,0:T(8,128)(2,1)S(1)}, bf16[16,8192]{1,0:T(8,128)(2,1)S(1)}, u32[]{:S(2)}, u32[]{:S(2)}) collective-permute-start(bf16[16,8192]{1,0:T(8,128)(2,1)S(1)} %join.1.near_ref), channel_id=1, source_target_pairs={{0,2},{2,0},{4,6},{6,4},{8,10},{10,8},{12,14},{14,12},{16,18},{18,... | collective-permute-start | bytes 786440 | tf_op jit(solution)/shard_map/ppermute | solution.py:224
  36.9 1.6 %collective-permute-start.9 = (bf16[16,8192]{1,0:T(8,128)(2,1)S(1)}, bf16[16,8192]{1,0:T(8,128)(2,1)S(1)}, u32[]{:S(2)}, u32[]{:S(2)}) collective-permute-start(bf16[16,8192]{1,0:T(8,128)(2,1)S(1)} %get-tuple-element.34), channel_id=1, source_target_pairs={{0,2},{2,0},{4,6},{6,4},{8,10},{10,8},{12,14},{14,12},{16,18},{18,... | collective-permute-start | bytes 786440 | tf_op jit(solution)/shard_map/ppermute | solution.py:224
  38.6 4.3 %collective-permute-start.10 = (bf16[4,8192]{1,0:T(4,128)(2,1)S(1)}, bf16[4,8192]{1,0:T(4,128)(2,1)S(1)}, u32[]{:S(2)}, u32[]{:S(2)}) collective-permute-start(bf16[4,8192]{1,0:T(4,128)(2,1)S(1)} %get-tuple-element.37), channel_id=1, source_target_pairs={{0,4},{2,6},{4,0},{6,2},{8,12},{10,14},{12,8},{14,10},{16,20},{18,... | collective-permute-start | bytes 196616 | tf_op jit(solution)/shard_map/ppermute | solution.py:224
  40.0 5.7 %collective-permute-start.12 = (bf16[4,8192]{1,0:T(4,128)(2,1)S(1)}, bf16[4,8192]{1,0:T(4,128)(2,1)S(1)}, u32[]{:S(2)}, u32[]{:S(2)}) collective-permute-start(bf16[4,8192]{1,0:T(4,128)(2,1)S(1)} %get-tuple-element.38), channel_id=1, source_target_pairs={{0,12},{2,14},{4,8},{6,10},{8,4},{10,6},{12,0},{14,2},{16,28},{18,... | collective-permute-start | bytes 196616 | tf_op jit(solution)/shard_map/ppermute | solution.py:224
  41.7 4.3 %collective-permute-start.11 = (bf16[4,8192]{1,0:T(4,128)(2,1)S(1)}, bf16[4,8192]{1,0:T(4,128)(2,1)S(1)}, u32[]{:S(2)}, u32[]{:S(2)}) collective-permute-start(bf16[4,8192]{1,0:T(4,128)(2,1)S(1)} %get-tuple-element.39), channel_id=1, source_target_pairs={{0,8},{2,10},{4,12},{6,14},{8,0},{10,2},{12,4},{14,6},{16,24},{18,... | collective-permute-start | bytes 196616 | tf_op jit(solution)/shard_map/ppermute | solution.py:224
  46.1 4.9 %collective-permute-start.13 = (bf16[2,8192]{1,0:T(2,128)(2,1)S(1)}, bf16[2,8192]{1,0:T(2,128)(2,1)S(1)}, u32[]{:S(2)}, u32[]{:S(2)}) collective-permute-start(bf16[2,8192]{1,0:T(2,128)(2,1)S(1)} %slice.47), channel_id=1, source_target_pairs={{0,16},{2,18},{4,20},{6,22},{8,24},{10,26},{12,28},{14,30},{16,0},... | collective-permute-start | bytes 98312 | tf_op jit(solution)/shard_map/ppermute | solution.py:224

commit v5 on v4

--- a/solution.py
+++ b/solution.py
@@ -10,7 +10,8 @@
 
 HD = 128
 BLK = 128
-TILE = 8
+PACKED = 16
+GROUP = 4
 DEAD = -1e30
 MIB = 1024 * 1024
 WHILE_EXCHANGING = pl.CostEstimate(flops=20 * 10**9, bytes_accessed=64 * MIB, transcendentals=0)
@@ -60,79 +61,88 @@
         move.wait()
 
 
-def attend_kernel(groups, per_group, shift, packed_ref, pool_ref, bias_ref, *refs):
+def attend_kernel(groups, per_group, shift, packed_ref, pool_ref, owner_ref, *refs):
     out_ref = refs[-1]
     rows = packed_ref.shape[0]
-    width = groups * per_group * HD
     kv_width = groups * HD
-    spots = bias_ref.shape[1]
-    fold = TILE // rows
-
-    def tiled(block):
-        return jnp.concatenate([block] * fold, axis=0)
-
-    packed = packed_ref[...].astype(jnp.float32)
-    parent = packed[:, width + 2 * kv_width : width + 2 * kv_width + 1] + shift
-    bias = jnp.full((rows, spots), DEAD, jnp.float32)
+    width = kv_width * per_group
+    spots = owner_ref.shape[0]
+    f32, bf16 = jnp.float32, jnp.bfloat16
+
+    query = packed_ref[:, :width].astype(f32)
+    tall = []
+    for g in range(groups):
+        heads = range(g * per_group, (g + 1) * per_group)
+        block = jnp.concatenate([query[:, j * HD : (j + 1) * HD] for j in heads], axis=0)
+        gap = jnp.zeros_like(block)
+        tall.append(jnp.concatenate([block if i == g else gap for i in range(groups)], axis=1))
+    tall = jnp.concatenate(tall, axis=0).astype(bf16)
+    lanes = tall.shape[0]
+
+    branch = lax.broadcasted_iota(jnp.int32, (1, lanes), 1) % rows
+    code = packed_ref[:, width + 2 * kv_width :].astype(f32) + shift
+    parent = jnp.zeros((1, lanes), f32)
     for r in range(rows):
-        bias = jnp.where(parent == r, bias_ref[r : r + 1, :], bias)
-    bias = tiled(bias)
-    here = (parent >= 0) & (parent < rows)
+        parent = jnp.where(branch == r, code[r : r + 1, :], parent)
+    gap = jnp.zeros((PACKED - rows, kv_width), f32)
+    key_own, value_own = (
+        jnp.concatenate([packed_ref[:, start : start + kv_width].astype(f32), gap], axis=0).astype(bf16)
+        for start in (width, width + kv_width)
+    )
+    of_branch = lax.broadcasted_iota(jnp.int32, (PACKED, lanes), 0) == branch
+
+    def against(keys):
+        return lax.dot_general(keys, tall, (((1,), (1,)), ((), ())), preferred_element_type=f32)
+
+    def mixed(weights, values):
+        return lax.dot_general(
+            weights, values, (((0,), (0,)), ((), ())), preferred_element_type=f32
+        )
 
     factor = 1.0 / math.sqrt(HD)
-    for g in range(groups):
-        base = g * per_group * HD
-        query = jnp.concatenate(
-            [packed[:, base + j * HD : base + (j + 1) * HD] for j in range(per_group)], axis=0
-        )
-        key_own = tiled(packed[:, width + g * HD : width + (g + 1) * HD])
-        value_own = tiled(packed[:, width + kv_width + g * HD : width + kv_width + (g + 1) * HD])
-        keys = pool_ref[0, :, :, g * HD : (g + 1) * HD].reshape(spots, HD)
-        values = pool_ref[1, :, :, g * HD : (g + 1) * HD].reshape(spots, HD)
-        scores = lax.dot_general(
-            query.astype(jnp.bfloat16), keys, (((1,), (1,)), ((), ())),
-            preferred_element_type=jnp.float32,
-        )
-        scores = scores.reshape(-1, TILE, spots) * factor + bias[None]
-        query = query.reshape(-1, TILE, HD)
-        own = jnp.sum(query * key_own[None], axis=-1, keepdims=True) * factor
-        top = jnp.maximum(jnp.max(scores, axis=-1, keepdims=True), own)
-        expo = jnp.exp(scores - top)
-        own_expo = jnp.exp(own - top)
-        total = jnp.sum(expo, axis=-1, keepdims=True) + own_expo
-        weights = (expo / total).astype(jnp.bfloat16)
-        own_weight = (own_expo / total).astype(jnp.bfloat16).astype(jnp.float32)
-        mixture = jnp.dot(
-            weights.reshape(per_group * rows, spots), values, preferred_element_type=jnp.float32
-        )
-        mixture = mixture.reshape(-1, TILE, HD) + own_weight * value_own[None]
-        mixture = mixture.reshape(per_group * rows, HD)
-        for j in range(per_group):
-            out_ref[:, base + j * HD : base + (j + 1) * HD] = jnp.where(
-                here, mixture[j * rows : (j + 1) * rows], 0.0
-            ).astype(jnp.bfloat16)
+    scores = against(pool_ref[0].reshape(spots, kv_width)) * factor
+    scores = jnp.where(owner_ref[...] == parent, scores, DEAD)
+    own = jnp.sum(jnp.where(of_branch, against(key_own), 0.0), axis=0, keepdims=True) * factor
+    top = jnp.maximum(jnp.max(scores, axis=0, keepdims=True), own)
+    expo = jnp.exp(scores - top)
+    own_expo = jnp.exp(own - top)
+    share = 1.0 / (jnp.sum(expo, axis=0, keepdims=True) + own_expo)
+    mixture = mixed((expo * share).astype(bf16), pool_ref[1].reshape(spots, kv_width))
+    own_weight = jnp.where(of_branch, own_expo * share, 0.0).astype(bf16)
+    mixture = mixture + mixed(own_weight, value_own)
+    here = (code[:, :1] >= 0) & (code[:, :1] < rows)
+    for j in range(groups * per_group):
+        g = j // per_group
+        out_ref[:, j * HD : (j + 1) * HD] = jnp.where(
+            here, mixture[j * rows : (j + 1) * rows, g * HD : (g + 1) * HD], 0.0
+        ).astype(bf16)
 
 
 def prepare_kernel(count, *refs):
     page_hbm, length_hbm, sources = refs[0], refs[1], refs[2 : 2 + count]
-    bias_ref, targets = refs[2 + count], refs[3 + count : 3 + 2 * count]
-    page_ref, length_ref, sems = refs[3 + 2 * count :]
+    lists, refs = refs[2 + count : 7 + count], refs[7 + count :]
+    owner_ref, targets, keeps_ref, scales_ref = refs[0], refs[1 : 1 + count], *refs[1 + count : 3 + count]
+    page_ref, length_ref, sems = refs[3 + count :]
+    stacked = [keeps_ref.at[i] for i in range(2)] + [scales_ref.at[i] for i in range(3)]
     moves = copies(
-        ((page_hbm, page_ref), (length_hbm, length_ref), *zip(sources, targets)), sems
+        (
+            (page_hbm, page_ref),
+            (length_hbm, length_ref),
+            *zip(sources, targets),
+            *zip(lists, stacked),
+        ),
+        sems,
     )
     for move in moves:
         move.start()
     moves[0].wait()
     moves[1].wait()
-    spots = bias_ref.shape[1]
-    page = spots // sources[0].shape[1]
-    spot = lax.broadcasted_iota(jnp.int32, (1, spots), 1)
-    page_of, offset = spot // page, spot % page
-    for r in range(bias_ref.shape[0]):
-        place = jnp.full((1, spots), 1 << 20, jnp.int32)
+    page = sources[0].shape[2]
+    offset = lax.broadcasted_iota(jnp.int32, (page, HD), 0)
+    for r in range(page_ref.shape[0]):
         for i in range(page_ref.shape[1]):
-            place = jnp.where(page_of == page_ref[r, i], i * page, place)
-        bias_ref[r : r + 1, :] = jnp.where(place + offset < length_ref[r], 0.0, DEAD)
+            places = pl.ds(pl.multiple_of(page_ref[r, i] * page, page), page)
+            owner_ref[places, :] = jnp.where(offset < length_ref[r] - i * page, float(r), -1.0)
     for move in moves[2:]:
         move.wait()
 
@@ -167,37 +177,51 @@
 
 
 def feed_kernel(
-    keep_ref, gate_scale_ref, up_scale_ref, down_keep_ref, down_scale_ref,
-    near_ref, far_ref, gate_ref, up_ref, down_ref, stay_ref, send_ref, hidden, total,
+    keeps_ref, scales_ref, near_ref, far_ref, gate_ref, up_ref, down_ref,
+    stay_ref, send_ref, far_total,
 ):
-    columns, keep = keep_ref.shape
+    _, columns, keep = keeps_ref.shape
     half = near_ref.shape[0]
-    total[...] = jnp.zeros_like(total)
-
+    stay_ref[...] = jnp.zeros_like(stay_ref)
+    far_total[...] = jnp.zeros_like(far_total)
+
+    def block(which, c, k):
+        return pl.ds(pl.multiple_of(keeps_ref[which, c, k] * BLK, BLK), BLK)
+
+    hidden = []
     for c in range(columns):
         gate_sum = jnp.zeros((2 * half, BLK), jnp.float32)
         up_sum = jnp.zeros((2 * half, BLK), jnp.float32)
         for k in range(keep):
-            where = pl.ds(pl.multiple_of(keep_ref[c, k] * BLK, BLK), BLK)
+            where = block(0, c, k)
             picked = jnp.concatenate([near_ref[:, where], far_ref[:, where]], axis=0)
             both = jnp.dot(
                 picked, jnp.concatenate([gate_ref[c, k], up_ref[c, k]], axis=1),
                 preferred_element_type=jnp.float32,
             )
-            gate_sum += gate_scale_ref[c, k] * both[:, :BLK]
-            up_sum += up_scale_ref[c, k] * both[:, BLK:]
-        hidden[c] = (gate_sum / (1.0 + jnp.exp(-gate_sum)) * up_sum).astype(jnp.bfloat16)
+            gate_sum += scales_ref[0, c, k] * both[:, :BLK]
+            up_sum += scales_ref[1, c, k] * both[:, BLK:]
+        hidden.append((gate_sum / (1.0 + jnp.exp(-gate_sum)) * up_sum).astype(jnp.bfloat16))
     for c in range(columns):
-        for k in range(0, keep, 2):
-            both = jnp.dot(
-                hidden[c], jnp.concatenate([down_ref[c, k], down_ref[c, k + 1]], axis=1),
-                preferred_element_type=jnp.float32,
-            )
-            for j in range(2):
-                where = pl.ds(pl.multiple_of(down_keep_ref[c, k + j] * BLK, BLK), BLK)
-                total[:, where] += down_scale_ref[c, k + j] * both[:, j * BLK : (j + 1) * BLK]
-    stay_ref[...] = total[:half, :]
-    send_ref[...] = total[half:, :].astype(jnp.bfloat16)
+        for start in range(0, keep, GROUP):
+            group = range(start, start + GROUP)
+            places = [block(1, c, k) for k in group]
+            near_sums = [stay_ref[:, where] for where in places]
+            far_sums = [far_total[:, where] for where in places]
+            for i in range(0, GROUP, 2):
+                both = jnp.dot(
+                    hidden[c],
+                    jnp.concatenate([down_ref[c, group[i]], down_ref[c, group[i + 1]]], axis=1),
+                    preferred_element_type=jnp.float32,
+                )
+                for j in range(2):
+                    term = scales_ref[2, c, group[i + j]] * both[:, j * BLK : (j + 1) * BLK]
+                    near_sums[i + j] += term[:half]
+                    far_sums[i + j] += term[half:]
+            for where, near_sum, far_sum in zip(places, near_sums, far_sums):
+                stay_ref[:, where] = near_sum
+                far_total[:, where] = far_sum
+    send_ref[...] = far_total[...].astype(jnp.bfloat16)
 
 
 def join_kernel(*refs):
@@ -260,22 +284,27 @@
     following = lax.ppermute(own, "wide", [(i, i - 1) for i in range(1, wide)])
 
     stored = [pool_pages, residual, norm_gain.reshape(1, model)]
-    stored += [gate_up_keep, gate_scale, up_scale, down_keep, down_scale]
+    lists = [gate_up_keep, down_keep, gate_scale, up_scale, down_scale]
     spots = pool_pages.shape[1] * pool_pages.shape[2]
-    bias, pool, residual, gain, *lists = pl.pallas_call(
+    owner, pool, residual, gain, keeps, scales = pl.pallas_call(
         functools.partial(prepare_kernel, len(stored)),
-        out_shape=(jax.ShapeDtypeStruct((rows, spots), f32), *[like(a) for a in stored]),
-        in_specs=[HBM] * (2 + len(stored)),
-        out_specs=(VMEM,) * (1 + len(stored)),
+        out_shape=(
+            jax.ShapeDtypeStruct((spots, HD), f32),
+            *[like(a) for a in stored],
+            jax.ShapeDtypeStruct((2, *gate_up_keep.shape), jnp.int32),
+            jax.ShapeDtypeStruct((3, *gate_scale.shape), f32),
+        ),
+        in_specs=[HBM] * (2 + len(stored) + len(lists)),
+        out_specs=(VMEM,) * (3 + len(stored)),
         scratch_shapes=[
             pltpu.SMEM(page_table.shape, jnp.int32),
             pltpu.SMEM(tail_length.shape, jnp.int32),
-            pltpu.SemaphoreType.DMA((2 + len(stored),)),
+            pltpu.SemaphoreType.DMA((2 + len(stored) + len(lists),)),
         ],
         compiler_params=pltpu.CompilerParams(vmem_limit_bytes=2 * MIB),
         cost_estimate=pl.CostEstimate(flops=0, bytes_accessed=8 * MIB, transcendentals=0),
         name="prepare",
-    )(*in_hbm([page_table, tail_length, *stored]))
+    )(*in_hbm([page_table, tail_length, *stored, *lists]))
 
     def attended(packed, shift, *after):
         return pl.pallas_call(
@@ -285,7 +314,7 @@
             out_specs=VMEM,
             compiler_params=pltpu.CompilerParams(vmem_limit_bytes=6 * MIB),
             name="attend",
-        )(packed, pool, bias, *after)
+        )(packed, pool, owner, *after)
 
     ahead = attended(following, rows)
     behind = lax.ppermute(ahead, "wide", [(i, i + 1) for i in range(wide - 1)])
@@ -334,17 +363,12 @@
             jax.ShapeDtypeStruct((half, model), f32),
             jax.ShapeDtypeStruct((half, model), bf16),
         ),
-        in_specs=[SMEM] * 5 + [VMEM] * 5,
+        in_specs=[SMEM] * 2 + [VMEM] * 5,
         out_specs=(VMEM,) * 2,
-        scratch_shapes=[
-            pltpu.VMEM((columns, 2 * half, BLK), bf16),
-            pltpu.VMEM((2 * half, model), f32),
-        ],
-        compiler_params=pltpu.CompilerParams(
-            vmem_limit_bytes=2 * half * model * 4 + half * model * 6 + 4 * MIB
-        ),
+        scratch_shapes=[pltpu.VMEM((half, model), f32)],
+        compiler_params=pltpu.CompilerParams(vmem_limit_bytes=half * model * 10 + 6 * MIB),
         name="feed",
-    )(*lists, gathered, far, gate_blocks, up_blocks, down_blocks)
+    )(keeps, scales, gathered, far, gate_blocks, up_blocks, down_blocks)
 
     total = kept + swapped(sent, bits[0]).astype(f32)
     for stage in stages[1:]:

time: 51.9 us -> 50.5 us (0.973)
  Pallas kernels: 11.8 us -> 10.1 us
    pallas_call x2, Pallas kernels: 3.5 us -> 2.6 us  [attended(): pl.pallas_call(functools.partial(attend_kernel, groups, per_group, shift)...]
    pallas_call x1, Pallas kernels: 5.51 us -> 4.63 us  [per_device(): pl.pallas_call(feed_kernel, out_shape=(jax.ShapeDtypeStruct((half, model)...]
  transfers between devices with their start and end apart: 14 -> 14, of which waited for: 11 -> 10; matrix products, arithmetic and copies ran while one was open for 0% -> 0% of each run, Pallas kernels for 7% -> 6%
where the time goes in v5:
time: 50.5 us; the launch traced here: 50.3 us
  starting transfers between devices  22.5 us (45%)
  waiting for transfers between devices  16.1 us (32%)
  Pallas kernels  10.1 us (20%)
  other arithmetic  0.77 us (2%)
  local copies, waits for them, and re-layouts  0.63 us (1%)
    ppermute x10, starting transfers between devices, swapped(): lax.ppermute(block, 'wide', [(i, i ^ bits) for i in range(lax.axis_size('...  14.2 us
    ppermute x10, waiting for transfers between devices, swapped(): lax.ppermute(block, 'wide', [(i, i ^ bits) for i in range(lax.axis_size('...  12 us
    ppermute x1, starting transfers between devices, per_device(): behind = lax.ppermute(ahead, 'wide', [(i, i + 1) for i in range(wide - 1)])  5.44 us
    pallas_call x1, Pallas kernels, per_device(): pl.pallas_call(feed_kernel, out_shape=(jax.ShapeDtypeStruct((half, model)...  4.63 us
    ppermute x1, waiting for transfers between devices, per_device(): lax.ppermute(cross, ('wide', 'head'), [(i * heads + h, (i ^ high) * heads...  3.99 us
    pallas_call x2, Pallas kernels, attended(): pl.pallas_call(functools.partial(attend_kernel, groups, per_group, shift)...  2.6 us
    pallas_call x1, Pallas kernels, per_device(): pl.pallas_call(functools.partial(prepare_kernel, len(stored)), out_shape=...  1.7 us
    ppermute x1, starting transfers between devices, per_device(): following = lax.ppermute(own, 'wide', [(i, i - 1) for i in range(1, wide)])  1.29 us
  transfers between devices with their start and end apart: 14, of which 10 were waited for; matrix products, arithmetic and copies ran while one was open for 0% of the time, Pallas kernels for 6%

profile of v5, /device:TPU:0, one launch (start us, length us, event | category | flops | bytes accessed | tf_op | source)
XLA Modules:
  0.0 50.3 jit_solution(16616263987134792709)
XLA Ops:
  0.0 0.8 %pack.1.packed_ref = bf16[4,5248]{1,0:T(4,128)(2,1)S(1)} custom-call(bf16[4,4096]{1,0:T(4,128)(2,1)} %query_hbm.1, bf16[4,512]{1,0:T(4,128)(2,1)} %key_hbm.1, bf16[4,512]{1,0:T(4,128)(2,1)} %value_hbm.1, s32[4]{0:T(128)} %parent_hbm.1), custom_call_target="tpu_custom_call" | custom-call | tf_op jit(solution)/shard_map/pack/pallas_call | solution.py:272
  0.8 1.3 %collective-permute-start = (bf16[4,5248]{1,0:T(4,128)(2,1)S(1)}, bf16[4,5248]{1,0:T(4,128)(2,1)S(1)}, u32[]{:S(2)}, u32[]{:S(2)}) collective-permute-start(bf16[4,5248]{1,0:T(4,128)(2,1)S(1)} %pack.1.packed_ref), channel_id=1, source_target_pairs={{2,0},{4,2},{6,4},{8,6},{10,8},{12,10},{14,12},{16,14},{18,16},{20... | collective-permute-start | bytes 125960 | tf_op jit(solution)/shard_map/ppermute | solution.py:284
  2.1 1.7 %prepare.1 = (f32[1024,128]{1,0:T(8,128)S(1)}, bf16[2,64,16,512]{3,2,1,0:T(8,128)(2,1)S(1)}, bf16[2,8192]{1,0:T(2,128)(2,1)S(1)}, f32[1,8192]{1,0:T(1,128)S(1)},...) custom-call(s32[4,16]{1,0:T(4,128)} %refs_0_.1, s32[4]{0:T(128)} %refs_1_.1, bf16[2,64,16,512]{3,2,1,0:T(8,128)(2,1)} %refs_2_.1, ...), custom_call_target="tpu_custom_call" | custom-call | bytes 8388608 | tf_op jit(solution)/shard_map/prepare/pallas_call | solution.py:289
  3.8 0.1 collective-permute-done.packed_ref
  3.9 1.3 %attend.2.refs_0_ = bf16[4,4096]{1,0:T(4,128)(2,1)S(1)} custom-call(bf16[4,5248]{1,0:T(4,128)(2,1)S(1)} %collective-permute-done.packed_ref, bf16[2,64,16,512]{3,2,1,0:T(8,128)(2,1)S(1)} %get-tuple-element.17.pool_ref, f32[1024,128]{1,0:T(8,128)S(1)} %get-tuple-element.18.owner_ref), custom_call_target="tpu_custom_call" | custom-call | tf_op jit(solution)/shard_map/attend/pallas_call | solution.py:310
  5.2 5.4 %collective-permute-start.1 = (bf16[4,4096]{1,0:T(4,128)(2,1)S(1)}, bf16[4,4096]{1,0:T(4,128)(2,1)S(1)}, u32[]{:S(2)}, u32[]{:S(2)}) collective-permute-start(bf16[4,4096]{1,0:T(4,128)(2,1)S(1)} %attend.2.refs_0_), channel_id=1, source_target_pairs={{0,2},{2,4},{4,6},{6,8},{8,10},{10,12},{12,14},{14,16},{16,18},{18... | collective-permute-start | bytes 98312 | tf_op jit(solution)/shard_map/ppermute | solution.py:320
  10.7 1.3 %attend.3.own_ref = bf16[4,4096]{1,0:T(4,128)(2,1)S(1)} custom-call(bf16[4,5248]{1,0:T(4,128)(2,1)S(1)} %pack.1.packed_ref, bf16[2,64,16,512]{3,2,1,0:T(8,128)(2,1)S(1)} %get-tuple-element.17.pool_ref, f32[1024,128]{1,0:T(8,128)S(1)} %get-tuple-element.18.owner_ref, bf16[4,4096]{1,0:T(4,128)(2,1)S(1)} %attend.2.refs_0_), custom_call_target="tpu_custom_call" | custom-call | tf_op jit(solution)/shard_map/attend/pallas_call | solution.py:310
  12.0 0.0 collective-permute-done.1.behind_ref
  12.0 4.8 %collective-permute-start.3 = (bf16[2,12288]{1,0:T(2,128)(2,1)S(1)}, bf16[2,12288]{1,0:T(2,128)(2,1)S(1)}, u32[]{:S(2)}, u32[]{:S(2)}) collective-permute-start(bf16[2,12288]{1,0:T(2,128)(2,1)S(1)} %get-tuple-element.20.stay_ref), channel_id=1, source_target_pairs={{0,16},{2,18},{4,20},{6,22},{8,24},{10,26},{12,28},{14,30},{16,0},... | collective-permute-start | bytes 147464 | tf_op jit(solution)/shard_map/ppermute | solution.py:248
  16.8 1.0 %collective-permute-start.4 = (bf16[2,4096]{1,0:T(2,128)(2,1)S(1)}, bf16[2,4096]{1,0:T(2,128)(2,1)S(1)}, u32[]{:S(2)}, u32[]{:S(2)}) collective-permute-start(bf16[2,4096]{1,0:T(2,128)(2,1)S(1)} %get-tuple-element.21), channel_id=1, source_target_pairs={{0,17},{1,16},{2,19},{3,18},{4,21},{5,20},{6,23},{7,22},{8,25},{9,... | collective-permute-start | bytes 49160 | tf_op jit(solution)/shard_map/ppermute | solution.py:336
  17.9 0.5 %collective-permute-start.2 = (bf16[2,4096]{1,0:T(2,128)(2,1)S(1)}, bf16[2,4096]{1,0:T(2,128)(2,1)S(1)}, u32[]{:S(2)}, u32[]{:S(2)}) collective-permute-start(bf16[2,4096]{1,0:T(2,128)(2,1)S(1)} %get-tuple-element.21), channel_id=1, source_target_pairs={{0,1},{1,0},{2,3},{3,2},{4,5},{5,4},{6,7},{7,6},{8,9},{9,8},{10,11... | collective-permute-start | bytes 49160 | tf_op jit(solution)/shard_map/ppermute | solution.py:342
  18.4 4.0 %collective-permute-done.4.far_cross_ref = bf16[2,4096]{1,0:T(2,128)(2,1)S(1)} collective-permute-done((bf16[2,4096]{1,0:T(2,128)(2,1)S(1)}, bf16[2,4096]{1,0:T(2,128)(2,1)S(1)}, u32[]{:S(2)}, u32[]{:S(2)}) %collective-permute-start.4) | collective-permute-done | bytes 16416 | tf_op jit(solution)/shard_map/ppermute | solution.py:336
  22.4 0.0 collective-permute-done.2.cross_ref
  22.4 0.0 collective-permute-done.3.far_stay_ref
  22.4 0.2 norm.1
  22.6 0.0 slice-start
  22.6 0.0 slice-start.2
  22.6 0.0 slice-start.4
  22.7 0.0 slice-start.1
  22.7 0.0 slice-start.3
  22.7 0.0 slice-start.5
  22.7 1.0 %collective-permute-start.7 = (bf16[4,8192]{1,0:T(4,128)(2,1)S(1)}, bf16[4,8192]{1,0:T(4,128)(2,1)S(1)}, u32[]{:S(2)}, u32[]{:S(2)}) collective-permute-start(bf16[4,8192]{1,0:T(4,128)(2,1)S(1)} %get-tuple-element.26.refs_0_), channel_id=1, source_target_pairs={{0,12},{2,14},{4,8},{6,10},{8,4},{10,6},{12,0},{14,2},{16,28},{18,... | collective-permute-start | bytes 196616 | tf_op jit(solution)/shard_map/ppermute | solution.py:248
  23.6 0.8 %collective-permute-start.6 = (bf16[4,8192]{1,0:T(4,128)(2,1)S(1)}, bf16[4,8192]{1,0:T(4,128)(2,1)S(1)}, u32[]{:S(2)}, u32[]{:S(2)}) collective-permute-start(bf16[4,8192]{1,0:T(4,128)(2,1)S(1)} %get-tuple-element.26.refs_0_), channel_id=1, source_target_pairs={{0,8},{2,10},{4,12},{6,14},{8,0},{10,2},{12,4},{14,6},{16,24},{18,... | collective-permute-start | bytes 196616 | tf_op jit(solution)/shard_map/ppermute | solution.py:248
  24.4 1.8 %collective-permute-start.5 = (bf16[4,8192]{1,0:T(4,128)(2,1)S(1)}, bf16[4,8192]{1,0:T(4,128)(2,1)S(1)}, u32[]{:S(2)}, u32[]{:S(2)}) collective-permute-start(bf16[4,8192]{1,0:T(4,128)(2,1)S(1)} %get-tuple-element.26.refs_0_), channel_id=1, source_target_pairs={{0,4},{2,6},{4,0},{6,2},{8,12},{10,14},{12,8},{14,10},{16,20},{18,... | collective-permute-start | bytes 196616 | tf_op jit(solution)/shard_map/ppermute | solution.py:248
  26.2 1.7 %collective-permute-done.7.refs_3_ = bf16[4,8192]{1,0:T(4,128)(2,1)S(1)} collective-permute-done((bf16[4,8192]{1,0:T(4,128)(2,1)S(1)}, bf16[4,8192]{1,0:T(4,128)(2,1)S(1)}, u32[]{:S(2)}, u32[]{:S(2)}) %collective-permute-start.7) | collective-permute-done | bytes 65568 | tf_op jit(solution)/shard_map/ppermute | solution.py:248
  27.9 0.0 collective-permute-done.6.refs_2_
  27.9 0.8 %collective-permute-done.5.refs_1_ = bf16[4,8192]{1,0:T(4,128)(2,1)S(1)} collective-permute-done((bf16[4,8192]{1,0:T(4,128)(2,1)S(1)}, bf16[4,8192]{1,0:T(4,128)(2,1)S(1)}, u32[]{:S(2)}, u32[]{:S(2)}) %collective-permute-start.5) | collective-permute-done | bytes 65568 | tf_op jit(solution)/shard_map/ppermute | solution.py:248
  28.7 0.1 join.1.near_ref
  28.8 0.1 collective-permute-start.8
  28.8 1.5 %collective-permute-done.8.far_ref = bf16[16,8192]{1,0:T(8,128)(2,1)S(1)} collective-permute-done((bf16[16,8192]{1,0:T(8,128)(2,1)S(1)}, bf16[16,8192]{1,0:T(8,128)(2,1)S(1)}, u32[]{:S(2)}, u32[]{:S(2)}) %collective-permute-start.8) | collective-permute-done | bytes 262176 | tf_op jit(solution)/shard_map/ppermute | solution.py:248
  30.4 0.0 slice-done
  30.4 0.0 slice-done.2
  30.4 0.0 slice-done.4
  30.4 0.0 slice-done.1
  30.4 0.0 slice-done.3
  30.4 0.5 slice-done.5
  30.9 4.6 %feed.1 = (f32[16,8192]{1,0:T(8,128)S(1)}, bf16[16,8192]{1,0:T(8,128)(2,1)S(1)}) custom-call(s32[2,8,32]{2,1,0:T(8,128)S(1)} %get-tuple-element.24.keeps_ref, f32[3,8,32]{2,1,0:T(8,128)S(1)} %get-tuple-element.25.scales_ref, bf16[16,8192]{1,0:T(8,128)(2,1)S(1)} %join.1.near_ref, bf16[16,8192]{1,0:T(8,128)(2,1)S(1)} %collective-permute-done.8.far_ref, ...), custom_call_target="tpu_custom_call" | custom-call | tf_op jit(solution)/shard_map/feed/pallas_call | solution.py:360
  35.5 0.1 collective-permute-start.9
  35.6 1.5 %collective-permute-done.9 = bf16[16,8192]{1,0:T(8,128)(2,1)S(1)} collective-permute-done((bf16[16,8192]{1,0:T(8,128)(2,1)S(1)}, bf16[16,8192]{1,0:T(8,128)(2,1)S(1)}, u32[]{:S(2)}, u32[]{:S(2)}) %collective-permute-start.9) | collective-permute-done | bytes 262176 | tf_op jit(solution)/shard_map/ppermute | solution.py:248
  37.1 0.1 fusion.4
  37.2 0.1 fusion.5
  37.3 1.4 %collective-permute-start.10 = (bf16[4,8192]{1,0:T(4,128)(2,1)S(1)}, bf16[4,8192]{1,0:T(4,128)(2,1)S(1)}, u32[]{:S(2)}, u32[]{:S(2)}) collective-permute-start(bf16[4,8192]{1,0:T(4,128)(2,1)S(1)} %get-tuple-element.31), channel_id=1, source_target_pairs={{0,4},{2,6},{4,0},{6,2},{8,12},{10,14},{12,8},{14,10},{16,20},{18,... | collective-permute-start | bytes 196616 | tf_op jit(solution)/shard_map/ppermute | solution.py:248
  38.7 1.7 %collective-permute-start.12 = (bf16[4,8192]{1,0:T(4,128)(2,1)S(1)}, bf16[4,8192]{1,0:T(4,128)(2,1)S(1)}, u32[]{:S(2)}, u32[]{:S(2)}) collective-permute-start(bf16[4,8192]{1,0:T(4,128)(2,1)S(1)} %get-tuple-element.32), channel_id=1, source_target_pairs={{0,12},{2,14},{4,8},{6,10},{8,4},{10,6},{12,0},{14,2},{16,28},{18,... | collective-permute-start | bytes 196616 | tf_op jit(solution)/shard_map/ppermute | solution.py:248
  40.4 0.5 collective-permute-start.11
  40.8 0.8 %collective-permute-done.10 = bf16[4,8192]{1,0:T(4,128)(2,1)S(1)} collective-permute-done((bf16[4,8192]{1,0:T(4,128)(2,1)S(1)}, bf16[4,8192]{1,0:T(4,128)(2,1)S(1)}, u32[]{:S(2)}, u32[]{:S(2)}) %collective-permute-start.10) | collective-permute-done | bytes 65568 | tf_op jit(solution)/shard_map/ppermute | solution.py:248
  41.6 2.8 %collective-permute-done.12 = bf16[4,8192]{1,0:T(4,128)(2,1)S(1)} collective-permute-done((bf16[4,8192]{1,0:T(4,128)(2,1)S(1)}, bf16[4,8192]{1,0:T(4,128)(2,1)S(1)}, u32[]{:S(2)}, u32[]{:S(2)}) %collective-permute-start.12) | collective-permute-done | bytes 65568 | tf_op jit(solution)/shard_map/ppermute | solution.py:248
  44.4 0.3 collective-permute-done.11
  44.6 0.1 fusion.1
  44.7 2.1 %collective-permute-start.13 = (bf16[2,8192]{1,0:T(2,128)(2,1)S(1)}, bf16[2,8192]{1,0:T(2,128)(2,1)S(1)}, u32[]{:S(2)}, u32[]{:S(2)}) collective-permute-start(bf16[2,8192]{1,0:T(2,128)(2,1)S(1)} %slice.47), channel_id=1, source_target_pairs={{0,16},{2,18},{4,20},{6,22},{8,24},{10,26},{12,28},{14,30},{16,0},... | collective-permute-start | bytes 98312 | tf_op jit(solution)/shard_map/ppermute | solution.py:248
  46.9 2.7 %collective-permute-done.13 = bf16[2,8192]{1,0:T(2,128)(2,1)S(1)} collective-permute-done((bf16[2,8192]{1,0:T(2,128)(2,1)S(1)}, bf16[2,8192]{1,0:T(2,128)(2,1)S(1)}, u32[]{:S(2)}, u32[]{:S(2)}) %collective-permute-start.13) | collective-permute-done | bytes 32800 | tf_op jit(solution)/shard_map/ppermute | solution.py:248
  49.6 0.7 %fusion.3 = bf16[2,8192]{1,0:T(2,128)(2,1)} fusion(f32[2,8192]{1,0:T(2,128)S(1)} %get-tuple-element.23, f32[4,8192]{1,0:T(4,128)S(1)} %fusion.1, bf16[2,8192]{1,0:T(2,128)(2,1)S(1)} %collective-permute-done.13), kind=kLoop, calls=%fused_computation.7 | loop fusion | flops 65536 | bytes 196608 | tf_op jit(solution)/shard_map/convert_element_type | solution.py:380
  (5 shorter events, 0.1 us)
Async XLA Ops:
  0.8 3.1 %collective-permute-start = (bf16[4,5248]{1,0:T(4,128)(2,1)S(1)}, bf16[4,5248]{1,0:T(4,128)(2,1)S(1)}, u32[]{:S(2)}, u32[]{:S(2)}) collective-permute-start(bf16[4,5248]{1,0:T(4,128)(2,1)S(1)} %pack.1.packed_ref), channel_id=1, source_target_pairs={{2,0},{4,2},{6,4},{8,6},{10,8},{12,10},{14,12},{16,14},{18,16},{20... | collective-permute-start | bytes 125960 | tf_op jit(solution)/shard_map/ppermute | solution.py:284
  5.2 6.8 %collective-permute-start.1 = (bf16[4,4096]{1,0:T(4,128)(2,1)S(1)}, bf16[4,4096]{1,0:T(4,128)(2,1)S(1)}, u32[]{:S(2)}, u32[]{:S(2)}) collective-permute-start(bf16[4,4096]{1,0:T(4,128)(2,1)S(1)} %attend.2.refs_0_), channel_id=1, source_target_pairs={{0,2},{2,4},{4,6},{6,8},{8,10},{10,12},{12,14},{14,16},{16,18},{18... | collective-permute-start | bytes 98312 | tf_op jit(solution)/shard_map/ppermute | solution.py:320
  12.0 10.3 %collective-permute-start.3 = (bf16[2,12288]{1,0:T(2,128)(2,1)S(1)}, bf16[2,12288]{1,0:T(2,128)(2,1)S(1)}, u32[]{:S(2)}, u32[]{:S(2)}) collective-permute-start(bf16[2,12288]{1,0:T(2,128)(2,1)S(1)} %get-tuple-element.20.stay_ref), channel_id=1, source_target_pairs={{0,16},{2,18},{4,20},{6,22},{8,24},{10,26},{12,28},{14,30},{16,0},... | collective-permute-start | bytes 147464 | tf_op jit(solution)/shard_map/ppermute | solution.py:248
  16.8 5.5 %collective-permute-start.4 = (bf16[2,4096]{1,0:T(2,128)(2,1)S(1)}, bf16[2,4096]{1,0:T(2,128)(2,1)S(1)}, u32[]{:S(2)}, u32[]{:S(2)}) collective-permute-start(bf16[2,4096]{1,0:T(2,128)(2,1)S(1)} %get-tuple-element.21), channel_id=1, source_target_pairs={{0,17},{1,16},{2,19},{3,18},{4,21},{5,20},{6,23},{7,22},{8,25},{9,... | collective-permute-start | bytes 49160 | tf_op jit(solution)/shard_map/ppermute | solution.py:336
  17.9 4.5 %collective-permute-start.2 = (bf16[2,4096]{1,0:T(2,128)(2,1)S(1)}, bf16[2,4096]{1,0:T(2,128)(2,1)S(1)}, u32[]{:S(2)}, u32[]{:S(2)}) collective-permute-start(bf16[2,4096]{1,0:T(2,128)(2,1)S(1)} %get-tuple-element.21), channel_id=1, source_target_pairs={{0,1},{1,0},{2,3},{3,2},{4,5},{5,4},{6,7},{7,6},{8,9},{9,8},{10,11... | collective-permute-start | bytes 49160 | tf_op jit(solution)/shard_map/ppermute | solution.py:342
  22.6 7.7 %slice-start = ((s8[8388608]{0:T(1024)(128)(4,1)}), s8[4194304]{0:T(1024)(128)(4,1)S(1)}, s32[]{:S(2)}) async-start(s8[8388608]{0:T(1024)(128)(4,1)} %bitcast.1), calls=%async_computation | async-start | bytes 8388608
  22.6 7.7 %slice-start.2 = ((s8[8388608]{0:T(1024)(128)(4,1)}), s8[4194304]{0:T(1024)(128)(4,1)S(1)}, s32[]{:S(2)}) async-start(s8[8388608]{0:T(1024)(128)(4,1)} %bitcast.3), calls=%async_computation.2 | async-start | bytes 8388608
  22.6 7.7 %slice-start.4 = ((s8[8388608]{0:T(1024)(128)(4,1)}), s8[4194304]{0:T(1024)(128)(4,1)S(1)}, s32[]{:S(2)}) async-start(s8[8388608]{0:T(1024)(128)(4,1)} %bitcast.5), calls=%async_computation.4 | async-start | bytes 8388608
  22.7 7.7 %slice-start.1 = ((s8[8388608]{0:T(1024)(128)(4,1)}), s8[4194304]{0:T(1024)(128)(4,1)S(1)}, s32[]{:S(2)}) async-start(s8[8388608]{0:T(1024)(128)(4,1)} %bitcast.1), calls=%async_computation.1 | async-start | bytes 8388608
  22.7 7.7 %slice-start.3 = ((s8[8388608]{0:T(1024)(128)(4,1)}), s8[4194304]{0:T(1024)(128)(4,1)S(1)}, s32[]{:S(2)}) async-start(s8[8388608]{0:T(1024)(128)(4,1)} %bitcast.3), calls=%async_computation.3 | async-start | bytes 8388608
  22.7 8.2 %slice-start.5 = ((s8[8388608]{0:T(1024)(128)(4,1)}), s8[4194304]{0:T(1024)(128)(4,1)S(1)}, s32[]{:S(2)}) async-start(s8[8388608]{0:T(1024)(128)(4,1)} %bitcast.5), calls=%async_computation.5 | async-start | bytes 8388608
  22.7 5.2 %collective-permute-start.7 = (bf16[4,8192]{1,0:T(4,128)(2,1)S(1)}, bf16[4,8192]{1,0:T(4,128)(2,1)S(1)}, u32[]{:S(2)}, u32[]{:S(2)}) collective-permute-start(bf16[4,8192]{1,0:T(4,128)(2,1)S(1)} %get-tuple-element.26.refs_0_), channel_id=1, source_target_pairs={{0,12},{2,14},{4,8},{6,10},{8,4},{10,6},{12,0},{14,2},{16,28},{18,... | collective-permute-start | bytes 196616 | tf_op jit(solution)/shard_map/ppermute | solution.py:248
  23.6 4.3 %collective-permute-start.6 = (bf16[4,8192]{1,0:T(4,128)(2,1)S(1)}, bf16[4,8192]{1,0:T(4,128)(2,1)S(1)}, u32[]{:S(2)}, u32[]{:S(2)}) collective-permute-start(bf16[4,8192]{1,0:T(4,128)(2,1)S(1)} %get-tuple-element.26.refs_0_), channel_id=1, source_target_pairs={{0,8},{2,10},{4,12},{6,14},{8,0},{10,2},{12,4},{14,6},{16,24},{18,... | collective-permute-start | bytes 196616 | tf_op jit(solution)/shard_map/ppermute | solution.py:248
  24.4 4.3 %collective-permute-start.5 = (bf16[4,8192]{1,0:T(4,128)(2,1)S(1)}, bf16[4,8192]{1,0:T(4,128)(2,1)S(1)}, u32[]{:S(2)}, u32[]{:S(2)}) collective-permute-start(bf16[4,8192]{1,0:T(4,128)(2,1)S(1)} %get-tuple-element.26.refs_0_), channel_id=1, source_target_pairs={{0,4},{2,6},{4,0},{6,2},{8,12},{10,14},{12,8},{14,10},{16,20},{18,... | collective-permute-start | bytes 196616 | tf_op jit(solution)/shard_map/ppermute | solution.py:248
  28.8 1.6 %collective-permute-start.8 = (bf16[16,8192]{1,0:T(8,128)(2,1)S(1)}, bf16[16,8192]{1,0:T(8,128)(2,1)S(1)}, u32[]{:S(2)}, u32[]{:S(2)}) collective-permute-start(bf16[16,8192]{1,0:T(8,128)(2,1)S(1)} %join.1.near_ref), channel_id=1, source_target_pairs={{0,2},{2,0},{4,6},{6,4},{8,10},{10,8},{12,14},{14,12},{16,18},{18,... | collective-permute-start | bytes 786440 | tf_op jit(solution)/shard_map/ppermute | solution.py:248
  35.5 1.6 %collective-permute-start.9 = (bf16[16,8192]{1,0:T(8,128)(2,1)S(1)}, bf16[16,8192]{1,0:T(8,128)(2,1)S(1)}, u32[]{:S(2)}, u32[]{:S(2)}) collective-permute-start(bf16[16,8192]{1,0:T(8,128)(2,1)S(1)} %get-tuple-element.28), channel_id=1, source_target_pairs={{0,2},{2,0},{4,6},{6,4},{8,10},{10,8},{12,14},{14,12},{16,18},{18,... | collective-permute-start | bytes 786440 | tf_op jit(solution)/shard_map/ppermute | solution.py:248
  37.3 4.3 %collective-permute-start.10 = (bf16[4,8192]{1,0:T(4,128)(2,1)S(1)}, bf16[4,8192]{1,0:T(4,128)(2,1)S(1)}, u32[]{:S(2)}, u32[]{:S(2)}) collective-permute-start(bf16[4,8192]{1,0:T(4,128)(2,1)S(1)} %get-tuple-element.31), channel_id=1, source_target_pairs={{0,4},{2,6},{4,0},{6,2},{8,12},{10,14},{12,8},{14,10},{16,20},{18,... | collective-permute-start | bytes 196616 | tf_op jit(solution)/shard_map/ppermute | solution.py:248
  38.7 5.7 %collective-permute-start.12 = (bf16[4,8192]{1,0:T(4,128)(2,1)S(1)}, bf16[4,8192]{1,0:T(4,128)(2,1)S(1)}, u32[]{:S(2)}, u32[]{:S(2)}) collective-permute-start(bf16[4,8192]{1,0:T(4,128)(2,1)S(1)} %get-tuple-element.32), channel_id=1, source_target_pairs={{0,12},{2,14},{4,8},{6,10},{8,4},{10,6},{12,0},{14,2},{16,28},{18,... | collective-permute-start | bytes 196616 | tf_op jit(solution)/shard_map/ppermute | solution.py:248
  40.4 4.3 %collective-permute-start.11 = (bf16[4,8192]{1,0:T(4,128)(2,1)S(1)}, bf16[4,8192]{1,0:T(4,128)(2,1)S(1)}, u32[]{:S(2)}, u32[]{:S(2)}) collective-permute-start(bf16[4,8192]{1,0:T(4,128)(2,1)S(1)} %get-tuple-element.33), channel_id=1, source_target_pairs={{0,8},{2,10},{4,12},{6,14},{8,0},{10,2},{12,4},{14,6},{16,24},{18,... | collective-permute-start | bytes 196616 | tf_op jit(solution)/shard_map/ppermute | solution.py:248
  44.7 4.9 %collective-permute-start.13 = (bf16[2,8192]{1,0:T(2,128)(2,1)S(1)}, bf16[2,8192]{1,0:T(2,128)(2,1)S(1)}, u32[]{:S(2)}, u32[]{:S(2)}) collective-permute-start(bf16[2,8192]{1,0:T(2,128)(2,1)S(1)} %slice.47), channel_id=1, source_target_pairs={{0,16},{2,18},{4,20},{6,22},{8,24},{10,26},{12,28},{14,30},{16,0},... | collective-permute-start | bytes 98312 | tf_op jit(solution)/shard_map/ppermute | solution.py:248

commit v6 on v5

--- a/solution.py
+++ b/solution.py
@@ -239,9 +239,35 @@
         in_specs=[VMEM] * len(blocks),
         out_specs=VMEM,
         compiler_params=pltpu.CompilerParams(vmem_limit_bytes=2 * MIB),
-        cost_estimate=WHILE_EXCHANGING,
         name="join",
     )(*blocks)
+
+
+def sum_kernel(count, kept_ref, *refs):
+    blocks, kept_out, sent = refs[:count], refs[count], refs[count + 1 :]
+    height = kept_out.shape[0]
+    for i, out_ref in enumerate((kept_out, *sent)):
+        rows = slice(i * height, (i + 1) * height)
+        total = kept_ref[rows, :]
+        for block in blocks:
+            total = total + block[rows, :].astype(jnp.float32)
+        out_ref[...] = total.astype(out_ref.dtype)
+
+
+def summed(kept, blocks, parts):
+    height, width = kept.shape
+    part = (height // parts, width)
+    return pl.pallas_call(
+        functools.partial(sum_kernel, len(blocks)),
+        out_shape=(
+            jax.ShapeDtypeStruct(part, jnp.float32),
+            *[jax.ShapeDtypeStruct(part, jnp.bfloat16)] * (parts - 1),
+        ),
+        in_specs=[VMEM] * (1 + len(blocks)),
+        out_specs=(VMEM,) * parts,
+        compiler_params=pltpu.CompilerParams(vmem_limit_bytes=2 * MIB),
+        name="sum",
+    )(kept, *blocks)
 
 
 def swapped(block, bits):
@@ -321,6 +347,7 @@
     mixed = attended(own, 0, ahead)
     bits = [1 << b for b in range(wide.bit_length() - 1)]
     stages = [(bits[0],), tuple(bits[1:3]), *[(bit,) for bit in bits[3:]]]
+    sum_stages = stages[1:]
     high = bits[-1]
     cross, stay = pl.pallas_call(
         merge_kernel,
@@ -331,6 +358,7 @@
         in_specs=[VMEM] * 3,
         out_specs=(VMEM,) * 2,
         compiler_params=pltpu.CompilerParams(vmem_limit_bytes=2 * MIB),
+        cost_estimate=WHILE_EXCHANGING,
         name="merge",
     )(mixed, behind, residual)
     far_cross = lax.ppermute(
@@ -349,7 +377,6 @@
         in_specs=[VMEM] * 5,
         out_specs=(VMEM,) * 2,
         compiler_params=pltpu.CompilerParams(vmem_limit_bytes=2 * MIB),
-        cost_estimate=WHILE_EXCHANGING,
         name="norm",
     )(stay, near_cross, far_stay, far_cross, gain)
     for stage in stages[-2:0:-1]:
@@ -370,14 +397,15 @@
         name="feed",
     )(keeps, scales, gathered, far, gate_blocks, up_blocks, down_blocks)
 
-    total = kept + swapped(sent, bits[0]).astype(f32)
-    for stage in stages[1:]:
-        half = half >> len(stage)
-        kept, sent = total[:half], total[half:].astype(bf16)
-        total = kept
-        for i, s in enumerate(combined(stage)):
-            total = total + swapped(sent[i * half : (i + 1) * half], s).astype(f32)
-    return (middle + total).astype(bf16)
+    blocks = [swapped(sent, bits[0])]
+    for stage in sum_stages:
+        sums = combined(stage)
+        kept, *sent = summed(kept, blocks, 1 + len(sums))
+        blocks = [swapped(block, s) for block, s in sorted(zip(sent, sums), key=lambda p: -bin(p[1]).count('1'))]
+    total = middle + kept
+    for block in blocks:
+        total = total + block.astype(f32)
+    return total.astype(bf16)
 
 
 def solution(mesh):

time: 50.5 us -> 49.9 us (0.988)
  local copies, waits for them, and re-layouts: 0.63 us -> 0.05 us
  transfers between devices with their start and end apart: 14 -> 14, of which waited for: 10 -> 11; matrix products, arithmetic and copies ran while one was open for 0% -> 0% of each run, Pallas kernels for 6% -> 6%
where the time goes in v6:
time: 49.9 us; the launch traced here: 49.6 us
  starting transfers between devices  22.5 us (45%)
  waiting for transfers between devices  16 us (32%)
  Pallas kernels  10.3 us (21%)
  other arithmetic  0.66 us (1%)
    ppermute x10, starting transfers between devices, swapped(): lax.ppermute(block, 'wide', [(i, i ^ bits) for i in range(lax.axis_size('...  14.2 us
    ppermute x10, waiting for transfers between devices, swapped(): lax.ppermute(block, 'wide', [(i, i ^ bits) for i in range(lax.axis_size('...  11.9 us
    ppermute x1, starting transfers between devices, per_device(): behind = lax.ppermute(ahead, 'wide', [(i, i + 1) for i in range(wide - 1)])  5.44 us
    pallas_call x1, Pallas kernels, per_device(): pl.pallas_call(feed_kernel, out_shape=(jax.ShapeDtypeStruct((half, model)...  4.64 us
    ppermute x1, waiting for transfers between devices, per_device(): lax.ppermute(cross, ('wide', 'head'), [(i * heads + h, (i ^ high) * heads...  3.99 us
    pallas_call x2, Pallas kernels, attended(): pl.pallas_call(functools.partial(attend_kernel, groups, per_group, shift)...  2.6 us
    pallas_call x1, Pallas kernels, per_device(): pl.pallas_call(functools.partial(prepare_kernel, len(stored)), out_shape=...  1.7 us
    ppermute x1, starting transfers between devices, per_device(): following = lax.ppermute(own, 'wide', [(i, i - 1) for i in range(1, wide)])  1.29 us
  transfers between devices with their start and end apart: 14, of which 11 were waited for; matrix products, arithmetic and copies ran while one was open for 0% of the time, Pallas kernels for 6%

profile of v6, /device:TPU:0, one launch (start us, length us, event | category | flops | bytes accessed | tf_op | source)
XLA Modules:
  0.0 49.6 jit_solution(411545024194606189)
XLA Ops:
  0.0 0.8 %pack.1.packed_ref = bf16[4,5248]{1,0:T(4,128)(2,1)S(1)} custom-call(bf16[4,4096]{1,0:T(4,128)(2,1)} %query_hbm.1, bf16[4,512]{1,0:T(4,128)(2,1)} %key_hbm.1, bf16[4,512]{1,0:T(4,128)(2,1)} %value_hbm.1, s32[4]{0:T(128)} %parent_hbm.1), custom_call_target="tpu_custom_call" | custom-call | tf_op jit(solution)/shard_map/pack/pallas_call | solution.py:298
  0.8 1.3 %collective-permute-start = (bf16[4,5248]{1,0:T(4,128)(2,1)S(1)}, bf16[4,5248]{1,0:T(4,128)(2,1)S(1)}, u32[]{:S(2)}, u32[]{:S(2)}) collective-permute-start(bf16[4,5248]{1,0:T(4,128)(2,1)S(1)} %pack.1.packed_ref), channel_id=1, source_target_pairs={{2,0},{4,2},{6,4},{8,6},{10,8},{12,10},{14,12},{16,14},{18,16},{20... | collective-permute-start | bytes 125960 | tf_op jit(solution)/shard_map/ppermute | solution.py:310
  2.1 1.7 %prepare.1 = (f32[1024,128]{1,0:T(8,128)S(1)}, bf16[2,64,16,512]{3,2,1,0:T(8,128)(2,1)S(1)}, bf16[2,8192]{1,0:T(2,128)(2,1)S(1)}, f32[1,8192]{1,0:T(1,128)S(1)},...) custom-call(s32[4,16]{1,0:T(4,128)} %refs_0_.1, s32[4]{0:T(128)} %refs_1_.1, bf16[2,64,16,512]{3,2,1,0:T(8,128)(2,1)} %refs_2_.1, ...), custom_call_target="tpu_custom_call" | custom-call | bytes 8388608 | tf_op jit(solution)/shard_map/prepare/pallas_call | solution.py:315
  3.8 0.1 collective-permute-done.packed_ref
  3.9 1.3 %attend.2.refs_0_ = bf16[4,4096]{1,0:T(4,128)(2,1)S(1)} custom-call(bf16[4,5248]{1,0:T(4,128)(2,1)S(1)} %collective-permute-done.packed_ref, bf16[2,64,16,512]{3,2,1,0:T(8,128)(2,1)S(1)} %get-tuple-element.23.pool_ref, f32[1024,128]{1,0:T(8,128)S(1)} %get-tuple-element.24.owner_ref), custom_call_target="tpu_custom_call" | custom-call | tf_op jit(solution)/shard_map/attend/pallas_call | solution.py:336
  5.2 5.4 %collective-permute-start.1 = (bf16[4,4096]{1,0:T(4,128)(2,1)S(1)}, bf16[4,4096]{1,0:T(4,128)(2,1)S(1)}, u32[]{:S(2)}, u32[]{:S(2)}) collective-permute-start(bf16[4,4096]{1,0:T(4,128)(2,1)S(1)} %attend.2.refs_0_), channel_id=1, source_target_pairs={{0,2},{2,4},{4,6},{6,8},{8,10},{10,12},{12,14},{14,16},{16,18},{18... | collective-permute-start | bytes 98312 | tf_op jit(solution)/shard_map/ppermute | solution.py:346
  10.7 0.0 slice-start
  10.7 0.0 slice-start.2
  10.7 0.0 slice-start.4
  10.7 1.3 %attend.3.own_ref = bf16[4,4096]{1,0:T(4,128)(2,1)S(1)} custom-call(bf16[4,5248]{1,0:T(4,128)(2,1)S(1)} %pack.1.packed_ref, bf16[2,64,16,512]{3,2,1,0:T(8,128)(2,1)S(1)} %get-tuple-element.23.pool_ref, f32[1024,128]{1,0:T(8,128)S(1)} %get-tuple-element.24.owner_ref, bf16[4,4096]{1,0:T(4,128)(2,1)S(1)} %attend.2.refs_0_), custom_call_target="tpu_custom_call" | custom-call | tf_op jit(solution)/shard_map/attend/pallas_call | solution.py:336
  12.0 0.0 collective-permute-done.1.behind_ref
  12.0 0.0 slice-start.1
  12.0 0.0 slice-start.3
  12.1 0.0 slice-start.5
  12.1 4.7 %collective-permute-start.3 = (bf16[2,12288]{1,0:T(2,128)(2,1)S(1)}, bf16[2,12288]{1,0:T(2,128)(2,1)S(1)}, u32[]{:S(2)}, u32[]{:S(2)}) collective-permute-start(bf16[2,12288]{1,0:T(2,128)(2,1)S(1)} %get-tuple-element.26.stay_ref), channel_id=1, source_target_pairs={{0,16},{2,18},{4,20},{6,22},{8,24},{10,26},{12,28},{14,30},{16,0},... | collective-permute-start | bytes 147464 | tf_op jit(solution)/shard_map/ppermute | solution.py:274
  16.8 1.0 %collective-permute-start.4 = (bf16[2,4096]{1,0:T(2,128)(2,1)S(1)}, bf16[2,4096]{1,0:T(2,128)(2,1)S(1)}, u32[]{:S(2)}, u32[]{:S(2)}) collective-permute-start(bf16[2,4096]{1,0:T(2,128)(2,1)S(1)} %get-tuple-element.27), channel_id=1, source_target_pairs={{0,17},{1,16},{2,19},{3,18},{4,21},{5,20},{6,23},{7,22},{8,25},{9,... | collective-permute-start | bytes 49160 | tf_op jit(solution)/shard_map/ppermute | solution.py:364
  17.9 0.5 %collective-permute-start.2 = (bf16[2,4096]{1,0:T(2,128)(2,1)S(1)}, bf16[2,4096]{1,0:T(2,128)(2,1)S(1)}, u32[]{:S(2)}, u32[]{:S(2)}) collective-permute-start(bf16[2,4096]{1,0:T(2,128)(2,1)S(1)} %get-tuple-element.27), channel_id=1, source_target_pairs={{0,1},{1,0},{2,3},{3,2},{4,5},{5,4},{6,7},{7,6},{8,9},{9,8},{10,11... | collective-permute-start | bytes 49160 | tf_op jit(solution)/shard_map/ppermute | solution.py:370
  18.4 4.0 %collective-permute-done.4.far_cross_ref = bf16[2,4096]{1,0:T(2,128)(2,1)S(1)} collective-permute-done((bf16[2,4096]{1,0:T(2,128)(2,1)S(1)}, bf16[2,4096]{1,0:T(2,128)(2,1)S(1)}, u32[]{:S(2)}, u32[]{:S(2)}) %collective-permute-start.4) | collective-permute-done | bytes 16416 | tf_op jit(solution)/shard_map/ppermute | solution.py:364
  22.4 0.0 collective-permute-done.2.cross_ref
  22.4 0.0 collective-permute-done.3.far_stay_ref
  22.4 0.2 norm.1
  22.6 1.0 %collective-permute-start.7 = (bf16[4,8192]{1,0:T(4,128)(2,1)S(1)}, bf16[4,8192]{1,0:T(4,128)(2,1)S(1)}, u32[]{:S(2)}, u32[]{:S(2)}) collective-permute-start(bf16[4,8192]{1,0:T(4,128)(2,1)S(1)} %get-tuple-element.32.refs_0_), channel_id=1, source_target_pairs={{0,12},{2,14},{4,8},{6,10},{8,4},{10,6},{12,0},{14,2},{16,28},{18,... | collective-permute-start | bytes 196616 | tf_op jit(solution)/shard_map/ppermute | solution.py:274
  23.6 0.8 %collective-permute-start.6 = (bf16[4,8192]{1,0:T(4,128)(2,1)S(1)}, bf16[4,8192]{1,0:T(4,128)(2,1)S(1)}, u32[]{:S(2)}, u32[]{:S(2)}) collective-permute-start(bf16[4,8192]{1,0:T(4,128)(2,1)S(1)} %get-tuple-element.32.refs_0_), channel_id=1, source_target_pairs={{0,8},{2,10},{4,12},{6,14},{8,0},{10,2},{12,4},{14,6},{16,24},{18,... | collective-permute-start | bytes 196616 | tf_op jit(solution)/shard_map/ppermute | solution.py:274
  24.4 1.7 %collective-permute-start.5 = (bf16[4,8192]{1,0:T(4,128)(2,1)S(1)}, bf16[4,8192]{1,0:T(4,128)(2,1)S(1)}, u32[]{:S(2)}, u32[]{:S(2)}) collective-permute-start(bf16[4,8192]{1,0:T(4,128)(2,1)S(1)} %get-tuple-element.32.refs_0_), channel_id=1, source_target_pairs={{0,4},{2,6},{4,0},{6,2},{8,12},{10,14},{12,8},{14,10},{16,20},{18,... | collective-permute-start | bytes 196616 | tf_op jit(solution)/shard_map/ppermute | solution.py:274
  26.2 1.7 %collective-permute-done.7.refs_3_ = bf16[4,8192]{1,0:T(4,128)(2,1)S(1)} collective-permute-done((bf16[4,8192]{1,0:T(4,128)(2,1)S(1)}, bf16[4,8192]{1,0:T(4,128)(2,1)S(1)}, u32[]{:S(2)}, u32[]{:S(2)}) %collective-permute-start.7) | collective-permute-done | bytes 65568 | tf_op jit(solution)/shard_map/ppermute | solution.py:274
  27.9 0.1 collective-permute-done.6.refs_2_
  27.9 0.8 %collective-permute-done.5.refs_1_ = bf16[4,8192]{1,0:T(4,128)(2,1)S(1)} collective-permute-done((bf16[4,8192]{1,0:T(4,128)(2,1)S(1)}, bf16[4,8192]{1,0:T(4,128)(2,1)S(1)}, u32[]{:S(2)}, u32[]{:S(2)}) %collective-permute-start.5) | collective-permute-done | bytes 65568 | tf_op jit(solution)/shard_map/ppermute | solution.py:274
  28.7 0.1 join.1.near_ref
  28.8 0.1 collective-permute-start.8
  28.9 1.5 %collective-permute-done.8.far_ref = bf16[16,8192]{1,0:T(8,128)(2,1)S(1)} collective-permute-done((bf16[16,8192]{1,0:T(8,128)(2,1)S(1)}, bf16[16,8192]{1,0:T(8,128)(2,1)S(1)}, u32[]{:S(2)}, u32[]{:S(2)}) %collective-permute-start.8) | collective-permute-done | bytes 262176 | tf_op jit(solution)/shard_map/ppermute | solution.py:274
  30.4 0.0 slice-done
  30.4 0.0 slice-done.2
  30.4 0.0 slice-done.4
  30.4 0.0 slice-done.1
  30.4 0.0 slice-done.3
  30.4 0.0 slice-done.5
  30.4 4.6 %feed.1 = (f32[16,8192]{1,0:T(8,128)S(1)}, bf16[16,8192]{1,0:T(8,128)(2,1)S(1)}) custom-call(s32[2,8,32]{2,1,0:T(8,128)S(1)} %get-tuple-element.30.keeps_ref, f32[3,8,32]{2,1,0:T(8,128)S(1)} %get-tuple-element.31.scales_ref, bf16[16,8192]{1,0:T(8,128)(2,1)S(1)} %join.1.near_ref, bf16[16,8192]{1,0:T(8,128)(2,1)S(1)} %collective-permute-done.8.far_ref, ...), custom_call_target="tpu_custom_call" | custom-call | tf_op jit(solution)/shard_map/feed/pallas_call | solution.py:387
  35.1 0.2 collective-permute-start.9
  35.3 1.4 %collective-permute-done.9.refs_0_ = bf16[16,8192]{1,0:T(8,128)(2,1)S(1)} collective-permute-done((bf16[16,8192]{1,0:T(8,128)(2,1)S(1)}, bf16[16,8192]{1,0:T(8,128)(2,1)S(1)}, u32[]{:S(2)}, u32[]{:S(2)}) %collective-permute-start.9) | collective-permute-done | bytes 262176 | tf_op jit(solution)/shard_map/ppermute | solution.py:274
  36.7 0.1 sum.2
  36.8 2.8 %collective-permute-start.10 = (bf16[4,8192]{1,0:T(4,128)(2,1)S(1)}, bf16[4,8192]{1,0:T(4,128)(2,1)S(1)}, u32[]{:S(2)}, u32[]{:S(2)}) collective-permute-start(bf16[4,8192]{1,0:T(4,128)(2,1)S(1)} %get-tuple-element.36), channel_id=1, source_target_pairs={{0,12},{2,14},{4,8},{6,10},{8,4},{10,6},{12,0},{14,2},{16,28},{18,... | collective-permute-start | bytes 196616 | tf_op jit(solution)/shard_map/ppermute | solution.py:274
  39.6 0.1 collective-permute-start.11
  39.8 0.6 %collective-permute-start.12 = (bf16[4,8192]{1,0:T(4,128)(2,1)S(1)}, bf16[4,8192]{1,0:T(4,128)(2,1)S(1)}, u32[]{:S(2)}, u32[]{:S(2)}) collective-permute-start(bf16[4,8192]{1,0:T(4,128)(2,1)S(1)} %get-tuple-element.38), channel_id=1, source_target_pairs={{0,8},{2,10},{4,12},{6,14},{8,0},{10,2},{12,4},{14,6},{16,24},{18,... | collective-permute-start | bytes 196616 | tf_op jit(solution)/shard_map/ppermute | solution.py:274
  40.4 1.7 %collective-permute-done.10.refs_0_ = bf16[4,8192]{1,0:T(4,128)(2,1)S(1)} collective-permute-done((bf16[4,8192]{1,0:T(4,128)(2,1)S(1)}, bf16[4,8192]{1,0:T(4,128)(2,1)S(1)}, u32[]{:S(2)}, u32[]{:S(2)}) %collective-permute-start.10) | collective-permute-done | bytes 65568 | tf_op jit(solution)/shard_map/ppermute | solution.py:274
  42.0 1.9 %collective-permute-done.11.refs_1_ = bf16[4,8192]{1,0:T(4,128)(2,1)S(1)} collective-permute-done((bf16[4,8192]{1,0:T(4,128)(2,1)S(1)}, bf16[4,8192]{1,0:T(4,128)(2,1)S(1)}, u32[]{:S(2)}, u32[]{:S(2)}) %collective-permute-start.11) | collective-permute-done | bytes 65568 | tf_op jit(solution)/shard_map/ppermute | solution.py:274
  43.9 0.1 collective-permute-done.12.refs_2_
  44.0 0.1 sum.3
  44.1 2.1 %collective-permute-start.13 = (bf16[2,8192]{1,0:T(2,128)(2,1)S(1)}, bf16[2,8192]{1,0:T(2,128)(2,1)S(1)}, u32[]{:S(2)}, u32[]{:S(2)}) collective-permute-start(bf16[2,8192]{1,0:T(2,128)(2,1)S(1)} %get-tuple-element.40), channel_id=1, source_target_pairs={{0,16},{2,18},{4,20},{6,22},{8,24},{10,26},{12,28},{14,30},{16,0},... | collective-permute-start | bytes 98312 | tf_op jit(solution)/shard_map/ppermute | solution.py:274
  46.2 2.7 %collective-permute-done.13 = bf16[2,8192]{1,0:T(2,128)(2,1)S(1)} collective-permute-done((bf16[2,8192]{1,0:T(2,128)(2,1)S(1)}, bf16[2,8192]{1,0:T(2,128)(2,1)S(1)}, u32[]{:S(2)}, u32[]{:S(2)}) %collective-permute-start.13) | collective-permute-done | bytes 32800 | tf_op jit(solution)/shard_map/ppermute | solution.py:274
  49.0 0.7 %add_convert_fusion = bf16[2,8192]{1,0:T(2,128)(2,1)} fusion(bf16[2,8192]{1,0:T(2,128)(2,1)S(1)} %collective-permute-done.13, f32[2,8192]{1,0:T(2,128)S(1)} %get-tuple-element.29, f32[2,8192]{1,0:T(2,128)S(1)} %get-tuple-element.39), kind=kLoop, calls=%fused_computation | loop fusion | flops 65536 | bytes 196608 | tf_op jit(solution)/shard_map/convert_element_type | solution.py:408
  (4 shorter events, 0.0 us)
Async XLA Ops:
  0.8 3.1 %collective-permute-start = (bf16[4,5248]{1,0:T(4,128)(2,1)S(1)}, bf16[4,5248]{1,0:T(4,128)(2,1)S(1)}, u32[]{:S(2)}, u32[]{:S(2)}) collective-permute-start(bf16[4,5248]{1,0:T(4,128)(2,1)S(1)} %pack.1.packed_ref), channel_id=1, source_target_pairs={{2,0},{4,2},{6,4},{8,6},{10,8},{12,10},{14,12},{16,14},{18,16},{20... | collective-permute-start | bytes 125960 | tf_op jit(solution)/shard_map/ppermute | solution.py:310
  5.2 6.8 %collective-permute-start.1 = (bf16[4,4096]{1,0:T(4,128)(2,1)S(1)}, bf16[4,4096]{1,0:T(4,128)(2,1)S(1)}, u32[]{:S(2)}, u32[]{:S(2)}) collective-permute-start(bf16[4,4096]{1,0:T(4,128)(2,1)S(1)} %attend.2.refs_0_), channel_id=1, source_target_pairs={{0,2},{2,4},{4,6},{6,8},{8,10},{10,12},{12,14},{14,16},{16,18},{18... | collective-permute-start | bytes 98312 | tf_op jit(solution)/shard_map/ppermute | solution.py:346
  10.7 19.7 %slice-start = ((s8[8388608]{0:T(1024)(128)(4,1)}), s8[4194304]{0:T(1024)(128)(4,1)S(1)}, s32[]{:S(2)}) async-start(s8[8388608]{0:T(1024)(128)(4,1)} %bitcast.1), calls=%async_computation | async-start | bytes 8388608
  10.7 19.7 %slice-start.2 = ((s8[8388608]{0:T(1024)(128)(4,1)}), s8[4194304]{0:T(1024)(128)(4,1)S(1)}, s32[]{:S(2)}) async-start(s8[8388608]{0:T(1024)(128)(4,1)} %bitcast.3), calls=%async_computation.2 | async-start | bytes 8388608
  10.7 19.7 %slice-start.4 = ((s8[8388608]{0:T(1024)(128)(4,1)}), s8[4194304]{0:T(1024)(128)(4,1)S(1)}, s32[]{:S(2)}) async-start(s8[8388608]{0:T(1024)(128)(4,1)} %bitcast.5), calls=%async_computation.4 | async-start | bytes 8388608
  12.0 18.4 %slice-start.1 = ((s8[8388608]{0:T(1024)(128)(4,1)}), s8[4194304]{0:T(1024)(128)(4,1)S(1)}, s32[]{:S(2)}) async-start(s8[8388608]{0:T(1024)(128)(4,1)} %bitcast.1), calls=%async_computation.1 | async-start | bytes 8388608
  12.0 18.3 %slice-start.3 = ((s8[8388608]{0:T(1024)(128)(4,1)}), s8[4194304]{0:T(1024)(128)(4,1)S(1)}, s32[]{:S(2)}) async-start(s8[8388608]{0:T(1024)(128)(4,1)} %bitcast.3), calls=%async_computation.3 | async-start | bytes 8388608
  12.1 18.3 %slice-start.5 = ((s8[8388608]{0:T(1024)(128)(4,1)}), s8[4194304]{0:T(1024)(128)(4,1)S(1)}, s32[]{:S(2)}) async-start(s8[8388608]{0:T(1024)(128)(4,1)} %bitcast.5), calls=%async_computation.5 | async-start | bytes 8388608
  12.1 10.3 %collective-permute-start.3 = (bf16[2,12288]{1,0:T(2,128)(2,1)S(1)}, bf16[2,12288]{1,0:T(2,128)(2,1)S(1)}, u32[]{:S(2)}, u32[]{:S(2)}) collective-permute-start(bf16[2,12288]{1,0:T(2,128)(2,1)S(1)} %get-tuple-element.26.stay_ref), channel_id=1, source_target_pairs={{0,16},{2,18},{4,20},{6,22},{8,24},{10,26},{12,28},{14,30},{16,0},... | collective-permute-start | bytes 147464 | tf_op jit(solution)/shard_map/ppermute | solution.py:274
  16.8 5.5 %collective-permute-start.4 = (bf16[2,4096]{1,0:T(2,128)(2,1)S(1)}, bf16[2,4096]{1,0:T(2,128)(2,1)S(1)}, u32[]{:S(2)}, u32[]{:S(2)}) collective-permute-start(bf16[2,4096]{1,0:T(2,128)(2,1)S(1)} %get-tuple-element.27), channel_id=1, source_target_pairs={{0,17},{1,16},{2,19},{3,18},{4,21},{5,20},{6,23},{7,22},{8,25},{9,... | collective-permute-start | bytes 49160 | tf_op jit(solution)/shard_map/ppermute | solution.py:364
  17.9 4.5 %collective-permute-start.2 = (bf16[2,4096]{1,0:T(2,128)(2,1)S(1)}, bf16[2,4096]{1,0:T(2,128)(2,1)S(1)}, u32[]{:S(2)}, u32[]{:S(2)}) collective-permute-start(bf16[2,4096]{1,0:T(2,128)(2,1)S(1)} %get-tuple-element.27), channel_id=1, source_target_pairs={{0,1},{1,0},{2,3},{3,2},{4,5},{5,4},{6,7},{7,6},{8,9},{9,8},{10,11... | collective-permute-start | bytes 49160 | tf_op jit(solution)/shard_map/ppermute | solution.py:370
  22.6 5.2 %collective-permute-start.7 = (bf16[4,8192]{1,0:T(4,128)(2,1)S(1)}, bf16[4,8192]{1,0:T(4,128)(2,1)S(1)}, u32[]{:S(2)}, u32[]{:S(2)}) collective-permute-start(bf16[4,8192]{1,0:T(4,128)(2,1)S(1)} %get-tuple-element.32.refs_0_), channel_id=1, source_target_pairs={{0,12},{2,14},{4,8},{6,10},{8,4},{10,6},{12,0},{14,2},{16,28},{18,... | collective-permute-start | bytes 196616 | tf_op jit(solution)/shard_map/ppermute | solution.py:274
  23.6 4.3 %collective-permute-start.6 = (bf16[4,8192]{1,0:T(4,128)(2,1)S(1)}, bf16[4,8192]{1,0:T(4,128)(2,1)S(1)}, u32[]{:S(2)}, u32[]{:S(2)}) collective-permute-start(bf16[4,8192]{1,0:T(4,128)(2,1)S(1)} %get-tuple-element.32.refs_0_), channel_id=1, source_target_pairs={{0,8},{2,10},{4,12},{6,14},{8,0},{10,2},{12,4},{14,6},{16,24},{18,... | collective-permute-start | bytes 196616 | tf_op jit(solution)/shard_map/ppermute | solution.py:274
  24.4 4.3 %collective-permute-start.5 = (bf16[4,8192]{1,0:T(4,128)(2,1)S(1)}, bf16[4,8192]{1,0:T(4,128)(2,1)S(1)}, u32[]{:S(2)}, u32[]{:S(2)}) collective-permute-start(bf16[4,8192]{1,0:T(4,128)(2,1)S(1)} %get-tuple-element.32.refs_0_), channel_id=1, source_target_pairs={{0,4},{2,6},{4,0},{6,2},{8,12},{10,14},{12,8},{14,10},{16,20},{18,... | collective-permute-start | bytes 196616 | tf_op jit(solution)/shard_map/ppermute | solution.py:274
  28.8 1.6 %collective-permute-start.8 = (bf16[16,8192]{1,0:T(8,128)(2,1)S(1)}, bf16[16,8192]{1,0:T(8,128)(2,1)S(1)}, u32[]{:S(2)}, u32[]{:S(2)}) collective-permute-start(bf16[16,8192]{1,0:T(8,128)(2,1)S(1)} %join.1.near_ref), channel_id=1, source_target_pairs={{0,2},{2,0},{4,6},{6,4},{8,10},{10,8},{12,14},{14,12},{16,18},{18,... | collective-permute-start | bytes 786440 | tf_op jit(solution)/shard_map/ppermute | solution.py:274
  35.1 1.6 %collective-permute-start.9 = (bf16[16,8192]{1,0:T(8,128)(2,1)S(1)}, bf16[16,8192]{1,0:T(8,128)(2,1)S(1)}, u32[]{:S(2)}, u32[]{:S(2)}) collective-permute-start(bf16[16,8192]{1,0:T(8,128)(2,1)S(1)} %get-tuple-element.34), channel_id=1, source_target_pairs={{0,2},{2,0},{4,6},{6,4},{8,10},{10,8},{12,14},{14,12},{16,18},{18,... | collective-permute-start | bytes 786440 | tf_op jit(solution)/shard_map/ppermute | solution.py:274
  36.8 5.2 %collective-permute-start.10 = (bf16[4,8192]{1,0:T(4,128)(2,1)S(1)}, bf16[4,8192]{1,0:T(4,128)(2,1)S(1)}, u32[]{:S(2)}, u32[]{:S(2)}) collective-permute-start(bf16[4,8192]{1,0:T(4,128)(2,1)S(1)} %get-tuple-element.36), channel_id=1, source_target_pairs={{0,12},{2,14},{4,8},{6,10},{8,4},{10,6},{12,0},{14,2},{16,28},{18,... | collective-permute-start | bytes 196616 | tf_op jit(solution)/shard_map/ppermute | solution.py:274
  39.6 4.3 %collective-permute-start.11 = (bf16[4,8192]{1,0:T(4,128)(2,1)S(1)}, bf16[4,8192]{1,0:T(4,128)(2,1)S(1)}, u32[]{:S(2)}, u32[]{:S(2)}) collective-permute-start(bf16[4,8192]{1,0:T(4,128)(2,1)S(1)} %get-tuple-element.37), channel_id=1, source_target_pairs={{0,4},{2,6},{4,0},{6,2},{8,12},{10,14},{12,8},{14,10},{16,20},{18,... | collective-permute-start | bytes 196616 | tf_op jit(solution)/shard_map/ppermute | solution.py:274
  39.8 4.3 %collective-permute-start.12 = (bf16[4,8192]{1,0:T(4,128)(2,1)S(1)}, bf16[4,8192]{1,0:T(4,128)(2,1)S(1)}, u32[]{:S(2)}, u32[]{:S(2)}) collective-permute-start(bf16[4,8192]{1,0:T(4,128)(2,1)S(1)} %get-tuple-element.38), channel_id=1, source_target_pairs={{0,8},{2,10},{4,12},{6,14},{8,0},{10,2},{12,4},{14,6},{16,24},{18,... | collective-permute-start | bytes 196616 | tf_op jit(solution)/shard_map/ppermute | solution.py:274
  44.1 4.9 %collective-permute-start.13 = (bf16[2,8192]{1,0:T(2,128)(2,1)S(1)}, bf16[2,8192]{1,0:T(2,128)(2,1)S(1)}, u32[]{:S(2)}, u32[]{:S(2)}) collective-permute-start(bf16[2,8192]{1,0:T(2,128)(2,1)S(1)} %get-tuple-element.40), channel_id=1, source_target_pairs={{0,16},{2,18},{4,20},{6,22},{8,24},{10,26},{12,28},{14,30},{16,0},... | collective-permute-start | bytes 98312 | tf_op jit(solution)/shard_map/ppermute | solution.py:274

commit v7 on v6

--- a/solution.py
+++ b/solution.py
@@ -17,7 +17,6 @@
 WHILE_EXCHANGING = pl.CostEstimate(flops=20 * 10**9, bytes_accessed=64 * MIB, transcendentals=0)
 
 VMEM = pl.BlockSpec(memory_space=pltpu.VMEM)
-SMEM = pl.BlockSpec(memory_space=pltpu.SMEM)
 HBM = pl.BlockSpec(memory_space=pltpu.HBM)
 
 
@@ -118,12 +117,25 @@
         ).astype(bf16)
 
 
+def side_by_side(block):
+    height, width = block.shape
+    per_row = HD // width
+    wide = jnp.concatenate([block, jnp.zeros((height, HD - width), block.dtype)], axis=1)
+    rows = []
+    for start in range(0, height, per_row):
+        row = wide[start : start + 1]
+        for j in range(1, min(per_row, height - start)):
+            row = row + pltpu.roll(wide[start + j : start + j + 1], j * width, 1)
+        rows.append(row)
+    return jnp.concatenate(rows, axis=0)
+
+
 def prepare_kernel(count, *refs):
     page_hbm, length_hbm, sources = refs[0], refs[1], refs[2 : 2 + count]
     lists, refs = refs[2 + count : 7 + count], refs[7 + count :]
     owner_ref, targets, keeps_ref, scales_ref = refs[0], refs[1 : 1 + count], *refs[1 + count : 3 + count]
-    page_ref, length_ref, sems = refs[3 + count :]
-    stacked = [keeps_ref.at[i] for i in range(2)] + [scales_ref.at[i] for i in range(3)]
+    page_ref, length_ref, keeps, scales, sems = refs[3 + count :]
+    stacked = [keeps.at[i] for i in range(2)] + [scales.at[i] for i in range(3)]
     moves = copies(
         (
             (page_hbm, page_ref),
@@ -145,6 +157,9 @@
             owner_ref[places, :] = jnp.where(offset < length_ref[r] - i * page, float(r), -1.0)
     for move in moves[2:]:
         move.wait()
+    for source, target in ((keeps, keeps_ref), (scales, scales_ref)):
+        for i in range(source.shape[0]):
+            target[i] = side_by_side(source[i])
 
 
 def merge_kernel(own_ref, behind_ref, residual_ref, cross_ref, stay_ref):
@@ -177,16 +192,25 @@
 
 
 def feed_kernel(
-    keeps_ref, scales_ref, near_ref, far_ref, gate_ref, up_ref, down_ref,
-    stay_ref, send_ref, far_total,
+    keeps_vmem, scales_vmem, near_ref, far_ref, gate_ref, up_ref, down_ref,
+    stay_ref, send_ref, far_total, keeps_ref, scales_ref, sems,
 ):
-    _, columns, keep = keeps_ref.shape
+    columns, keep = gate_ref.shape[:2]
     half = near_ref.shape[0]
+    per_row = HD // keep
+    moves = copies(((keeps_vmem, keeps_ref), (scales_vmem, scales_ref)), sems)
+    for move in moves:
+        move.start()
     stay_ref[...] = jnp.zeros_like(stay_ref)
     far_total[...] = jnp.zeros_like(far_total)
+    for move in moves:
+        move.wait()
+
+    def entry(ref, which, c, k):
+        return ref[which, c // per_row, c % per_row * keep + k]
 
     def block(which, c, k):
-        return pl.ds(pl.multiple_of(keeps_ref[which, c, k] * BLK, BLK), BLK)
+        return pl.ds(pl.multiple_of(entry(keeps_ref, which, c, k) * BLK, BLK), BLK)
 
     hidden = []
     for c in range(columns):
@@ -199,8 +223,8 @@
                 picked, jnp.concatenate([gate_ref[c, k], up_ref[c, k]], axis=1),
                 preferred_element_type=jnp.float32,
             )
-            gate_sum += scales_ref[0, c, k] * both[:, :BLK]
-            up_sum += scales_ref[1, c, k] * both[:, BLK:]
+            gate_sum += entry(scales_ref, 0, c, k) * both[:, :BLK]
+            up_sum += entry(scales_ref, 1, c, k) * both[:, BLK:]
         hidden.append((gate_sum / (1.0 + jnp.exp(-gate_sum)) * up_sum).astype(jnp.bfloat16))
     for c in range(columns):
         for start in range(0, keep, GROUP):
@@ -215,7 +239,7 @@
                     preferred_element_type=jnp.float32,
                 )
                 for j in range(2):
-                    term = scales_ref[2, c, group[i + j]] * both[:, j * BLK : (j + 1) * BLK]
+                    term = entry(scales_ref, 2, c, group[i + j]) * both[:, j * BLK : (j + 1) * BLK]
                     near_sums[i + j] += term[:half]
                     far_sums[i + j] += term[half:]
             for where, near_sum, far_sum in zip(places, near_sums, far_sums):
@@ -293,7 +317,7 @@
     groups = kv_width // HD
     per_group = width // kv_width
     part, model = residual.shape
-    columns = gate_blocks.shape[0]
+    columns, keep = gate_up_keep.shape
 
     own = pl.pallas_call(
         pack_kernel,
@@ -317,14 +341,16 @@
         out_shape=(
             jax.ShapeDtypeStruct((spots, HD), f32),
             *[like(a) for a in stored],
-            jax.ShapeDtypeStruct((2, *gate_up_keep.shape), jnp.int32),
-            jax.ShapeDtypeStruct((3, *gate_scale.shape), f32),
+            jax.ShapeDtypeStruct((2, -(-columns * keep // HD), HD), jnp.int32),
+            jax.ShapeDtypeStruct((3, -(-columns * keep // HD), HD), f32),
         ),
         in_specs=[HBM] * (2 + len(stored) + len(lists)),
         out_specs=(VMEM,) * (3 + len(stored)),
         scratch_shapes=[
             pltpu.SMEM(page_table.shape, jnp.int32),
             pltpu.SMEM(tail_length.shape, jnp.int32),
+            pltpu.VMEM((2, columns, keep), jnp.int32),
+            pltpu.VMEM((3, columns, keep), f32),
             pltpu.SemaphoreType.DMA((2 + len(stored) + len(lists),)),
         ],
         compiler_params=pltpu.CompilerParams(vmem_limit_bytes=2 * MIB),
@@ -390,9 +416,14 @@
             jax.ShapeDtypeStruct((half, model), f32),
             jax.ShapeDtypeStruct((half, model), bf16),
         ),
-        in_specs=[SMEM] * 2 + [VMEM] * 5,
+        in_specs=[VMEM] * 7,
         out_specs=(VMEM,) * 2,
-        scratch_shapes=[pltpu.VMEM((half, model), f32)],
+        scratch_shapes=[
+            pltpu.VMEM((half, model), f32),
+            pltpu.SMEM(keeps.shape, jnp.int32),
+            pltpu.SMEM(scales.shape, f32),
+            pltpu.SemaphoreType.DMA((2,)),
+        ],
         compiler_params=pltpu.CompilerParams(vmem_limit_bytes=half * model * 10 + 6 * MIB),
         name="feed",
     )(keeps, scales, gathered, far, gate_blocks, up_blocks, down_blocks)
@@ -401,7 +432,8 @@
     for stage in sum_stages:
         sums = combined(stage)
         kept, *sent = summed(kept, blocks, 1 + len(sums))
-        blocks = [swapped(block, s) for block, s in sorted(zip(sent, sums), key=lambda p: -bin(p[1]).count('1'))]
+        farthest = sorted(zip(sent, sums), key=lambda pair: -bin(pair[1]).count("1"))
+        blocks = [swapped(block, s) for block, s in farthest]
     total = middle + kept
     for block in blocks:
         total = total + block.astype(f32)

time: 49.9 us -> 49.7 us (level)
  transfers between devices with their start and end apart: 14 -> 14, of which waited for: 11 -> 9; matrix products, arithmetic and copies ran while one was open for 0% -> 0% of each run, Pallas kernels for 6% -> 6%
where the time goes in v7:
time: 49.7 us; the launch traced here: 49.5 us
  starting transfers between devices  22.6 us (45%)
  waiting for transfers between devices  15.8 us (32%)
  Pallas kernels  10.1 us (20%)
  other arithmetic  0.67 us (1%)
    ppermute x10, starting transfers between devices, swapped(): lax.ppermute(block, 'wide', [(i, i ^ bits) for i in range(lax.axis_size('...  14.3 us
    ppermute x10, waiting for transfers between devices, swapped(): lax.ppermute(block, 'wide', [(i, i ^ bits) for i in range(lax.axis_size('...  11.8 us
    ppermute x1, starting transfers between devices, per_device(): behind = lax.ppermute(ahead, 'wide', [(i, i + 1) for i in range(wide - 1)])  5.44 us
    pallas_call x1, Pallas kernels, per_device(): pl.pallas_call(feed_kernel, out_shape=(jax.ShapeDtypeStruct((half, model)...  4.35 us
    ppermute x1, waiting for transfers between devices, per_device(): lax.ppermute(cross, ('wide', 'head'), [(i * heads + h, (i ^ high) * heads...  3.99 us
    pallas_call x2, Pallas kernels, attended(): pl.pallas_call(functools.partial(attend_kernel, groups, per_group, shift)...  2.6 us
    pallas_call x1, Pallas kernels, per_device(): pl.pallas_call(functools.partial(prepare_kernel, len(stored)), out_shape=...  1.8 us
    ppermute x1, starting transfers between devices, per_device(): following = lax.ppermute(own, 'wide', [(i, i - 1) for i in range(1, wide)])  1.29 us
  transfers between devices with their start and end apart: 14, of which 9 were waited for; matrix products, arithmetic and copies ran while one was open for 0% of the time, Pallas kernels for 6%

profile of v7, /device:TPU:0, one launch (start us, length us, event | category | flops | bytes accessed | tf_op | source)
XLA Modules:
  0.0 49.5 jit_solution(12332621708849099317)
XLA Ops:
  0.0 0.8 %pack.1.packed_ref = bf16[4,5248]{1,0:T(4,128)(2,1)S(1)} custom-call(bf16[4,4096]{1,0:T(4,128)(2,1)} %query_hbm.1, bf16[4,512]{1,0:T(4,128)(2,1)} %key_hbm.1, bf16[4,512]{1,0:T(4,128)(2,1)} %value_hbm.1, s32[4]{0:T(128)} %parent_hbm.1), custom_call_target="tpu_custom_call" | custom-call | tf_op jit(solution)/shard_map/pack/pallas_call | solution.py:322
  0.8 1.3 %collective-permute-start = (bf16[4,5248]{1,0:T(4,128)(2,1)S(1)}, bf16[4,5248]{1,0:T(4,128)(2,1)S(1)}, u32[]{:S(2)}, u32[]{:S(2)}) collective-permute-start(bf16[4,5248]{1,0:T(4,128)(2,1)S(1)} %pack.1.packed_ref), channel_id=1, source_target_pairs={{2,0},{4,2},{6,4},{8,6},{10,8},{12,10},{14,12},{16,14},{18,16},{20... | collective-permute-start | bytes 125960 | tf_op jit(solution)/shard_map/ppermute | solution.py:334
  2.1 1.8 %prepare.1 = (f32[1024,128]{1,0:T(8,128)S(1)}, bf16[2,64,16,512]{3,2,1,0:T(8,128)(2,1)S(1)}, bf16[2,8192]{1,0:T(2,128)(2,1)S(1)}, f32[1,8192]{1,0:T(1,128)S(1)},...) custom-call(s32[4,16]{1,0:T(4,128)} %refs_0_.1, s32[4]{0:T(128)} %refs_1_.1, bf16[2,64,16,512]{3,2,1,0:T(8,128)(2,1)} %refs_2_.1, ...), custom_call_target="tpu_custom_call" | custom-call | bytes 8388608 | tf_op jit(solution)/shard_map/prepare/pallas_call | solution.py:339
  3.9 0.0 collective-permute-done.packed_ref
  3.9 1.3 %attend.2.refs_0_ = bf16[4,4096]{1,0:T(4,128)(2,1)S(1)} custom-call(bf16[4,5248]{1,0:T(4,128)(2,1)S(1)} %collective-permute-done.packed_ref, bf16[2,64,16,512]{3,2,1,0:T(8,128)(2,1)S(1)} %get-tuple-element.23.pool_ref, f32[1024,128]{1,0:T(8,128)S(1)} %get-tuple-element.24.owner_ref), custom_call_target="tpu_custom_call" | custom-call | tf_op jit(solution)/shard_map/attend/pallas_call | solution.py:362
  5.2 5.4 %collective-permute-start.1 = (bf16[4,4096]{1,0:T(4,128)(2,1)S(1)}, bf16[4,4096]{1,0:T(4,128)(2,1)S(1)}, u32[]{:S(2)}, u32[]{:S(2)}) collective-permute-start(bf16[4,4096]{1,0:T(4,128)(2,1)S(1)} %attend.2.refs_0_), channel_id=1, source_target_pairs={{0,2},{2,4},{4,6},{6,8},{8,10},{10,12},{12,14},{14,16},{16,18},{18... | collective-permute-start | bytes 98312 | tf_op jit(solution)/shard_map/ppermute | solution.py:372
  10.7 0.0 slice-start
  10.7 0.0 slice-start.2
  10.7 0.0 slice-start.4
  10.7 1.3 %attend.3.own_ref = bf16[4,4096]{1,0:T(4,128)(2,1)S(1)} custom-call(bf16[4,5248]{1,0:T(4,128)(2,1)S(1)} %pack.1.packed_ref, bf16[2,64,16,512]{3,2,1,0:T(8,128)(2,1)S(1)} %get-tuple-element.23.pool_ref, f32[1024,128]{1,0:T(8,128)S(1)} %get-tuple-element.24.owner_ref, bf16[4,4096]{1,0:T(4,128)(2,1)S(1)} %attend.2.refs_0_), custom_call_target="tpu_custom_call" | custom-call | tf_op jit(solution)/shard_map/attend/pallas_call | solution.py:362
  12.0 0.0 collective-permute-done.1.behind_ref
  12.0 0.0 slice-start.1
  12.0 0.0 slice-start.3
  12.1 0.0 slice-start.5
  12.1 4.8 %collective-permute-start.3 = (bf16[2,12288]{1,0:T(2,128)(2,1)S(1)}, bf16[2,12288]{1,0:T(2,128)(2,1)S(1)}, u32[]{:S(2)}, u32[]{:S(2)}) collective-permute-start(bf16[2,12288]{1,0:T(2,128)(2,1)S(1)} %get-tuple-element.26.stay_ref), channel_id=1, source_target_pairs={{0,16},{2,18},{4,20},{6,22},{8,24},{10,26},{12,28},{14,30},{16,0},... | collective-permute-start | bytes 147464 | tf_op jit(solution)/shard_map/ppermute | solution.py:298
  16.9 1.0 %collective-permute-start.4 = (bf16[2,4096]{1,0:T(2,128)(2,1)S(1)}, bf16[2,4096]{1,0:T(2,128)(2,1)S(1)}, u32[]{:S(2)}, u32[]{:S(2)}) collective-permute-start(bf16[2,4096]{1,0:T(2,128)(2,1)S(1)} %get-tuple-element.27), channel_id=1, source_target_pairs={{0,17},{1,16},{2,19},{3,18},{4,21},{5,20},{6,23},{7,22},{8,25},{9,... | collective-permute-start | bytes 49160 | tf_op jit(solution)/shard_map/ppermute | solution.py:390
  18.0 0.5 %collective-permute-start.2 = (bf16[2,4096]{1,0:T(2,128)(2,1)S(1)}, bf16[2,4096]{1,0:T(2,128)(2,1)S(1)}, u32[]{:S(2)}, u32[]{:S(2)}) collective-permute-start(bf16[2,4096]{1,0:T(2,128)(2,1)S(1)} %get-tuple-element.27), channel_id=1, source_target_pairs={{0,1},{1,0},{2,3},{3,2},{4,5},{5,4},{6,7},{7,6},{8,9},{9,8},{10,11... | collective-permute-start | bytes 49160 | tf_op jit(solution)/shard_map/ppermute | solution.py:396
  18.5 4.0 %collective-permute-done.4.far_cross_ref = bf16[2,4096]{1,0:T(2,128)(2,1)S(1)} collective-permute-done((bf16[2,4096]{1,0:T(2,128)(2,1)S(1)}, bf16[2,4096]{1,0:T(2,128)(2,1)S(1)}, u32[]{:S(2)}, u32[]{:S(2)}) %collective-permute-start.4) | collective-permute-done | bytes 16416 | tf_op jit(solution)/shard_map/ppermute | solution.py:390
  22.5 0.0 collective-permute-done.2.cross_ref
  22.5 0.0 collective-permute-done.3.far_stay_ref
  22.5 0.2 norm.1
  22.7 0.9 %collective-permute-start.7 = (bf16[4,8192]{1,0:T(4,128)(2,1)S(1)}, bf16[4,8192]{1,0:T(4,128)(2,1)S(1)}, u32[]{:S(2)}, u32[]{:S(2)}) collective-permute-start(bf16[4,8192]{1,0:T(4,128)(2,1)S(1)} %get-tuple-element.32.refs_0_), channel_id=1, source_target_pairs={{0,12},{2,14},{4,8},{6,10},{8,4},{10,6},{12,0},{14,2},{16,28},{18,... | collective-permute-start | bytes 196616 | tf_op jit(solution)/shard_map/ppermute | solution.py:298
  23.7 0.8 %collective-permute-start.6 = (bf16[4,8192]{1,0:T(4,128)(2,1)S(1)}, bf16[4,8192]{1,0:T(4,128)(2,1)S(1)}, u32[]{:S(2)}, u32[]{:S(2)}) collective-permute-start(bf16[4,8192]{1,0:T(4,128)(2,1)S(1)} %get-tuple-element.32.refs_0_), channel_id=1, source_target_pairs={{0,8},{2,10},{4,12},{6,14},{8,0},{10,2},{12,4},{14,6},{16,24},{18,... | collective-permute-start | bytes 196616 | tf_op jit(solution)/shard_map/ppermute | solution.py:298
  24.4 1.8 %collective-permute-start.5 = (bf16[4,8192]{1,0:T(4,128)(2,1)S(1)}, bf16[4,8192]{1,0:T(4,128)(2,1)S(1)}, u32[]{:S(2)}, u32[]{:S(2)}) collective-permute-start(bf16[4,8192]{1,0:T(4,128)(2,1)S(1)} %get-tuple-element.32.refs_0_), channel_id=1, source_target_pairs={{0,4},{2,6},{4,0},{6,2},{8,12},{10,14},{12,8},{14,10},{16,20},{18,... | collective-permute-start | bytes 196616 | tf_op jit(solution)/shard_map/ppermute | solution.py:298
  26.3 1.7 %collective-permute-done.7.refs_3_ = bf16[4,8192]{1,0:T(4,128)(2,1)S(1)} collective-permute-done((bf16[4,8192]{1,0:T(4,128)(2,1)S(1)}, bf16[4,8192]{1,0:T(4,128)(2,1)S(1)}, u32[]{:S(2)}, u32[]{:S(2)}) %collective-permute-start.7) | collective-permute-done | bytes 65568 | tf_op jit(solution)/shard_map/ppermute | solution.py:298
  28.0 0.0 collective-permute-done.6.refs_2_
  28.0 0.8 %collective-permute-done.5.refs_1_ = bf16[4,8192]{1,0:T(4,128)(2,1)S(1)} collective-permute-done((bf16[4,8192]{1,0:T(4,128)(2,1)S(1)}, bf16[4,8192]{1,0:T(4,128)(2,1)S(1)}, u32[]{:S(2)}, u32[]{:S(2)}) %collective-permute-start.5) | collective-permute-done | bytes 65568 | tf_op jit(solution)/shard_map/ppermute | solution.py:298
  28.7 0.1 join.1.near_ref
  28.8 0.1 collective-permute-start.8
  28.9 1.5 %collective-permute-done.8.far_ref = bf16[16,8192]{1,0:T(8,128)(2,1)S(1)} collective-permute-done((bf16[16,8192]{1,0:T(8,128)(2,1)S(1)}, bf16[16,8192]{1,0:T(8,128)(2,1)S(1)}, u32[]{:S(2)}, u32[]{:S(2)}) %collective-permute-start.8) | collective-permute-done | bytes 262176 | tf_op jit(solution)/shard_map/ppermute | solution.py:298
  30.4 0.0 slice-done
  30.4 0.0 slice-done.2
  30.4 0.0 slice-done.4
  30.4 0.0 slice-done.1
  30.4 0.0 slice-done.3
  30.4 0.0 slice-done.5
  30.4 4.3 %feed.1 = (f32[16,8192]{1,0:T(8,128)S(1)}, bf16[16,8192]{1,0:T(8,128)(2,1)S(1)}) custom-call(s32[2,2,128]{2,1,0:T(2,128)S(1)} %get-tuple-element.30.keeps_vmem, f32[3,2,128]{2,1,0:T(2,128)S(1)} %get-tuple-element.31.scales_vmem, bf16[16,8192]{1,0:T(8,128)(2,1)S(1)} %join.1.near_ref, bf16[16,8192]{1,0:T(8,128)(2,1)S(1)} %collective-permute-done.8.far_ref, ...), custom_call_target="tpu_custom_call" | custom-call | tf_op jit(solution)/shard_map/feed/pallas_call | solution.py:413
  34.8 0.2 collective-permute-start.9
  35.0 1.4 %collective-permute-done.9.refs_0_ = bf16[16,8192]{1,0:T(8,128)(2,1)S(1)} collective-permute-done((bf16[16,8192]{1,0:T(8,128)(2,1)S(1)}, bf16[16,8192]{1,0:T(8,128)(2,1)S(1)}, u32[]{:S(2)}, u32[]{:S(2)}) %collective-permute-start.9) | collective-permute-done | bytes 262176 | tf_op jit(solution)/shard_map/ppermute | solution.py:298
  36.4 0.1 sum.2
  36.5 2.9 %collective-permute-start.10 = (bf16[4,8192]{1,0:T(4,128)(2,1)S(1)}, bf16[4,8192]{1,0:T(4,128)(2,1)S(1)}, u32[]{:S(2)}, u32[]{:S(2)}) collective-permute-start(bf16[4,8192]{1,0:T(4,128)(2,1)S(1)} %get-tuple-element.36), channel_id=1, source_target_pairs={{0,12},{2,14},{4,8},{6,10},{8,4},{10,6},{12,0},{14,2},{16,28},{18,... | collective-permute-start | bytes 196616 | tf_op jit(solution)/shard_map/ppermute | solution.py:298
  39.4 0.1 collective-permute-start.11
  39.6 0.5 %collective-permute-start.12 = (bf16[4,8192]{1,0:T(4,128)(2,1)S(1)}, bf16[4,8192]{1,0:T(4,128)(2,1)S(1)}, u32[]{:S(2)}, u32[]{:S(2)}) collective-permute-start(bf16[4,8192]{1,0:T(4,128)(2,1)S(1)} %get-tuple-element.38), channel_id=1, source_target_pairs={{0,8},{2,10},{4,12},{6,14},{8,0},{10,2},{12,4},{14,6},{16,24},{18,... | collective-permute-start | bytes 196616 | tf_op jit(solution)/shard_map/ppermute | solution.py:298
  40.1 1.7 %collective-permute-done.10.refs_0_ = bf16[4,8192]{1,0:T(4,128)(2,1)S(1)} collective-permute-done((bf16[4,8192]{1,0:T(4,128)(2,1)S(1)}, bf16[4,8192]{1,0:T(4,128)(2,1)S(1)}, u32[]{:S(2)}, u32[]{:S(2)}) %collective-permute-start.10) | collective-permute-done | bytes 65568 | tf_op jit(solution)/shard_map/ppermute | solution.py:298
  41.8 1.9 %collective-permute-done.11.refs_1_ = bf16[4,8192]{1,0:T(4,128)(2,1)S(1)} collective-permute-done((bf16[4,8192]{1,0:T(4,128)(2,1)S(1)}, bf16[4,8192]{1,0:T(4,128)(2,1)S(1)}, u32[]{:S(2)}, u32[]{:S(2)}) %collective-permute-start.11) | collective-permute-done | bytes 65568 | tf_op jit(solution)/shard_map/ppermute | solution.py:298
  43.7 0.1 collective-permute-done.12.refs_2_
  43.8 0.1 sum.3
  43.9 2.2 %collective-permute-start.13 = (bf16[2,8192]{1,0:T(2,128)(2,1)S(1)}, bf16[2,8192]{1,0:T(2,128)(2,1)S(1)}, u32[]{:S(2)}, u32[]{:S(2)}) collective-permute-start(bf16[2,8192]{1,0:T(2,128)(2,1)S(1)} %get-tuple-element.40), channel_id=1, source_target_pairs={{0,16},{2,18},{4,20},{6,22},{8,24},{10,26},{12,28},{14,30},{16,0},... | collective-permute-start | bytes 98312 | tf_op jit(solution)/shard_map/ppermute | solution.py:298
  46.1 2.7 %collective-permute-done.13 = bf16[2,8192]{1,0:T(2,128)(2,1)S(1)} collective-permute-done((bf16[2,8192]{1,0:T(2,128)(2,1)S(1)}, bf16[2,8192]{1,0:T(2,128)(2,1)S(1)}, u32[]{:S(2)}, u32[]{:S(2)}) %collective-permute-start.13) | collective-permute-done | bytes 32800 | tf_op jit(solution)/shard_map/ppermute | solution.py:298
  48.8 0.7 %add_convert_fusion = bf16[2,8192]{1,0:T(2,128)(2,1)} fusion(bf16[2,8192]{1,0:T(2,128)(2,1)S(1)} %collective-permute-done.13, f32[2,8192]{1,0:T(2,128)S(1)} %get-tuple-element.29, f32[2,8192]{1,0:T(2,128)S(1)} %get-tuple-element.39), kind=kLoop, calls=%fused_computation | loop fusion | flops 65536 | bytes 196608 | tf_op jit(solution)/shard_map/convert_element_type | solution.py:440
  (4 shorter events, 0.0 us)
Async XLA Ops:
  0.8 3.1 %collective-permute-start = (bf16[4,5248]{1,0:T(4,128)(2,1)S(1)}, bf16[4,5248]{1,0:T(4,128)(2,1)S(1)}, u32[]{:S(2)}, u32[]{:S(2)}) collective-permute-start(bf16[4,5248]{1,0:T(4,128)(2,1)S(1)} %pack.1.packed_ref), channel_id=1, source_target_pairs={{2,0},{4,2},{6,4},{8,6},{10,8},{12,10},{14,12},{16,14},{18,16},{20... | collective-permute-start | bytes 125960 | tf_op jit(solution)/shard_map/ppermute | solution.py:334
  5.2 6.8 %collective-permute-start.1 = (bf16[4,4096]{1,0:T(4,128)(2,1)S(1)}, bf16[4,4096]{1,0:T(4,128)(2,1)S(1)}, u32[]{:S(2)}, u32[]{:S(2)}) collective-permute-start(bf16[4,4096]{1,0:T(4,128)(2,1)S(1)} %attend.2.refs_0_), channel_id=1, source_target_pairs={{0,2},{2,4},{4,6},{6,8},{8,10},{10,12},{12,14},{14,16},{16,18},{18... | collective-permute-start | bytes 98312 | tf_op jit(solution)/shard_map/ppermute | solution.py:372
  10.7 19.7 %slice-start = ((s8[8388608]{0:T(1024)(128)(4,1)}), s8[4194304]{0:T(1024)(128)(4,1)S(1)}, s32[]{:S(2)}) async-start(s8[8388608]{0:T(1024)(128)(4,1)} %bitcast.1), calls=%async_computation | async-start | bytes 8388608
  10.7 19.7 %slice-start.2 = ((s8[8388608]{0:T(1024)(128)(4,1)}), s8[4194304]{0:T(1024)(128)(4,1)S(1)}, s32[]{:S(2)}) async-start(s8[8388608]{0:T(1024)(128)(4,1)} %bitcast.3), calls=%async_computation.2 | async-start | bytes 8388608
  10.7 19.7 %slice-start.4 = ((s8[8388608]{0:T(1024)(128)(4,1)}), s8[4194304]{0:T(1024)(128)(4,1)S(1)}, s32[]{:S(2)}) async-start(s8[8388608]{0:T(1024)(128)(4,1)} %bitcast.5), calls=%async_computation.4 | async-start | bytes 8388608
  12.0 18.4 %slice-start.1 = ((s8[8388608]{0:T(1024)(128)(4,1)}), s8[4194304]{0:T(1024)(128)(4,1)S(1)}, s32[]{:S(2)}) async-start(s8[8388608]{0:T(1024)(128)(4,1)} %bitcast.1), calls=%async_computation.1 | async-start | bytes 8388608
  12.0 18.4 %slice-start.3 = ((s8[8388608]{0:T(1024)(128)(4,1)}), s8[4194304]{0:T(1024)(128)(4,1)S(1)}, s32[]{:S(2)}) async-start(s8[8388608]{0:T(1024)(128)(4,1)} %bitcast.3), calls=%async_computation.3 | async-start | bytes 8388608
  12.1 18.4 %slice-start.5 = ((s8[8388608]{0:T(1024)(128)(4,1)}), s8[4194304]{0:T(1024)(128)(4,1)S(1)}, s32[]{:S(2)}) async-start(s8[8388608]{0:T(1024)(128)(4,1)} %bitcast.5), calls=%async_computation.5 | async-start | bytes 8388608
  12.1 10.4 %collective-permute-start.3 = (bf16[2,12288]{1,0:T(2,128)(2,1)S(1)}, bf16[2,12288]{1,0:T(2,128)(2,1)S(1)}, u32[]{:S(2)}, u32[]{:S(2)}) collective-permute-start(bf16[2,12288]{1,0:T(2,128)(2,1)S(1)} %get-tuple-element.26.stay_ref), channel_id=1, source_target_pairs={{0,16},{2,18},{4,20},{6,22},{8,24},{10,26},{12,28},{14,30},{16,0},... | collective-permute-start | bytes 147464 | tf_op jit(solution)/shard_map/ppermute | solution.py:298
  16.9 5.5 %collective-permute-start.4 = (bf16[2,4096]{1,0:T(2,128)(2,1)S(1)}, bf16[2,4096]{1,0:T(2,128)(2,1)S(1)}, u32[]{:S(2)}, u32[]{:S(2)}) collective-permute-start(bf16[2,4096]{1,0:T(2,128)(2,1)S(1)} %get-tuple-element.27), channel_id=1, source_target_pairs={{0,17},{1,16},{2,19},{3,18},{4,21},{5,20},{6,23},{7,22},{8,25},{9,... | collective-permute-start | bytes 49160 | tf_op jit(solution)/shard_map/ppermute | solution.py:390
  18.0 4.5 %collective-permute-start.2 = (bf16[2,4096]{1,0:T(2,128)(2,1)S(1)}, bf16[2,4096]{1,0:T(2,128)(2,1)S(1)}, u32[]{:S(2)}, u32[]{:S(2)}) collective-permute-start(bf16[2,4096]{1,0:T(2,128)(2,1)S(1)} %get-tuple-element.27), channel_id=1, source_target_pairs={{0,1},{1,0},{2,3},{3,2},{4,5},{5,4},{6,7},{7,6},{8,9},{9,8},{10,11... | collective-permute-start | bytes 49160 | tf_op jit(solution)/shard_map/ppermute | solution.py:396
  22.7 5.2 %collective-permute-start.7 = (bf16[4,8192]{1,0:T(4,128)(2,1)S(1)}, bf16[4,8192]{1,0:T(4,128)(2,1)S(1)}, u32[]{:S(2)}, u32[]{:S(2)}) collective-permute-start(bf16[4,8192]{1,0:T(4,128)(2,1)S(1)} %get-tuple-element.32.refs_0_), channel_id=1, source_target_pairs={{0,12},{2,14},{4,8},{6,10},{8,4},{10,6},{12,0},{14,2},{16,28},{18,... | collective-permute-start | bytes 196616 | tf_op jit(solution)/shard_map/ppermute | solution.py:298
  23.7 4.3 %collective-permute-start.6 = (bf16[4,8192]{1,0:T(4,128)(2,1)S(1)}, bf16[4,8192]{1,0:T(4,128)(2,1)S(1)}, u32[]{:S(2)}, u32[]{:S(2)}) collective-permute-start(bf16[4,8192]{1,0:T(4,128)(2,1)S(1)} %get-tuple-element.32.refs_0_), channel_id=1, source_target_pairs={{0,8},{2,10},{4,12},{6,14},{8,0},{10,2},{12,4},{14,6},{16,24},{18,... | collective-permute-start | bytes 196616 | tf_op jit(solution)/shard_map/ppermute | solution.py:298
  24.4 4.3 %collective-permute-start.5 = (bf16[4,8192]{1,0:T(4,128)(2,1)S(1)}, bf16[4,8192]{1,0:T(4,128)(2,1)S(1)}, u32[]{:S(2)}, u32[]{:S(2)}) collective-permute-start(bf16[4,8192]{1,0:T(4,128)(2,1)S(1)} %get-tuple-element.32.refs_0_), channel_id=1, source_target_pairs={{0,4},{2,6},{4,0},{6,2},{8,12},{10,14},{12,8},{14,10},{16,20},{18,... | collective-permute-start | bytes 196616 | tf_op jit(solution)/shard_map/ppermute | solution.py:298
  28.8 1.6 %collective-permute-start.8 = (bf16[16,8192]{1,0:T(8,128)(2,1)S(1)}, bf16[16,8192]{1,0:T(8,128)(2,1)S(1)}, u32[]{:S(2)}, u32[]{:S(2)}) collective-permute-start(bf16[16,8192]{1,0:T(8,128)(2,1)S(1)} %join.1.near_ref), channel_id=1, source_target_pairs={{0,2},{2,0},{4,6},{6,4},{8,10},{10,8},{12,14},{14,12},{16,18},{18,... | collective-permute-start | bytes 786440 | tf_op jit(solution)/shard_map/ppermute | solution.py:298
  34.8 1.6 %collective-permute-start.9 = (bf16[16,8192]{1,0:T(8,128)(2,1)S(1)}, bf16[16,8192]{1,0:T(8,128)(2,1)S(1)}, u32[]{:S(2)}, u32[]{:S(2)}) collective-permute-start(bf16[16,8192]{1,0:T(8,128)(2,1)S(1)} %get-tuple-element.34), channel_id=1, source_target_pairs={{0,2},{2,0},{4,6},{6,4},{8,10},{10,8},{12,14},{14,12},{16,18},{18,... | collective-permute-start | bytes 786440 | tf_op jit(solution)/shard_map/ppermute | solution.py:298
  36.5 5.3 %collective-permute-start.10 = (bf16[4,8192]{1,0:T(4,128)(2,1)S(1)}, bf16[4,8192]{1,0:T(4,128)(2,1)S(1)}, u32[]{:S(2)}, u32[]{:S(2)}) collective-permute-start(bf16[4,8192]{1,0:T(4,128)(2,1)S(1)} %get-tuple-element.36), channel_id=1, source_target_pairs={{0,12},{2,14},{4,8},{6,10},{8,4},{10,6},{12,0},{14,2},{16,28},{18,... | collective-permute-start | bytes 196616 | tf_op jit(solution)/shard_map/ppermute | solution.py:298
  39.4 4.3 %collective-permute-start.11 = (bf16[4,8192]{1,0:T(4,128)(2,1)S(1)}, bf16[4,8192]{1,0:T(4,128)(2,1)S(1)}, u32[]{:S(2)}, u32[]{:S(2)}) collective-permute-start(bf16[4,8192]{1,0:T(4,128)(2,1)S(1)} %get-tuple-element.37), channel_id=1, source_target_pairs={{0,4},{2,6},{4,0},{6,2},{8,12},{10,14},{12,8},{14,10},{16,20},{18,... | collective-permute-start | bytes 196616 | tf_op jit(solution)/shard_map/ppermute | solution.py:298
  39.6 4.3 %collective-permute-start.12 = (bf16[4,8192]{1,0:T(4,128)(2,1)S(1)}, bf16[4,8192]{1,0:T(4,128)(2,1)S(1)}, u32[]{:S(2)}, u32[]{:S(2)}) collective-permute-start(bf16[4,8192]{1,0:T(4,128)(2,1)S(1)} %get-tuple-element.38), channel_id=1, source_target_pairs={{0,8},{2,10},{4,12},{6,14},{8,0},{10,2},{12,4},{14,6},{16,24},{18,... | collective-permute-start | bytes 196616 | tf_op jit(solution)/shard_map/ppermute | solution.py:298
  43.9 4.9 %collective-permute-start.13 = (bf16[2,8192]{1,0:T(2,128)(2,1)S(1)}, bf16[2,8192]{1,0:T(2,128)(2,1)S(1)}, u32[]{:S(2)}, u32[]{:S(2)}) collective-permute-start(bf16[2,8192]{1,0:T(2,128)(2,1)S(1)} %get-tuple-element.40), channel_id=1, source_target_pairs={{0,16},{2,18},{4,20},{6,22},{8,24},{10,26},{12,28},{14,30},{16,0},... | collective-permute-start | bytes 98312 | tf_op jit(solution)/shard_map/ppermute | solution.py:298

commit v8 on v7

--- a/solution.py
+++ b/solution.py
@@ -11,7 +11,7 @@
 HD = 128
 BLK = 128
 PACKED = 16
-GROUP = 4
+GROUP = 2
 DEAD = -1e30
 MIB = 1024 * 1024
 WHILE_EXCHANGING = pl.CostEstimate(flops=20 * 10**9, bytes_accessed=64 * MIB, transcendentals=0)
@@ -201,10 +201,10 @@
     moves = copies(((keeps_vmem, keeps_ref), (scales_vmem, scales_ref)), sems)
     for move in moves:
         move.start()
+    moves[0].wait()
     stay_ref[...] = jnp.zeros_like(stay_ref)
     far_total[...] = jnp.zeros_like(far_total)
-    for move in moves:
-        move.wait()
+    moves[1].wait()
 
     def entry(ref, which, c, k):
         return ref[which, c // per_row, c % per_row * keep + k]

time: 49.7 us -> 49.8 us (level)
  no operation moved by 1% of the time
where the time goes in v8:
time: 49.8 us; the launch traced here: 49.5 us
  starting transfers between devices  22.6 us (45%)
  waiting for transfers between devices  15.8 us (32%)
  Pallas kernels  10.1 us (20%)
  other arithmetic  0.67 us (1%)
    ppermute x10, starting transfers between devices, swapped(): lax.ppermute(block, 'wide', [(i, i ^ bits) for i in range(lax.axis_size('...  14.4 us
    ppermute x10, waiting for transfers between devices, swapped(): lax.ppermute(block, 'wide', [(i, i ^ bits) for i in range(lax.axis_size('...  11.8 us
    ppermute x1, starting transfers between devices, per_device(): behind = lax.ppermute(ahead, 'wide', [(i, i + 1) for i in range(wide - 1)])  5.44 us
    pallas_call x1, Pallas kernels, per_device(): pl.pallas_call(feed_kernel, out_shape=(jax.ShapeDtypeStruct((half, model)...  4.38 us
    ppermute x1, waiting for transfers between devices, per_device(): lax.ppermute(cross, ('wide', 'head'), [(i * heads + h, (i ^ high) * heads...  3.99 us
    pallas_call x2, Pallas kernels, attended(): pl.pallas_call(functools.partial(attend_kernel, groups, per_group, shift)...  2.6 us
    pallas_call x1, Pallas kernels, per_device(): pl.pallas_call(functools.partial(prepare_kernel, len(stored)), out_shape=...  1.8 us
    ppermute x1, starting transfers between devices, per_device(): following = lax.ppermute(own, 'wide', [(i, i - 1) for i in range(1, wide)])  1.29 us
  transfers between devices with their start and end apart: 14, of which 9 were waited for; matrix products, arithmetic and copies ran while one was open for 0% of the time, Pallas kernels for 6%

profile of v8, /device:TPU:0, one launch (start us, length us, event | category | flops | bytes accessed | tf_op | source)
XLA Modules:
  0.0 49.5 jit_solution(12809706205068344235)
XLA Ops:
  0.0 0.8 %pack.1.packed_ref = bf16[4,5248]{1,0:T(4,128)(2,1)S(1)} custom-call(bf16[4,4096]{1,0:T(4,128)(2,1)} %query_hbm.1, bf16[4,512]{1,0:T(4,128)(2,1)} %key_hbm.1, bf16[4,512]{1,0:T(4,128)(2,1)} %value_hbm.1, s32[4]{0:T(128)} %parent_hbm.1), custom_call_target="tpu_custom_call" | custom-call | tf_op jit(solution)/shard_map/pack/pallas_call | solution.py:322
  0.8 1.3 %collective-permute-start = (bf16[4,5248]{1,0:T(4,128)(2,1)S(1)}, bf16[4,5248]{1,0:T(4,128)(2,1)S(1)}, u32[]{:S(2)}, u32[]{:S(2)}) collective-permute-start(bf16[4,5248]{1,0:T(4,128)(2,1)S(1)} %pack.1.packed_ref), channel_id=1, source_target_pairs={{2,0},{4,2},{6,4},{8,6},{10,8},{12,10},{14,12},{16,14},{18,16},{20... | collective-permute-start | bytes 125960 | tf_op jit(solution)/shard_map/ppermute | solution.py:334
  2.1 1.8 %prepare.1 = (f32[1024,128]{1,0:T(8,128)S(1)}, bf16[2,64,16,512]{3,2,1,0:T(8,128)(2,1)S(1)}, bf16[2,8192]{1,0:T(2,128)(2,1)S(1)}, f32[1,8192]{1,0:T(1,128)S(1)},...) custom-call(s32[4,16]{1,0:T(4,128)} %refs_0_.1, s32[4]{0:T(128)} %refs_1_.1, bf16[2,64,16,512]{3,2,1,0:T(8,128)(2,1)} %refs_2_.1, ...), custom_call_target="tpu_custom_call" | custom-call | bytes 8388608 | tf_op jit(solution)/shard_map/prepare/pallas_call | solution.py:339
  3.9 0.0 collective-permute-done.packed_ref
  3.9 1.3 %attend.2.refs_0_ = bf16[4,4096]{1,0:T(4,128)(2,1)S(1)} custom-call(bf16[4,5248]{1,0:T(4,128)(2,1)S(1)} %collective-permute-done.packed_ref, bf16[2,64,16,512]{3,2,1,0:T(8,128)(2,1)S(1)} %get-tuple-element.23.pool_ref, f32[1024,128]{1,0:T(8,128)S(1)} %get-tuple-element.24.owner_ref), custom_call_target="tpu_custom_call" | custom-call | tf_op jit(solution)/shard_map/attend/pallas_call | solution.py:362
  5.2 5.4 %collective-permute-start.1 = (bf16[4,4096]{1,0:T(4,128)(2,1)S(1)}, bf16[4,4096]{1,0:T(4,128)(2,1)S(1)}, u32[]{:S(2)}, u32[]{:S(2)}) collective-permute-start(bf16[4,4096]{1,0:T(4,128)(2,1)S(1)} %attend.2.refs_0_), channel_id=1, source_target_pairs={{0,2},{2,4},{4,6},{6,8},{8,10},{10,12},{12,14},{14,16},{16,18},{18... | collective-permute-start | bytes 98312 | tf_op jit(solution)/shard_map/ppermute | solution.py:372
  10.7 0.0 slice-start
  10.7 0.0 slice-start.2
  10.7 0.0 slice-start.4
  10.7 1.3 %attend.3.own_ref = bf16[4,4096]{1,0:T(4,128)(2,1)S(1)} custom-call(bf16[4,5248]{1,0:T(4,128)(2,1)S(1)} %pack.1.packed_ref, bf16[2,64,16,512]{3,2,1,0:T(8,128)(2,1)S(1)} %get-tuple-element.23.pool_ref, f32[1024,128]{1,0:T(8,128)S(1)} %get-tuple-element.24.owner_ref, bf16[4,4096]{1,0:T(4,128)(2,1)S(1)} %attend.2.refs_0_), custom_call_target="tpu_custom_call" | custom-call | tf_op jit(solution)/shard_map/attend/pallas_call | solution.py:362
  12.0 0.0 collective-permute-done.1.behind_ref
  12.0 0.0 slice-start.1
  12.0 0.0 slice-start.3
  12.1 0.0 slice-start.5
  12.1 4.8 %collective-permute-start.3 = (bf16[2,12288]{1,0:T(2,128)(2,1)S(1)}, bf16[2,12288]{1,0:T(2,128)(2,1)S(1)}, u32[]{:S(2)}, u32[]{:S(2)}) collective-permute-start(bf16[2,12288]{1,0:T(2,128)(2,1)S(1)} %get-tuple-element.26.stay_ref), channel_id=1, source_target_pairs={{0,16},{2,18},{4,20},{6,22},{8,24},{10,26},{12,28},{14,30},{16,0},... | collective-permute-start | bytes 147464 | tf_op jit(solution)/shard_map/ppermute | solution.py:298
  16.9 1.0 %collective-permute-start.4 = (bf16[2,4096]{1,0:T(2,128)(2,1)S(1)}, bf16[2,4096]{1,0:T(2,128)(2,1)S(1)}, u32[]{:S(2)}, u32[]{:S(2)}) collective-permute-start(bf16[2,4096]{1,0:T(2,128)(2,1)S(1)} %get-tuple-element.27), channel_id=1, source_target_pairs={{0,17},{1,16},{2,19},{3,18},{4,21},{5,20},{6,23},{7,22},{8,25},{9,... | collective-permute-start | bytes 49160 | tf_op jit(solution)/shard_map/ppermute | solution.py:390
  18.0 0.5 %collective-permute-start.2 = (bf16[2,4096]{1,0:T(2,128)(2,1)S(1)}, bf16[2,4096]{1,0:T(2,128)(2,1)S(1)}, u32[]{:S(2)}, u32[]{:S(2)}) collective-permute-start(bf16[2,4096]{1,0:T(2,128)(2,1)S(1)} %get-tuple-element.27), channel_id=1, source_target_pairs={{0,1},{1,0},{2,3},{3,2},{4,5},{5,4},{6,7},{7,6},{8,9},{9,8},{10,11... | collective-permute-start | bytes 49160 | tf_op jit(solution)/shard_map/ppermute | solution.py:396
  18.5 4.0 %collective-permute-done.4.far_cross_ref = bf16[2,4096]{1,0:T(2,128)(2,1)S(1)} collective-permute-done((bf16[2,4096]{1,0:T(2,128)(2,1)S(1)}, bf16[2,4096]{1,0:T(2,128)(2,1)S(1)}, u32[]{:S(2)}, u32[]{:S(2)}) %collective-permute-start.4) | collective-permute-done | bytes 16416 | tf_op jit(solution)/shard_map/ppermute | solution.py:390
  22.5 0.0 collective-permute-done.2.cross_ref
  22.5 0.0 collective-permute-done.3.far_stay_ref
  22.5 0.2 norm.1
  22.7 0.9 %collective-permute-start.7 = (bf16[4,8192]{1,0:T(4,128)(2,1)S(1)}, bf16[4,8192]{1,0:T(4,128)(2,1)S(1)}, u32[]{:S(2)}, u32[]{:S(2)}) collective-permute-start(bf16[4,8192]{1,0:T(4,128)(2,1)S(1)} %get-tuple-element.32.refs_0_), channel_id=1, source_target_pairs={{0,12},{2,14},{4,8},{6,10},{8,4},{10,6},{12,0},{14,2},{16,28},{18,... | collective-permute-start | bytes 196616 | tf_op jit(solution)/shard_map/ppermute | solution.py:298
  23.7 0.8 %collective-permute-start.6 = (bf16[4,8192]{1,0:T(4,128)(2,1)S(1)}, bf16[4,8192]{1,0:T(4,128)(2,1)S(1)}, u32[]{:S(2)}, u32[]{:S(2)}) collective-permute-start(bf16[4,8192]{1,0:T(4,128)(2,1)S(1)} %get-tuple-element.32.refs_0_), channel_id=1, source_target_pairs={{0,8},{2,10},{4,12},{6,14},{8,0},{10,2},{12,4},{14,6},{16,24},{18,... | collective-permute-start | bytes 196616 | tf_op jit(solution)/shard_map/ppermute | solution.py:298
  24.4 1.8 %collective-permute-start.5 = (bf16[4,8192]{1,0:T(4,128)(2,1)S(1)}, bf16[4,8192]{1,0:T(4,128)(2,1)S(1)}, u32[]{:S(2)}, u32[]{:S(2)}) collective-permute-start(bf16[4,8192]{1,0:T(4,128)(2,1)S(1)} %get-tuple-element.32.refs_0_), channel_id=1, source_target_pairs={{0,4},{2,6},{4,0},{6,2},{8,12},{10,14},{12,8},{14,10},{16,20},{18,... | collective-permute-start | bytes 196616 | tf_op jit(solution)/shard_map/ppermute | solution.py:298
  26.3 1.7 %collective-permute-done.7.refs_3_ = bf16[4,8192]{1,0:T(4,128)(2,1)S(1)} collective-permute-done((bf16[4,8192]{1,0:T(4,128)(2,1)S(1)}, bf16[4,8192]{1,0:T(4,128)(2,1)S(1)}, u32[]{:S(2)}, u32[]{:S(2)}) %collective-permute-start.7) | collective-permute-done | bytes 65568 | tf_op jit(solution)/shard_map/ppermute | solution.py:298
  28.0 0.0 collective-permute-done.6.refs_2_
  28.0 0.8 %collective-permute-done.5.refs_1_ = bf16[4,8192]{1,0:T(4,128)(2,1)S(1)} collective-permute-done((bf16[4,8192]{1,0:T(4,128)(2,1)S(1)}, bf16[4,8192]{1,0:T(4,128)(2,1)S(1)}, u32[]{:S(2)}, u32[]{:S(2)}) %collective-permute-start.5) | collective-permute-done | bytes 65568 | tf_op jit(solution)/shard_map/ppermute | solution.py:298
  28.7 0.1 join.1.near_ref
  28.8 0.1 collective-permute-start.8
  28.9 1.5 %collective-permute-done.8.far_ref = bf16[16,8192]{1,0:T(8,128)(2,1)S(1)} collective-permute-done((bf16[16,8192]{1,0:T(8,128)(2,1)S(1)}, bf16[16,8192]{1,0:T(8,128)(2,1)S(1)}, u32[]{:S(2)}, u32[]{:S(2)}) %collective-permute-start.8) | collective-permute-done | bytes 262176 | tf_op jit(solution)/shard_map/ppermute | solution.py:298
  30.4 0.0 slice-done
  30.4 0.0 slice-done.2
  30.4 0.0 slice-done.4
  30.4 0.0 slice-done.1
  30.4 0.0 slice-done.3
  30.4 0.0 slice-done.5
  30.4 4.4 %feed.1 = (f32[16,8192]{1,0:T(8,128)S(1)}, bf16[16,8192]{1,0:T(8,128)(2,1)S(1)}) custom-call(s32[2,2,128]{2,1,0:T(2,128)S(1)} %get-tuple-element.30.keeps_vmem, f32[3,2,128]{2,1,0:T(2,128)S(1)} %get-tuple-element.31.scales_vmem, bf16[16,8192]{1,0:T(8,128)(2,1)S(1)} %join.1.near_ref, bf16[16,8192]{1,0:T(8,128)(2,1)S(1)} %collective-permute-done.8.far_ref, ...), custom_call_target="tpu_custom_call" | custom-call | tf_op jit(solution)/shard_map/feed/pallas_call | solution.py:413
  34.8 0.2 collective-permute-start.9
  35.0 1.4 %collective-permute-done.9.refs_0_ = bf16[16,8192]{1,0:T(8,128)(2,1)S(1)} collective-permute-done((bf16[16,8192]{1,0:T(8,128)(2,1)S(1)}, bf16[16,8192]{1,0:T(8,128)(2,1)S(1)}, u32[]{:S(2)}, u32[]{:S(2)}) %collective-permute-start.9) | collective-permute-done | bytes 262176 | tf_op jit(solution)/shard_map/ppermute | solution.py:298
  36.4 0.1 sum.2
  36.6 2.9 %collective-permute-start.10 = (bf16[4,8192]{1,0:T(4,128)(2,1)S(1)}, bf16[4,8192]{1,0:T(4,128)(2,1)S(1)}, u32[]{:S(2)}, u32[]{:S(2)}) collective-permute-start(bf16[4,8192]{1,0:T(4,128)(2,1)S(1)} %get-tuple-element.36), channel_id=1, source_target_pairs={{0,12},{2,14},{4,8},{6,10},{8,4},{10,6},{12,0},{14,2},{16,28},{18,... | collective-permute-start | bytes 196616 | tf_op jit(solution)/shard_map/ppermute | solution.py:298
  39.5 0.1 collective-permute-start.11
  39.6 0.5 %collective-permute-start.12 = (bf16[4,8192]{1,0:T(4,128)(2,1)S(1)}, bf16[4,8192]{1,0:T(4,128)(2,1)S(1)}, u32[]{:S(2)}, u32[]{:S(2)}) collective-permute-start(bf16[4,8192]{1,0:T(4,128)(2,1)S(1)} %get-tuple-element.38), channel_id=1, source_target_pairs={{0,8},{2,10},{4,12},{6,14},{8,0},{10,2},{12,4},{14,6},{16,24},{18,... | collective-permute-start | bytes 196616 | tf_op jit(solution)/shard_map/ppermute | solution.py:298
  40.1 1.7 %collective-permute-done.10.refs_0_ = bf16[4,8192]{1,0:T(4,128)(2,1)S(1)} collective-permute-done((bf16[4,8192]{1,0:T(4,128)(2,1)S(1)}, bf16[4,8192]{1,0:T(4,128)(2,1)S(1)}, u32[]{:S(2)}, u32[]{:S(2)}) %collective-permute-start.10) | collective-permute-done | bytes 65568 | tf_op jit(solution)/shard_map/ppermute | solution.py:298
  41.9 1.9 %collective-permute-done.11.refs_1_ = bf16[4,8192]{1,0:T(4,128)(2,1)S(1)} collective-permute-done((bf16[4,8192]{1,0:T(4,128)(2,1)S(1)}, bf16[4,8192]{1,0:T(4,128)(2,1)S(1)}, u32[]{:S(2)}, u32[]{:S(2)}) %collective-permute-start.11) | collective-permute-done | bytes 65568 | tf_op jit(solution)/shard_map/ppermute | solution.py:298
  43.8 0.1 collective-permute-done.12.refs_2_
  43.9 0.1 sum.3
  44.0 2.1 %collective-permute-start.13 = (bf16[2,8192]{1,0:T(2,128)(2,1)S(1)}, bf16[2,8192]{1,0:T(2,128)(2,1)S(1)}, u32[]{:S(2)}, u32[]{:S(2)}) collective-permute-start(bf16[2,8192]{1,0:T(2,128)(2,1)S(1)} %get-tuple-element.40), channel_id=1, source_target_pairs={{0,16},{2,18},{4,20},{6,22},{8,24},{10,26},{12,28},{14,30},{16,0},... | collective-permute-start | bytes 98312 | tf_op jit(solution)/shard_map/ppermute | solution.py:298
  46.1 2.7 %collective-permute-done.13 = bf16[2,8192]{1,0:T(2,128)(2,1)S(1)} collective-permute-done((bf16[2,8192]{1,0:T(2,128)(2,1)S(1)}, bf16[2,8192]{1,0:T(2,128)(2,1)S(1)}, u32[]{:S(2)}, u32[]{:S(2)}) %collective-permute-start.13) | collective-permute-done | bytes 32800 | tf_op jit(solution)/shard_map/ppermute | solution.py:298
  48.9 0.7 %add_convert_fusion = bf16[2,8192]{1,0:T(2,128)(2,1)} fusion(bf16[2,8192]{1,0:T(2,128)(2,1)S(1)} %collective-permute-done.13, f32[2,8192]{1,0:T(2,128)S(1)} %get-tuple-element.29, f32[2,8192]{1,0:T(2,128)S(1)} %get-tuple-element.39), kind=kLoop, calls=%fused_computation | loop fusion | flops 65536 | bytes 196608 | tf_op jit(solution)/shard_map/convert_element_type | solution.py:440
  (4 shorter events, 0.0 us)
Async XLA Ops:
  0.8 3.1 %collective-permute-start = (bf16[4,5248]{1,0:T(4,128)(2,1)S(1)}, bf16[4,5248]{1,0:T(4,128)(2,1)S(1)}, u32[]{:S(2)}, u32[]{:S(2)}) collective-permute-start(bf16[4,5248]{1,0:T(4,128)(2,1)S(1)} %pack.1.packed_ref), channel_id=1, source_target_pairs={{2,0},{4,2},{6,4},{8,6},{10,8},{12,10},{14,12},{16,14},{18,16},{20... | collective-permute-start | bytes 125960 | tf_op jit(solution)/shard_map/ppermute | solution.py:334
  5.2 6.8 %collective-permute-start.1 = (bf16[4,4096]{1,0:T(4,128)(2,1)S(1)}, bf16[4,4096]{1,0:T(4,128)(2,1)S(1)}, u32[]{:S(2)}, u32[]{:S(2)}) collective-permute-start(bf16[4,4096]{1,0:T(4,128)(2,1)S(1)} %attend.2.refs_0_), channel_id=1, source_target_pairs={{0,2},{2,4},{4,6},{6,8},{8,10},{10,12},{12,14},{14,16},{16,18},{18... | collective-permute-start | bytes 98312 | tf_op jit(solution)/shard_map/ppermute | solution.py:372
  10.7 19.7 %slice-start = ((s8[8388608]{0:T(1024)(128)(4,1)}), s8[4194304]{0:T(1024)(128)(4,1)S(1)}, s32[]{:S(2)}) async-start(s8[8388608]{0:T(1024)(128)(4,1)} %bitcast.1), calls=%async_computation | async-start | bytes 8388608
  10.7 19.7 %slice-start.2 = ((s8[8388608]{0:T(1024)(128)(4,1)}), s8[4194304]{0:T(1024)(128)(4,1)S(1)}, s32[]{:S(2)}) async-start(s8[8388608]{0:T(1024)(128)(4,1)} %bitcast.3), calls=%async_computation.2 | async-start | bytes 8388608
  10.7 19.7 %slice-start.4 = ((s8[8388608]{0:T(1024)(128)(4,1)}), s8[4194304]{0:T(1024)(128)(4,1)S(1)}, s32[]{:S(2)}) async-start(s8[8388608]{0:T(1024)(128)(4,1)} %bitcast.5), calls=%async_computation.4 | async-start | bytes 8388608
  12.0 18.4 %slice-start.1 = ((s8[8388608]{0:T(1024)(128)(4,1)}), s8[4194304]{0:T(1024)(128)(4,1)S(1)}, s32[]{:S(2)}) async-start(s8[8388608]{0:T(1024)(128)(4,1)} %bitcast.1), calls=%async_computation.1 | async-start | bytes 8388608
  12.0 18.4 %slice-start.3 = ((s8[8388608]{0:T(1024)(128)(4,1)}), s8[4194304]{0:T(1024)(128)(4,1)S(1)}, s32[]{:S(2)}) async-start(s8[8388608]{0:T(1024)(128)(4,1)} %bitcast.3), calls=%async_computation.3 | async-start | bytes 8388608
  12.1 18.4 %slice-start.5 = ((s8[8388608]{0:T(1024)(128)(4,1)}), s8[4194304]{0:T(1024)(128)(4,1)S(1)}, s32[]{:S(2)}) async-start(s8[8388608]{0:T(1024)(128)(4,1)} %bitcast.5), calls=%async_computation.5 | async-start | bytes 8388608
  12.1 10.4 %collective-permute-start.3 = (bf16[2,12288]{1,0:T(2,128)(2,1)S(1)}, bf16[2,12288]{1,0:T(2,128)(2,1)S(1)}, u32[]{:S(2)}, u32[]{:S(2)}) collective-permute-start(bf16[2,12288]{1,0:T(2,128)(2,1)S(1)} %get-tuple-element.26.stay_ref), channel_id=1, source_target_pairs={{0,16},{2,18},{4,20},{6,22},{8,24},{10,26},{12,28},{14,30},{16,0},... | collective-permute-start | bytes 147464 | tf_op jit(solution)/shard_map/ppermute | solution.py:298
  16.9 5.5 %collective-permute-start.4 = (bf16[2,4096]{1,0:T(2,128)(2,1)S(1)}, bf16[2,4096]{1,0:T(2,128)(2,1)S(1)}, u32[]{:S(2)}, u32[]{:S(2)}) collective-permute-start(bf16[2,4096]{1,0:T(2,128)(2,1)S(1)} %get-tuple-element.27), channel_id=1, source_target_pairs={{0,17},{1,16},{2,19},{3,18},{4,21},{5,20},{6,23},{7,22},{8,25},{9,... | collective-permute-start | bytes 49160 | tf_op jit(solution)/shard_map/ppermute | solution.py:390
  18.0 4.5 %collective-permute-start.2 = (bf16[2,4096]{1,0:T(2,128)(2,1)S(1)}, bf16[2,4096]{1,0:T(2,128)(2,1)S(1)}, u32[]{:S(2)}, u32[]{:S(2)}) collective-permute-start(bf16[2,4096]{1,0:T(2,128)(2,1)S(1)} %get-tuple-element.27), channel_id=1, source_target_pairs={{0,1},{1,0},{2,3},{3,2},{4,5},{5,4},{6,7},{7,6},{8,9},{9,8},{10,11... | collective-permute-start | bytes 49160 | tf_op jit(solution)/shard_map/ppermute | solution.py:396
  22.7 5.2 %collective-permute-start.7 = (bf16[4,8192]{1,0:T(4,128)(2,1)S(1)}, bf16[4,8192]{1,0:T(4,128)(2,1)S(1)}, u32[]{:S(2)}, u32[]{:S(2)}) collective-permute-start(bf16[4,8192]{1,0:T(4,128)(2,1)S(1)} %get-tuple-element.32.refs_0_), channel_id=1, source_target_pairs={{0,12},{2,14},{4,8},{6,10},{8,4},{10,6},{12,0},{14,2},{16,28},{18,... | collective-permute-start | bytes 196616 | tf_op jit(solution)/shard_map/ppermute | solution.py:298
  23.7 4.3 %collective-permute-start.6 = (bf16[4,8192]{1,0:T(4,128)(2,1)S(1)}, bf16[4,8192]{1,0:T(4,128)(2,1)S(1)}, u32[]{:S(2)}, u32[]{:S(2)}) collective-permute-start(bf16[4,8192]{1,0:T(4,128)(2,1)S(1)} %get-tuple-element.32.refs_0_), channel_id=1, source_target_pairs={{0,8},{2,10},{4,12},{6,14},{8,0},{10,2},{12,4},{14,6},{16,24},{18,... | collective-permute-start | bytes 196616 | tf_op jit(solution)/shard_map/ppermute | solution.py:298
  24.4 4.3 %collective-permute-start.5 = (bf16[4,8192]{1,0:T(4,128)(2,1)S(1)}, bf16[4,8192]{1,0:T(4,128)(2,1)S(1)}, u32[]{:S(2)}, u32[]{:S(2)}) collective-permute-start(bf16[4,8192]{1,0:T(4,128)(2,1)S(1)} %get-tuple-element.32.refs_0_), channel_id=1, source_target_pairs={{0,4},{2,6},{4,0},{6,2},{8,12},{10,14},{12,8},{14,10},{16,20},{18,... | collective-permute-start | bytes 196616 | tf_op jit(solution)/shard_map/ppermute | solution.py:298
  28.8 1.6 %collective-permute-start.8 = (bf16[16,8192]{1,0:T(8,128)(2,1)S(1)}, bf16[16,8192]{1,0:T(8,128)(2,1)S(1)}, u32[]{:S(2)}, u32[]{:S(2)}) collective-permute-start(bf16[16,8192]{1,0:T(8,128)(2,1)S(1)} %join.1.near_ref), channel_id=1, source_target_pairs={{0,2},{2,0},{4,6},{6,4},{8,10},{10,8},{12,14},{14,12},{16,18},{18,... | collective-permute-start | bytes 786440 | tf_op jit(solution)/shard_map/ppermute | solution.py:298
  34.8 1.6 %collective-permute-start.9 = (bf16[16,8192]{1,0:T(8,128)(2,1)S(1)}, bf16[16,8192]{1,0:T(8,128)(2,1)S(1)}, u32[]{:S(2)}, u32[]{:S(2)}) collective-permute-start(bf16[16,8192]{1,0:T(8,128)(2,1)S(1)} %get-tuple-element.34), channel_id=1, source_target_pairs={{0,2},{2,0},{4,6},{6,4},{8,10},{10,8},{12,14},{14,12},{16,18},{18,... | collective-permute-start | bytes 786440 | tf_op jit(solution)/shard_map/ppermute | solution.py:298
  36.6 5.3 %collective-permute-start.10 = (bf16[4,8192]{1,0:T(4,128)(2,1)S(1)}, bf16[4,8192]{1,0:T(4,128)(2,1)S(1)}, u32[]{:S(2)}, u32[]{:S(2)}) collective-permute-start(bf16[4,8192]{1,0:T(4,128)(2,1)S(1)} %get-tuple-element.36), channel_id=1, source_target_pairs={{0,12},{2,14},{4,8},{6,10},{8,4},{10,6},{12,0},{14,2},{16,28},{18,... | collective-permute-start | bytes 196616 | tf_op jit(solution)/shard_map/ppermute | solution.py:298
  39.5 4.3 %collective-permute-start.11 = (bf16[4,8192]{1,0:T(4,128)(2,1)S(1)}, bf16[4,8192]{1,0:T(4,128)(2,1)S(1)}, u32[]{:S(2)}, u32[]{:S(2)}) collective-permute-start(bf16[4,8192]{1,0:T(4,128)(2,1)S(1)} %get-tuple-element.37), channel_id=1, source_target_pairs={{0,4},{2,6},{4,0},{6,2},{8,12},{10,14},{12,8},{14,10},{16,20},{18,... | collective-permute-start | bytes 196616 | tf_op jit(solution)/shard_map/ppermute | solution.py:298
  39.6 4.3 %collective-permute-start.12 = (bf16[4,8192]{1,0:T(4,128)(2,1)S(1)}, bf16[4,8192]{1,0:T(4,128)(2,1)S(1)}, u32[]{:S(2)}, u32[]{:S(2)}) collective-permute-start(bf16[4,8192]{1,0:T(4,128)(2,1)S(1)} %get-tuple-element.38), channel_id=1, source_target_pairs={{0,8},{2,10},{4,12},{6,14},{8,0},{10,2},{12,4},{14,6},{16,24},{18,... | collective-permute-start | bytes 196616 | tf_op jit(solution)/shard_map/ppermute | solution.py:298
  44.0 4.9 %collective-permute-start.13 = (bf16[2,8192]{1,0:T(2,128)(2,1)S(1)}, bf16[2,8192]{1,0:T(2,128)(2,1)S(1)}, u32[]{:S(2)}, u32[]{:S(2)}) collective-permute-start(bf16[2,8192]{1,0:T(2,128)(2,1)S(1)} %get-tuple-element.40), channel_id=1, source_target_pairs={{0,16},{2,18},{4,20},{6,22},{8,24},{10,26},{12,28},{14,30},{16,0},... | collective-permute-start | bytes 98312 | tf_op jit(solution)/shard_map/ppermute | solution.py:298
